TPU v7x, 32 devices: a whole 2x2x4 slice. The times are simulated.
32 devices in a mesh: tm: 8 (over z, x), space: 4 (over y, core).
Axes of the slice: x: 2, y: 2, z: 4, core: 2. Of those that a mesh axis runs over, the one named last changes fastest.
Arguments:
- snapshots: bfloat16 [256, 3, 131072], P('tm', None, 'space'), may hold values from -12 to 12
- cell_weights: float32 [131072], P('space'), may hold values from 0.2 to 5
- freq_order: int32 [32], replicated, may hold values from 0 to 31, each once
Outputs:
- energies: float32 [32, 4], P('tm')
- modes: bfloat16 [32, 4, 2, 3, 131072], P('tm', None, None, None, 'space')
All inputs are finite; a program needn't handle non-finite values.
Results may differ from a plain program's by a relative error of at most 0.0043.
Values may be sent and summed in bfloat16 or wider, within the bound.
No kernel may reach another device: no remote copies, remote signals or barrier semaphores. Data moves between devices by JAX's collectives and lax.ppermute only.
A program may use at most 192 MiB of HBM per device.

v0:
```python
import math

import jax
import jax.numpy as jnp
from jax import lax
from jax.sharding import PartitionSpec as P

NFFT = 64
COMP = 3
MODES = 4
SWEEPS = 3
NF = 32


shift_rate = 0.61
top_precision = lax.Precision.HIGHEST


def from_behind(value, axis, steps):
    count = lax.axis_size(axis)
    initial, last = (max(0, -steps), min(count, count - steps))
    return lax.ppermute(value, axis, [(source, source + steps) for source in range(initial, last)])


def window_tables():
    sample = jnp.arange(NFFT, dtype=jnp.int32)
    freq_rows = jnp.arange(NF, dtype=jnp.int32)
    turn_index = (freq_rows[:, None] * sample[None, :] % NFFT).astype(jnp.float32)
    angle_grid = 2.0 * math.pi * turn_index / NFFT
    hann_window = 0.5 - 0.5 * jnp.cos(2.0 * math.pi * sample.astype(jnp.float32) / NFFT)
    dft_basis = jnp.stack(
        [hann_window * jnp.cos(angle_grid), -hann_window * jnp.sin(angle_grid)], 0
    )
    return (dft_basis.astype(jnp.bfloat16), jnp.sum(hann_window * hann_window))


def start_vectors(block_count):
    rows_idx = jnp.arange(block_count, dtype=jnp.float32)[:, None] + 1.0
    cols_idx = jnp.arange(MODES, dtype=jnp.float32)[None, :] + 1.0
    return jnp.cos(shift_rate * rows_idx * cols_idx)


def complex_apply(real_part, imag_part, vec_re, vec_im):
    first_re = jnp.einsum("fab,fbk->fak", real_part, vec_re, precision=top_precision)
    first_im = jnp.einsum("fab,fbk->fak", imag_part, vec_im, precision=top_precision)
    cross_re = jnp.einsum("fab,fbk->fak", real_part, vec_im, precision=top_precision)
    cross_im = jnp.einsum("fab,fbk->fak", imag_part, vec_re, precision=top_precision)
    return (first_re - first_im, cross_re + cross_im)


def orthonormal(image_re, image_im):
    done_re = []
    done_im = []
    for column in range(MODES):
        col_re = image_re[:, :, column]
        col_im = image_im[:, :, column]
        for earlier in range(column):
            prev_re = done_re[earlier]
            prev_im = done_im[earlier]
            inner_re = jnp.sum(prev_re * col_re + prev_im * col_im, axis=1, keepdims=True)
            inner_im = jnp.sum(prev_re * col_im - prev_im * col_re, axis=1, keepdims=True)
            col_re = col_re - (inner_re * prev_re - inner_im * prev_im)
            col_im = col_im - (inner_re * prev_im + inner_im * prev_re)
        length = jnp.sqrt(jnp.sum(col_re * col_re + col_im * col_im, axis=1, keepdims=True))
        done_re.append(col_re / length)
        done_im.append(col_im / length)
    return (jnp.stack(done_re, 2), jnp.stack(done_im, 2))


def power_sweeps(real_part, imag_part):
    start_table = start_vectors(real_part.shape[-1])
    vec_re = jnp.broadcast_to(start_table, real_part.shape[:1] + start_table.shape)
    vec_im = jnp.zeros_like(vec_re)
    for sweep_step in range(SWEEPS):
        image_re, image_im = complex_apply(real_part, imag_part, vec_re, vec_im)
        vec_re, vec_im = orthonormal(image_re, image_im)
    applied_re, applied_im = complex_apply(real_part, imag_part, vec_re, vec_im)
    energy = jnp.sum(vec_re * applied_re + vec_im * applied_im, axis=1)
    return (vec_re, vec_im, energy)


def mixing_rows(vec_re, vec_im, factor):
    turned_re = jnp.swapaxes(vec_re, 1, 2) * factor
    turned_im = jnp.swapaxes(vec_im, 1, 2) * factor
    real_out = jnp.stack([turned_re, -turned_im], 2)
    imag_out = jnp.stack([turned_im, turned_re], 2)
    return jnp.stack([real_out, imag_out], 2).astype(jnp.bfloat16)


def gram_parts(weighted, spectra):
    products = jnp.einsum("arfp,bsfp->frasb", weighted, spectra, preferred_element_type=jnp.float32)
    return (
        products[:, 0, :, 0, :] + products[:, 1, :, 1, :],
        products[:, 0, :, 1, :] - products[:, 1, :, 0, :],
    )


def per_device(snapshots, cell_weights, freq_order):
    dft_basis, energy_sum = window_tables()
    flat_basis = dft_basis.reshape(2 * NF, NFFT)
    half_len = snapshots.shape[0]
    cells_dev = snapshots.shape[2]
    devices_tm = lax.axis_size("tm")
    point_total = COMP * cells_dev * lax.axis_size("space")
    gram_scale = 1.0 / (energy_sum * point_total)
    factor = 1.0 / jnp.sqrt(energy_sum)
    flat_rows = snapshots.reshape(half_len, -1)
    following = from_behind(flat_rows, "tm", -1)
    joined = jnp.concatenate([flat_rows, following], 0)
    spectra = jnp.dot(flat_basis, joined, preferred_element_type=jnp.float32).astype(jnp.bfloat16)
    ordered = jnp.take(spectra.reshape(2, NF, -1), freq_order, axis=1)
    received = lax.all_to_all(ordered[None], "tm", split_axis=2, concat_axis=0, tiled=True)[
        : devices_tm - 1
    ]
    point_weights = jnp.tile(cell_weights, COMP)
    weighted = (received.astype(jnp.float32) * point_weights).astype(jnp.bfloat16)
    gram_re, gram_im = gram_parts(weighted, received)
    gram_re, gram_im = lax.psum((gram_re, gram_im), "space")
    vec_re, vec_im, energies = power_sweeps(gram_re * gram_scale, gram_im * gram_scale)
    mixing = mixing_rows(vec_re, vec_im, factor)
    mode_rows = jnp.einsum("fkorb,brfp->fkop", mixing, received, preferred_element_type=jnp.float32)
    mode_out = mode_rows.astype(jnp.bfloat16).reshape(mode_rows.shape[0], MODES, 2, COMP, cells_dev)
    return (energies, mode_out)


def solution(mesh):
    return jax.shard_map(
        per_device,
        mesh=mesh,
        in_specs=(P("tm", None, "space"), P("space"), P()),
        out_specs=(P("tm", None), P("tm", None, None, None, "space")),
        check_vma=False,
    )
```

profile of v0, /device:TPU:8, one launch (start us, length us, event | category | flops | bytes accessed | tf_op | source)
XLA Modules:
  0.0 607.0 jit_solution(15525865652656288427)
XLA Ops:
  0.6 3.2 copy.230
  3.8 3.3 collective-permute-start
  7.5 135.5 %collective-permute-done = bf16[32,98304]{1,0:T(8,128)(2,1)S(1)} collective-permute-done((bf16[32,98304]{1,0:T(8,128)(2,1)S(1)}, bf16[32,98304]{1,0:T(8,128)(2,1)S(1)}, u32[]{:S(2)}, u32[]{:S(2)}) %collective-permute-start) | collective-permute-done | bytes 6291488 | tf_op jit(solution)/shard_map/ppermute | solution.py:22
  143.0 2.7 copy-done.1
  145.7 8.2 %convolution_convert_fusion = bf16[64,98304]{1,0:T(8,128)(2,1)} fusion(bf16[64,64]{1,0:T(8,128)(2,1)S(1)} %bitcast.506, bf16[32,98304]{1,0:T(8,128)(2,1)} %copy-done.1, bf16[32,98304]{1,0:T(8,128)(2,1)S(1)} %bitcast.504), kind=kOutput, calls=%fused_computation.1 | convolution fusion | flops 836763648 | bytes 25174016 | tf_op jit(solution)/shard_map/dot_general | solution.py:110
  153.9 23.6 %copy.143 = bf16[2,32,98304]{2,0,1:T(2,128)(2,1)} copy(bf16[2,32,98304]{2,1,0:T(8,128)(2,1)} %bitcast.501) | data formatting | bytes 25165824 | tf_op jit(solution)/shard_map/reshape | solution.py:111
  177.5 31.3 %gather_fusion = bf16[32,2,98304]{2,1,0:T(2,128)(2,1)} fusion(bf16[2,32,98304]{2,0,1:T(2,128)(2,1)} %copy.143, s32[1024]{0:T(1024)S(1)} %pad_clamp_fusion), kind=kCustom, calls=%fused_computation | custom fusion | bytes 25165952 | tf_op jit(solution)/shard_map/jit(_take)/gather | solution.py:111
  208.8 15.1 %fusion.11 = bf16[1,2,32,98304]{3,1,0,2:T(2,128)(2,1)} fusion(bf16[32,2,98304]{2,1,0:T(2,128)(2,1)} %gather_fusion, pred[32]{0:T(512)(128)(4,1)S(1)} %compare_and_fusion), kind=kLoop, calls=%fused_computation.16 | loop fusion | flops 6291456 | bytes 25165856 | tf_op jit(solution)/shard_map/jit(_take)/select_n | solution.py:111
  223.9 6.3 %all-to-all-start = ((bf16[1,2,32,98304]{3,1,0,2:T(2,128)(2,1)}), bf16[1,2,32,98304]{3,1,0,2:T(2,128)(2,1)}, u32[]{:S(2)}, u32[]{:S(2)}) async-start(bf16[1,2,32,98304]{3,1,0,2:T(2,128)(2,1)} %fusion.11), calls=%async_computation | async-start | bytes 25165824 | tf_op jit(solution)/shard_map/all_to_all | solution.py:112
  230.3 0.3 mul.1341
  230.6 0.6 multiply_reduce_fusion
  232.7 267.1 %all-to-all-done = bf16[1,2,32,98304]{3,1,0,2:T(2,128)(2,1)} async-done(((bf16[1,2,32,98304]{3,1,0,2:T(2,128)(2,1)}), bf16[1,2,32,98304]{3,1,0,2:T(2,128)(2,1)}, u32[]{:S(2)}, u32[]{:S(2)}) %all-to-all-start) | async-done | bytes 12582944 | tf_op jit(solution)/shard_map/all_to_all | solution.py:112
  499.8 14.5 %copy.283 = bf16[1,2,8,4,98304]{4,2,1,3,0:T(8,128)(2,1)} copy(bf16[1,2,8,4,98304]{4,1,3,2,0:T(2,128)(2,1)} %bitcast.5) | data formatting | bytes 25165824 | tf_op jit(solution)/shard_map/all_to_all | solution.py:112
  514.2 38.4 %fusion.14 = f32[4,2,7,2,7]{2,4,1,3,0:T(8,128)S(1)} fusion(f32[98304]{0:T(1024)S(1)} %mul.1341, bf16[8,1,2,4,98304]{4,0,2,3,1:T(8,128)(2,1)} %bitcast.499), kind=kOutput, calls=%fused_computation.19 | convolution fusion | flops 170655744 | bytes 25562176 | tf_op jit(solution)/shard_map/arfp,bsfp->frasb/dot_general | solution.py:91
  552.7 11.4 %all-reduce = (f32[4,7,7]{1,2,0:T(8,128)S(1)}, f32[4,7,7]{1,2,0:T(8,128)S(1)}) all-reduce(f32[4,7,7]{1,2,0:T(8,128)S(1)} %fusion.22, f32[4,7,7]{1,2,0:T(8,128)S(1)} %fusion.24), channel_id=1, replica_groups=mesh['tm'=8,'space'=4] {'space'}, use_global_device_ids=true, to_apply=%region_2.3 | all-reduce | flops 392 | bytes 3136 | tf_op jit(solution)/shard_map/psum | solution.py:118
  564.3 0.2 fusion.61
  564.4 0.2 fusion.43
  564.6 0.2 fusion.45
  564.9 0.3 fusion.135
  565.2 0.2 add_reduce_fusion.17
  565.4 0.2 add_reduce_fusion.14
  565.7 0.2 add_reduce_fusion.15
  565.9 0.2 add_reduce_fusion.13
  566.1 0.2 add_reduce_fusion.12
  566.5 0.2 fusion.57
  566.8 0.2 fusion.55
  567.0 0.2 fusion.41
  567.3 0.3 fusion.121
  567.5 0.2 add_reduce_fusion.11
  567.7 0.2 add_reduce_fusion.8
  568.0 0.2 add_reduce_fusion.9
  568.2 0.2 add_reduce_fusion.7
  568.4 0.2 add_reduce_fusion.6
  568.9 0.2 fusion.53
  569.3 0.2 fusion.37
  569.6 0.3 fusion.107
  569.9 0.2 add_reduce_fusion.5
  570.1 0.2 add_reduce_fusion.2
  570.3 0.2 add_reduce_fusion.3
  570.5 0.2 add_reduce_fusion.1
  570.7 0.2 add_reduce_fusion
  571.3 0.2 fusion.47
  571.5 0.2 fusion.49
  571.6 0.2 fusion.31
  572.0 11.4 %fusion = bf16[4,4,2,98304]{3,1,2,0:T(4,128)(2,1)} fusion(bf16[8,1,2,4,98304]{4,0,2,3,1:T(8,128)(2,1)} %bitcast.500, bf16[4,4,1,2,7]{4,1,3,2,0:T(4,128)(2,1)S(1)} %get-tuple-element.132, bf16[4,4,1,2,7]{4,1,3,2,0:T(4,128)(2,1)S(1)} %get-tuple-element.131), kind=kOutput, calls=%fused_computation.3 | convolution fusion | flops 91227904 | bytes 18875264 | tf_op jit(solution)/shard_map/fkorb,brfp->fkop/dot_general | solution.py:121
  583.3 9.9 %reshape.1724 = bf16[4,4,2,3,32768]{4,3,1,2,0:T(4,128)(2,1)} reshape(bf16[4,4,2,98304]{3,1,2,0:T(4,128)(2,1)} %fusion) | data formatting | bytes 12582912 | tf_op jit(solution)/shard_map/reshape | solution.py:122
  593.3 13.1 %copy.201 = bf16[4,4,2,3,32768]{4,2,3,1,0:T(2,128)(2,1)} copy(bf16[4,4,2,3,32768]{4,3,1,2,0:T(4,128)(2,1)} %reshape.1724) | data formatting | bytes 12582912
  606.4 0.7 copy.200
  (61 shorter events, 2.5 us)
Async XLA Ops:
  0.6 6.6 %copy-start.2 = (s32[32]{0:T(128)S(1)}, s32[32]{0:T(128)}, u32[]{:S(2)}) copy-start(s32[32]{0:T(128)} %param.5) | copy-start | bytes 388
  3.8 139.1 %collective-permute-start = (bf16[32,98304]{1,0:T(8,128)(2,1)S(1)}, bf16[32,98304]{1,0:T(8,128)(2,1)S(1)}, u32[]{:S(2)}, u32[]{:S(2)}) collective-permute-start(bf16[32,98304]{1,0:T(8,128)(2,1)S(1)} %bitcast.503), channel_id=1, source_target_pairs={{4,0},{8,4},{12,8},{16,12},{20,16},{24,20},{28,24},{5,1},{9,5},{13... | collective-permute-start | bytes 18874376 | tf_op jit(solution)/shard_map/ppermute | solution.py:22
  143.0 2.7 copy-start.1
  223.9 6.3 %copy-start = (f32[32768]{0:T(1024)S(1)}, f32[32768]{0:T(1024)}, u32[]{:S(2)}) copy-start(f32[32768]{0:T(1024)} %param.4) | copy-start | bytes 393220
  223.9 275.9 %all-to-all-start = ((bf16[1,2,32,98304]{3,1,0,2:T(2,128)(2,1)}), bf16[1,2,32,98304]{3,1,0,2:T(2,128)(2,1)}, u32[]{:S(2)}, u32[]{:S(2)}) async-start(bf16[1,2,32,98304]{3,1,0,2:T(2,128)(2,1)} %fusion.11), calls=%async_computation | async-start | bytes 25165824 | tf_op jit(solution)/shard_map/all_to_all | solution.py:112
where the time goes:
time: 611 us; the launch traced here: 607 us
  waiting for transfers between devices  403 us (66%)
  local copies, waits for them, and re-layouts  99.4 us (16%)
  matrix products  60.7 us (10%)
  other arithmetic  21.1 us (3%)
  blocking collectives  11.4 us (2%)
  starting transfers between devices  9.56 us (2%)
    all_to_all x1, waiting for transfers between devices, per_device(): lax.all_to_all(ordered[None], 'tm', split_axis=2, concat_axis=0, tiled=True)  267 us
    ppermute x1, waiting for transfers between devices, from_behind(): lax.ppermute(value, axis, [(source, source + steps) for source in range(i...  136 us
    dot_general x1, matrix products, gram_parts(): jnp.einsum('arfp,bsfp->frasb', weighted, spectra, preferred_element_type=...  38.4 us
    gather x1, local copies, waits for them, and re-layouts, per_device(): ordered = jnp.take(spectra.reshape(2, NF, -1), freq_order, axis=1)  31.3 us
    reshape x1, local copies, waits for them, and re-layouts, per_device(): ordered = jnp.take(spectra.reshape(2, NF, -1), freq_order, axis=1)  23.6 us
    unnamed x8, local copies, waits for them, and re-layouts  16.5 us
    select_n x2, other arithmetic, per_device(): ordered = jnp.take(spectra.reshape(2, NF, -1), freq_order, axis=1)  15.1 us
    all_to_all x1, local copies, waits for them, and re-layouts, per_device(): lax.all_to_all(ordered[None], 'tm', split_axis=2, concat_axis=0, tiled=True)  14.5 us
  transfers between devices with their start and end apart: 2, of which 2 were waited for; matrix products, arithmetic and copies ran while one was open for 0% of the time, Pallas kernels for 0%

commit v1 on v0

v1 whole, which is shorter than its diff:
```python
import functools
import math

import jax
import jax.numpy as jnp
from jax import lax
from jax.experimental import pallas as pl
from jax.experimental.pallas import tpu as pltpu
from jax.sharding import PartitionSpec as P

NFFT = 64
COMP = 3
MODES = 4
SWEEPS = 3
NF = 32

CHUNKS = ((0, 0, 2), (0, 2, 6), (0, 8, 8), (1, 0, 8), (1, 8, 8), (2, 0, 8), (2, 8, 6), (2, 14, 2))
KINDS = (0, 1, 0, 1, 0, 1, 0, 1)
PARTS = 16

shift_rate = 0.61
top_precision = lax.Precision.HIGHEST


def hann_window():
    sample = jnp.arange(NFFT, dtype=jnp.int32)
    return 0.5 - 0.5 * jnp.cos(2.0 * math.pi * sample.astype(jnp.float32) / NFFT)


def basis_rows(freqs, sines):
    sample = jnp.arange(NFFT, dtype=jnp.int32)
    turn_index = (freqs[:, None] * sample[None, :] % NFFT).astype(jnp.float32)
    angle_grid = 2.0 * math.pi * turn_index / NFFT
    window = hann_window()
    rows = jnp.where(sines[:, None], -window * jnp.sin(angle_grid), window * jnp.cos(angle_grid))
    return rows.astype(jnp.bfloat16)


def pick(values, places):
    hot = places[:, None] == jnp.arange(values.shape[0], dtype=jnp.int32)[None, :]
    return jnp.sum(jnp.where(hot, values[None, :], 0), axis=1)


def start_vectors(block_count):
    rows_idx = jnp.arange(block_count, dtype=jnp.float32)[:, None] + 1.0
    cols_idx = jnp.arange(MODES, dtype=jnp.float32)[None, :] + 1.0
    return jnp.cos(shift_rate * rows_idx * cols_idx)


def table_of(role, devices, freqs, sines):
    rows = basis_rows(freqs, sines)
    first, second = rows[:, : NFFT // 2], rows[:, NFFT // 2 :]
    low = role < devices // 2
    middle = (role == devices // 2 - 1) | (role == devices // 2)
    near = jnp.where(low, first, second)
    beside = jnp.where(middle, jnp.zeros_like(first), jnp.where(low, second, first))
    return near, beside


def beside_of(role, devices):
    if role in (devices // 2 - 1, devices // 2):
        return None
    return role + 1 if role < devices // 2 else role - 1


def transform_kernel(count, rows, table_ref, *refs):
    ins, outs = refs[:count], refs[count:]
    total = None
    for place, ref in enumerate(ins):
        data = ref[...].reshape(ref.shape[-2:])
        half = data.shape[0]
        part = jnp.dot(
            table_ref[:, place * half : (place + 1) * half], data, preferred_element_type=jnp.float32
        )
        total = part if total is None else total + part
    for place, out in enumerate(outs):
        out[...] = total[place * rows : (place + 1) * rows].astype(out.dtype)


def transform(table, own, others, comp, start, size, devices, rows, tile):
    half = own.shape[1]
    ins = [pl.BlockSpec(table.shape, lambda g: (0, 0))]
    ins.append(pl.BlockSpec((1, half, tile), lambda g: (comp, 0, start // tile + g)))
    ins += [pl.BlockSpec((half, tile), lambda g: (0, g)) for _ in others]
    return pl.pallas_call(
        functools.partial(transform_kernel, 1 + len(others), rows),
        grid=(size // tile,),
        in_specs=ins,
        out_specs=[pl.BlockSpec((rows, tile), lambda g: (0, g))] * devices,
        out_shape=[jax.ShapeDtypeStruct((rows, size), jnp.bfloat16)] * devices,
        cost_estimate=pl.CostEstimate(
            flops=2 * table.size * size, bytes_accessed=2 * size * (table.shape[0] + table.shape[1]), transcendentals=0
        ),
        name="transform",
    )(table, own, *others)


def gram_kernel(count, weight_ref, *refs):
    messages = refs[:count]
    before, store, total = refs[-4], refs[-2], refs[-1]

    @pl.when(pl.program_id(0) == 0)
    def _():
        total[...] = before[...]

    wide = jnp.concatenate([ref[...].astype(jnp.float32) for ref in messages], 0)
    spectra = wide.astype(jnp.bfloat16)
    weighted = (wide * weight_ref[...]).astype(jnp.bfloat16)
    store[...] = spectra[None]
    total[...] += lax.dot_general(
        weighted, spectra, (((1,), (1,)), ((), ())), preferred_element_type=jnp.float32
    )


def gram(messages, weights, before, held, comp, start, size, tile):
    count = len(messages)
    rows = messages[0].shape[0]
    whole = count * rows
    spot = lambda g: (comp, 0, start // tile + g)
    return pl.pallas_call(
        functools.partial(gram_kernel, count),
        grid=(size // tile,),
        in_specs=[pl.BlockSpec((1, tile), lambda g: (0, start // tile + g))]
        + [pl.BlockSpec((rows, tile), lambda g: (0, g))] * count
        + [pl.BlockSpec((whole, whole), lambda g: (0, 0))]
        + [pl.BlockSpec(memory_space=pl.ANY)],
        out_specs=[pl.BlockSpec((1, whole, tile), spot), pl.BlockSpec((whole, whole), lambda g: (0, 0))],
        out_shape=[
            jax.ShapeDtypeStruct(held.shape, held.dtype),
            jax.ShapeDtypeStruct((whole, whole), jnp.float32),
        ],
        input_output_aliases={count + 2: 0},
        cost_estimate=pl.CostEstimate(flops=2 * whole * whole * size, bytes_accessed=4 * whole * size, transcendentals=0),
        name="gram",
    )(weights, *messages, before, held)


def modes_kernel(mix_ref, held_ref, out_ref):
    rows = jnp.dot(mix_ref[...], held_ref[0], preferred_element_type=jnp.float32)
    freqs, modes = out_ref.shape[:2]
    for f in range(freqs):
        for k in range(modes):
            place = 2 * (f * modes + k)
            out_ref[f, k, 0] = rows[place : place + 2].astype(out_ref.dtype)


def modes_of(mix, held, freqs, tile):
    comps, whole, cells = held.shape
    return pl.pallas_call(
        modes_kernel,
        grid=(comps, cells // tile),
        in_specs=[
            pl.BlockSpec(mix.shape, lambda c, g: (0, 0)),
            pl.BlockSpec((1, whole, tile), lambda c, g: (c, 0, g)),
        ],
        out_specs=pl.BlockSpec((freqs, MODES, 1, 2, tile), lambda c, g: (0, 0, c, 0, g)),
        out_shape=jax.ShapeDtypeStruct((freqs, MODES, comps, 2, cells), jnp.bfloat16),
        name="modes",
    )(mix, held)


def blank_kernel(out_ref):
    pass


def blank(shape, dtype):
    return pl.pallas_call(
        blank_kernel,
        out_specs=pl.BlockSpec(memory_space=pl.ANY),
        out_shape=jax.ShapeDtypeStruct(shape, dtype),
        name="blank",
    )()


def complex_apply(real_part, imag_part, vec_re, vec_im):
    first_re = jnp.einsum("fab,fbk->fak", real_part, vec_re, precision=top_precision)
    first_im = jnp.einsum("fab,fbk->fak", imag_part, vec_im, precision=top_precision)
    cross_re = jnp.einsum("fab,fbk->fak", real_part, vec_im, precision=top_precision)
    cross_im = jnp.einsum("fab,fbk->fak", imag_part, vec_re, precision=top_precision)
    return (first_re - first_im, cross_re + cross_im)


def orthonormal(image_re, image_im):
    done_re = []
    done_im = []
    for column in range(MODES):
        col_re = image_re[:, :, column]
        col_im = image_im[:, :, column]
        for earlier in range(column):
            prev_re = done_re[earlier]
            prev_im = done_im[earlier]
            inner_re = jnp.sum(prev_re * col_re + prev_im * col_im, axis=1, keepdims=True)
            inner_im = jnp.sum(prev_re * col_im - prev_im * col_re, axis=1, keepdims=True)
            col_re = col_re - (inner_re * prev_re - inner_im * prev_im)
            col_im = col_im - (inner_re * prev_im + inner_im * prev_re)
        length = jnp.sqrt(jnp.sum(col_re * col_re + col_im * col_im, axis=1, keepdims=True))
        done_re.append(col_re / length)
        done_im.append(col_im / length)
    return (jnp.stack(done_re, 2), jnp.stack(done_im, 2))


def power_sweeps(real_part, imag_part):
    start_table = start_vectors(real_part.shape[-1])
    vec_re = jnp.broadcast_to(start_table, real_part.shape[:1] + start_table.shape)
    vec_im = jnp.zeros_like(vec_re)
    for sweep_step in range(SWEEPS):
        image_re, image_im = complex_apply(real_part, imag_part, vec_re, vec_im)
        vec_re, vec_im = orthonormal(image_re, image_im)
    applied_re, applied_im = complex_apply(real_part, imag_part, vec_re, vec_im)
    energy = jnp.sum(vec_re * applied_re + vec_im * applied_im, axis=1)
    return (vec_re, vec_im, energy)


def mixing_rows(vec_re, vec_im, factor):
    turned_re = jnp.swapaxes(vec_re, 1, 2) * factor
    turned_im = jnp.swapaxes(vec_im, 1, 2) * factor
    real_out = jnp.stack([turned_re, -turned_im], 2)
    imag_out = jnp.stack([turned_im, turned_re], 2)
    return jnp.stack([real_out, imag_out], 2)


def per_device(snapshots, cell_weights, freq_order):
    devices = lax.axis_size("tm")
    spaces = lax.axis_size("space")
    me = lax.axis_index("tm")
    half, comps, cells = snapshots.shape
    freqs = NF // devices
    rows = 2 * freqs
    unit = cells // PARTS
    window = hann_window()
    energy_sum = jnp.sum(window * window)
    gram_scale = 1.0 / (energy_sum * (comps * cells * spaces))
    factor = 1.0 / jnp.sqrt(energy_sum)

    own = jnp.transpose(snapshots, (1, 0, 2))
    weights = cell_weights.reshape(1, cells)

    line = jnp.arange(devices * rows, dtype=jnp.int32)
    target = jnp.bitwise_xor(me, line // rows)
    line_freq = pick(freq_order, target * freqs + line % rows // 2)
    line_sine = line % 2 == 1
    near, beside = table_of(me, devices, line_freq, line_sine)
    table_0 = jnp.concatenate([near, beside], 1)
    near, beside = table_of(jnp.bitwise_xor(me, 1), devices, line_freq, line_sine)
    odd = me % 2 == 1
    own_beside = jnp.where(me < devices // 2, odd, ~odd)
    nothing = jnp.zeros_like(beside)
    table_1 = jnp.concatenate(
        [jnp.where(own_beside, beside, nothing), near, jnp.where(own_beside, nothing, beside)], 1
    )
    pairs_0 = []
    pairs_1 = []
    for device in range(devices):
        source = beside_of(device, devices)
        if source is not None:
            pairs_0.append((source, device))
        source = beside_of(device ^ 1, devices)
        if source is not None and source != device:
            pairs_1.append((source, device))
    swap = [(device, device ^ 1) for device in range(devices)]

    total = jnp.zeros((devices * rows, devices * rows), jnp.float32)
    held = blank((comps, devices * rows, cells), jnp.bfloat16)
    for (comp, first, length), kind in zip(CHUNKS, KINDS):
        start, size = first * unit, length * unit
        piece = own[comp, :, start : start + size]
        if kind == 0:
            table, others = table_0, [lax.ppermute(piece, "tm", pairs_0)]
        else:
            table, others = table_1, [lax.ppermute(piece, "tm", swap), lax.ppermute(piece, "tm", pairs_1)]
        messages = transform(table, own, others, comp, start, size, devices, rows, unit)
        landed = [None] * devices
        across = list(range(devices // 2, devices))
        inside = list(range(1, devices // 2)) + [0]
        for place in [p for pair in zip(across, inside) for p in pair]:
            landed[place ^ kind] = (
                messages[0]
                if place == 0
                else lax.ppermute(messages[place], "tm", [(d, d ^ place) for d in range(devices)])
            )
        held, total = gram(landed, weights, total, held, comp, start, size, unit)
    step = 1
    while step < spaces:
        total = total + lax.ppermute(total, "space", [(d, d ^ step) for d in range(spaces)])
        step *= 2

    slot = jnp.arange(devices, dtype=jnp.int32)
    role = jnp.bitwise_xor(me, slot)
    block = jnp.where(role < devices // 2, role, role - 1)
    to_block = (block[None, :] == jnp.arange(devices - 1, dtype=jnp.int32)[:, None]).astype(jnp.float32)
    products = total.reshape(devices, freqs, 2, devices, freqs, 2)
    same = jnp.eye(freqs, dtype=jnp.float32)[None, :, None, None, :, None]
    products = jnp.sum(products * same, axis=4)
    products = jnp.einsum(
        "ai,ifrjs,bj->frasb", to_block, products, to_block, precision=top_precision
    )
    gram_re = products[:, 0, :, 0, :] + products[:, 1, :, 1, :]
    gram_im = products[:, 0, :, 1, :] - products[:, 1, :, 0, :]
    vec_re, vec_im, energies = power_sweeps(gram_re * gram_scale, gram_im * gram_scale)
    mixing = mixing_rows(vec_re, vec_im, factor)
    spread = jnp.einsum("fkorb,bi->fkoir", mixing, to_block, precision=top_precision)
    eye = jnp.eye(freqs, dtype=jnp.float32)
    mix = spread[:, :, :, :, None, :] * eye[:, None, None, None, :, None]
    mix = mix.reshape(freqs * MODES * 2, devices * rows).astype(jnp.bfloat16)
    out = modes_of(mix, held, freqs, cells // 8)
    return (energies, jnp.transpose(out, (0, 1, 3, 2, 4)))


def solution(mesh):
    return jax.shard_map(
        per_device,
        mesh=mesh,
        in_specs=(P("tm", None, "space"), P("space"), P()),
        out_specs=(P("tm", None), P("tm", None, None, None, "space")),
        check_vma=False,
    )
```

time: 611 us -> 498 us (0.82)
  waiting for transfers between devices: 403 us -> 235 us
  starting transfers between devices: 9.56 us -> 125 us
  Pallas kernels: 0 us -> 99.9 us
  local copies, waits for them, and re-layouts: 99.4 us -> 15.4 us
  matrix products: 60.7 us -> 3.47 us
  blocking collectives: 11.4 us -> 0 us
  other arithmetic: 21.1 us -> 11.3 us
    all_to_all x1 -> x0, waiting for transfers between devices: 267 us -> none  [per_device(): lax.all_to_all(ordered[None], 'tm', split_axis=2, concat_axis=0, tiled=True)]
    ppermute x1 -> x70, starting transfers between devices: 3.29 us -> 125 us  [the longest x56 87 us: per_device(): lax.ppermute(messages[place], 'tm', [(d, d ^ place) for d in range(device...]
    pallas_call x0 -> x18, Pallas kernels: none -> 99.9 us  [the longest x8 44.7 us: transform(): pl.pallas_call(functools.partial(transform_kernel, 1 + len(others), rows)...]
    ppermute x1 -> x70, waiting for transfers between devices: 136 us -> 235 us  [the longest x56 168 us: per_device(): lax.ppermute(messages[place], 'tm', [(d, d ^ place) for d in range(device...]
    dot_general x3, matrix products: 58.1 us -> 0.89 us  [the longest x2 0.74 us: per_device(): jnp.einsum('ai,ifrjs,bj->frasb', to_block, products, to_block, precision=...]
    reshape x3 -> x1, local copies, waits for them, and re-layouts: 36.7 us -> 1.36 us  [per_device(): products = total.reshape(devices, freqs, 2, devices, freqs, 2)]
    gather x1 -> x0, local copies, waits for them, and re-layouts: 31.3 us -> none  [per_device(): ordered = jnp.take(spectra.reshape(2, NF, -1), freq_order, axis=1)]
    all_to_all x1 -> x0, local copies, waits for them, and re-layouts: 14.5 us -> none  [per_device(): lax.all_to_all(ordered[None], 'tm', split_axis=2, concat_axis=0, tiled=True)]
  transfers between devices with their start and end apart: 2 -> 70, of which waited for: 2 -> 32; matrix products, arithmetic and copies ran while one was open for 0% -> 2% of each run, Pallas kernels for 0% -> 16%
where the time goes in v1:
time: 498 us; the launch traced here: 493 us
  waiting for transfers between devices  235 us (47%)
  starting transfers between devices  125 us (25%)
  Pallas kernels  99.9 us (20%)
  local copies, waits for them, and re-layouts  15.4 us (3%)
  other arithmetic  11.3 us (2%)
    ppermute x56, waiting for transfers between devices, per_device(): lax.ppermute(messages[place], 'tm', [(d, d ^ place) for d in range(device...  168 us
    ppermute x56, starting transfers between devices, per_device(): lax.ppermute(messages[place], 'tm', [(d, d ^ place) for d in range(device...  87 us
    pallas_call x8, Pallas kernels, transform(): pl.pallas_call(functools.partial(transform_kernel, 1 + len(others), rows)...  44.7 us
    ppermute x4, waiting for transfers between devices, per_device(): table, others = (table_0, [lax.ppermute(piece, 'tm', pairs_0)])  40.2 us
    pallas_call x8, Pallas kernels, gram(): pl.pallas_call(functools.partial(gram_kernel, count), grid=(size // tile,...  37 us
    ppermute x4, waiting for transfers between devices, per_device(): lax.ppermute(piece, 'tm', pairs_1)  19.9 us
    pallas_call x1, Pallas kernels, modes_of(): pl.pallas_call(modes_kernel, grid=(comps, cells // tile), in_specs=[pl.Bl...  18.1 us
    ppermute x4, starting transfers between devices, per_device(): table, others = (table_0, [lax.ppermute(piece, 'tm', pairs_0)])  17.4 us
  transfers between devices with their start and end apart: 70, of which 32 were waited for; matrix products, arithmetic and copies ran while one was open for 2% of the time, Pallas kernels for 16%

profile of v1, /device:TPU:8, one launch (start us, length us, event | category | flops | bytes accessed | tf_op | source)
XLA Modules:
  0.0 492.9 jit_solution(5463657209802627580)
XLA Ops:
  14.9 20.2 %collective-permute-done.60.refs_1_ = bf16[32,4096]{1,0:T(8,128)(2,1)S(1)} collective-permute-done((bf16[32,4096]{1,0:T(8,128)(2,1)S(1)}, bf16[32,4096]{1,0:T(8,128)(2,1)S(1)}, u32[]{:S(2)}, u32[]{:S(2)}) %collective-permute-start.60) | collective-permute-done | bytes 262176 | tf_op jit(solution)/shard_map/ppermute | solution.py:268
  35.1 5.3 %collective-permute-start.9 = (bf16[32,12288]{1,0:T(8,128)(2,1)}, bf16[32,12288]{1,0:T(8,128)(2,1)S(1)}, u32[]{:S(2)}, u32[]{:S(2)}) collective-permute-start(bf16[32,12288]{1,0:T(8,128)(2,1)} %get-tuple-element.266), channel_id=1, source_target_pairs={{4,0},{8,4},{12,8},{16,20},{20,24},{24,28},{5,1},{9,5},{13,9},{17,... | collective-permute-start | bytes 2359304 | tf_op jit(solution)/shard_map/ppermute | solution.py:268
  43.4 4.0 slice_bitcast_fusion
  47.4 9.3 %collective-permute-done.61.refs_1_ = bf16[8,4096]{1,0:T(8,128)(2,1)S(1)} collective-permute-done((bf16[8,4096]{1,0:T(8,128)(2,1)}, bf16[8,4096]{1,0:T(8,128)(2,1)S(1)}, u32[]{:S(2)}, u32[]{:S(2)}) %collective-permute-start.61) | collective-permute-done | bytes 65568 | tf_op jit(solution)/shard_map/ppermute | solution.py:279
  57.3 6.2 %collective-permute-start.43 = (bf16[32,16384]{1,0:T(8,128)(2,1)}, bf16[32,16384]{1,0:T(8,128)(2,1)S(1)}, u32[]{:S(2)}, u32[]{:S(2)}) collective-permute-start(bf16[32,16384]{1,0:T(8,128)(2,1)} %get-tuple-element.267), channel_id=1, source_target_pairs={{4,0},{8,4},{12,8},{16,20},{20,24},{24,28},{5,1},{9,5},{13,9},{17,... | collective-permute-start | bytes 3145736 | tf_op jit(solution)/shard_map/ppermute | solution.py:268
  63.6 4.1 collective-permute-start.64
  69.1 5.8 %transform.14 = (bf16[8,12288]{1,0:T(8,128)(2,1)}, bf16[8,12288]{1,0:T(8,128)(2,1)}, bf16[8,12288]{1,0:T(8,128)(2,1)}, bf16[8,12288]{1,0:T(8,128)(2,1)}, bf16[8,...) custom-call(bf16[64,96]{1,0:T(8,128)(2,1)} %pad_maximum_fusion.table_ref, ...), custom_call_target="tpu_custom_call" | custom-call | flops 150994944 | bytes 3932160 | tf_op jit(solution)/shard_map/transform/pallas_call | solution.py:85
  74.9 15.3 %collective-permute-done.63.refs_3_ = bf16[8,4096]{1,0:T(8,128)(2,1)S(1)} collective-permute-done((bf16[8,4096]{1,0:T(8,128)(2,1)}, bf16[8,4096]{1,0:T(8,128)(2,1)S(1)}, u32[]{:S(2)}, u32[]{:S(2)}) %collective-permute-start.63) | collective-permute-done | bytes 65568 | tf_op jit(solution)/shard_map/ppermute | solution.py:279
  99.9 4.7 collective-permute-start.3
  110.6 3.7 collective-permute-start.57
  114.3 5.5 %transform.9 = (bf16[8,12288]{1,0:T(8,128)(2,1)}, bf16[8,12288]{1,0:T(8,128)(2,1)}, bf16[8,12288]{1,0:T(8,128)(2,1)}, bf16[8,12288]{1,0:T(8,128)(2,1)}, bf16[8,1...) custom-call(bf16[64,64]{1,0:T(8,128)(2,1)} %pad_maximum_fusion.1.table_ref, ...), custom_call_target="tpu_custom_call" | custom-call | flops 100663296 | bytes 3145728 | tf_op jit(solution)/shard_map/transform/pallas_call | solution.py:85
  121.5 9.4 %collective-permute-done.56.refs_4_ = bf16[8,12288]{1,0:T(8,128)(2,1)S(1)} collective-permute-done((bf16[8,12288]{1,0:T(8,128)(2,1)}, bf16[8,12288]{1,0:T(8,128)(2,1)S(1)}, u32[]{:S(2)}, u32[]{:S(2)}) %collective-permute-start.56) | collective-permute-done | bytes 196640 | tf_op jit(solution)/shard_map/ppermute | solution.py:279
  130.9 5.2 %collective-permute-done.57.refs_5_ = bf16[8,12288]{1,0:T(8,128)(2,1)} collective-permute-done((bf16[8,12288]{1,0:T(8,128)(2,1)}, bf16[8,12288]{1,0:T(8,128)(2,1)}, u32[]{:S(2)}, u32[]{:S(2)}) %collective-permute-start.57) | collective-permute-done | bytes 196640 | tf_op jit(solution)/shard_map/ppermute | solution.py:279
  136.1 3.4 collective-permute-start.11
  142.0 8.1 %collective-permute-done.59.refs_7_ = bf16[8,12288]{1,0:T(8,128)(2,1)S(1)} collective-permute-done((bf16[8,12288]{1,0:T(8,128)(2,1)}, bf16[8,12288]{1,0:T(8,128)(2,1)S(1)}, u32[]{:S(2)}, u32[]{:S(2)}) %collective-permute-start.59) | collective-permute-done | bytes 196640 | tf_op jit(solution)/shard_map/ppermute | solution.py:279
  154.7 7.4 %collective-permute-done.13.refs_4_ = bf16[8,12288]{1,0:T(8,128)(2,1)S(1)} collective-permute-done((bf16[8,12288]{1,0:T(8,128)(2,1)}, bf16[8,12288]{1,0:T(8,128)(2,1)S(1)}, u32[]{:S(2)}, u32[]{:S(2)}) %collective-permute-start.13) | collective-permute-done | bytes 196640 | tf_op jit(solution)/shard_map/ppermute | solution.py:279
  162.1 5.1 %collective-permute-start.35 = (bf16[32,16384]{1,0:T(8,128)(2,1)}, bf16[32,16384]{1,0:T(8,128)(2,1)}, u32[]{:S(2)}, u32[]{:S(2)}) collective-permute-start(bf16[32,16384]{1,0:T(8,128)(2,1)} %get-tuple-element.268), channel_id=1, source_target_pairs={{8,0},{20,28},{9,1},{21,29},{10,2},{22,30},{11,3},{23,31}} | collective-permute-start | bytes 3145736 | tf_op jit(solution)/shard_map/ppermute | solution.py:270
  167.9 4.0 collective-permute-start.26
  172.1 7.2 %collective-permute-done.16.refs_7_ = bf16[8,12288]{1,0:T(8,128)(2,1)S(1)} collective-permute-done((bf16[8,12288]{1,0:T(8,128)(2,1)}, bf16[8,12288]{1,0:T(8,128)(2,1)S(1)}, u32[]{:S(2)}, u32[]{:S(2)}) %collective-permute-start.16) | collective-permute-done | bytes 196640 | tf_op jit(solution)/shard_map/ppermute | solution.py:279
  184.3 6.9 %transform.13 = (bf16[8,16384]{1,0:T(8,128)(2,1)}, bf16[8,16384]{1,0:T(8,128)(2,1)}, bf16[8,16384]{1,0:T(8,128)(2,1)}, bf16[8,16384]{1,0:T(8,128)(2,1)}, bf16[8,...) custom-call(bf16[64,64]{1,0:T(8,128)(2,1)} %pad_maximum_fusion.1.table_ref, ...), custom_call_target="tpu_custom_call" | custom-call | flops 134217728 | bytes 4194304 | tf_op jit(solution)/shard_map/transform/pallas_call | solution.py:85
  196.8 20.0 %collective-permute-done.26.refs_1_ = bf16[32,16384]{1,0:T(8,128)(2,1)S(1)} collective-permute-done((bf16[32,16384]{1,0:T(8,128)(2,1)}, bf16[32,16384]{1,0:T(8,128)(2,1)S(1)}, u32[]{:S(2)}, u32[]{:S(2)}) %collective-permute-start.26) | collective-permute-done | bytes 1048608 | tf_op jit(solution)/shard_map/ppermute | solution.py:268
  220.1 7.4 %transform.12 = (bf16[8,16384]{1,0:T(8,128)(2,1)}, bf16[8,16384]{1,0:T(8,128)(2,1)}, bf16[8,16384]{1,0:T(8,128)(2,1)}, bf16[8,16384]{1,0:T(8,128)(2,1)}, bf16[8,...) custom-call(bf16[64,96]{1,0:T(8,128)(2,1)} %pad_maximum_fusion.table_ref, ...), custom_call_target="tpu_custom_call" | custom-call | flops 201326592 | bytes 5242880 | tf_op jit(solution)/shard_map/transform/pallas_call | solution.py:85
  227.5 5.2 %collective-permute-done.17.refs_1_ = bf16[32,16384]{1,0:T(8,128)(2,1)} collective-permute-done((bf16[32,16384]{1,0:T(8,128)(2,1)S(1)}, bf16[32,16384]{1,0:T(8,128)(2,1)}, u32[]{:S(2)}, u32[]{:S(2)}) %collective-permute-start.17) | collective-permute-done | bytes 1048608 | tf_op jit(solution)/shard_map/ppermute | solution.py:270
  232.7 16.9 %collective-permute-done.18.refs_2_ = bf16[32,16384]{1,0:T(8,128)(2,1)} collective-permute-done((bf16[32,16384]{1,0:T(8,128)(2,1)S(1)}, bf16[32,16384]{1,0:T(8,128)(2,1)}, u32[]{:S(2)}, u32[]{:S(2)}) %collective-permute-start.18) | collective-permute-done | bytes 1048608 | tf_op jit(solution)/shard_map/ppermute | solution.py:270
  249.6 5.1 %collective-permute-start.48 = (bf16[8,16384]{1,0:T(8,128)(2,1)}, bf16[8,16384]{1,0:T(8,128)(2,1)S(1)}, u32[]{:S(2)}, u32[]{:S(2)}) collective-permute-start(bf16[8,16384]{1,0:T(8,128)(2,1)} %get-tuple-element.127), channel_id=1, source_target_pairs={{0,20},{4,16},{8,28},{12,24},{16,4},{20,0},{24,12},{28,8},{1,21},{... | collective-permute-start | bytes 786440 | tf_op jit(solution)/shard_map/ppermute | solution.py:279
  254.7 11.0 %collective-permute-done.45.refs_2_ = bf16[8,16384]{1,0:T(8,128)(2,1)S(1)} collective-permute-done((bf16[8,16384]{1,0:T(8,128)(2,1)}, bf16[8,16384]{1,0:T(8,128)(2,1)S(1)}, u32[]{:S(2)}, u32[]{:S(2)}) %collective-permute-start.45) | collective-permute-done | bytes 262176 | tf_op jit(solution)/shard_map/ppermute | solution.py:279
  266.9 5.9 %collective-permute-done.46.refs_3_ = bf16[8,16384]{1,0:T(8,128)(2,1)S(1)} collective-permute-done((bf16[8,16384]{1,0:T(8,128)(2,1)}, bf16[8,16384]{1,0:T(8,128)(2,1)S(1)}, u32[]{:S(2)}, u32[]{:S(2)}) %collective-permute-start.46) | collective-permute-done | bytes 262176 | tf_op jit(solution)/shard_map/ppermute | solution.py:279
  276.9 4.2 collective-permute-done.49.refs_6_
  281.1 15.1 %collective-permute-done.50.refs_7_ = bf16[8,16384]{1,0:T(8,128)(2,1)S(1)} collective-permute-done((bf16[8,16384]{1,0:T(8,128)(2,1)}, bf16[8,16384]{1,0:T(8,128)(2,1)S(1)}, u32[]{:S(2)}, u32[]{:S(2)}) %collective-permute-start.50) | collective-permute-done | bytes 262176 | tf_op jit(solution)/shard_map/ppermute | solution.py:279
  299.3 6.9 %transform.11 = (bf16[8,16384]{1,0:T(8,128)(2,1)}, bf16[8,16384]{1,0:T(8,128)(2,1)}, bf16[8,16384]{1,0:T(8,128)(2,1)}, bf16[8,16384]{1,0:T(8,128)(2,1)}, bf16[8,...) custom-call(bf16[64,64]{1,0:T(8,128)(2,1)} %pad_maximum_fusion.1.table_ref, ...), custom_call_target="tpu_custom_call" | custom-call | flops 134217728 | bytes 4194304 | tf_op jit(solution)/shard_map/transform/pallas_call | solution.py:85
  311.6 5.7 %collective-permute-done.40.refs_5_ = bf16[8,16384]{1,0:T(8,128)(2,1)} collective-permute-done((bf16[8,16384]{1,0:T(8,128)(2,1)}, bf16[8,16384]{1,0:T(8,128)(2,1)}, u32[]{:S(2)}, u32[]{:S(2)}) %collective-permute-start.40) | collective-permute-done | bytes 262176 | tf_op jit(solution)/shard_map/ppermute | solution.py:279
  317.3 3.6 collective-permute-start.29
  320.8 13.9 %collective-permute-done.41.refs_6_ = bf16[8,16384]{1,0:T(8,128)(2,1)} collective-permute-done((bf16[8,16384]{1,0:T(8,128)(2,1)}, bf16[8,16384]{1,0:T(8,128)(2,1)}, u32[]{:S(2)}, u32[]{:S(2)}) %collective-permute-start.41) | collective-permute-done | bytes 262176 | tf_op jit(solution)/shard_map/ppermute | solution.py:279
  334.7 7.3 %transform.10 = (bf16[8,16384]{1,0:T(8,128)(2,1)}, bf16[8,16384]{1,0:T(8,128)(2,1)}, bf16[8,16384]{1,0:T(8,128)(2,1)}, bf16[8,16384]{1,0:T(8,128)(2,1)}, bf16[8,...) custom-call(bf16[64,96]{1,0:T(8,128)(2,1)} %pad_maximum_fusion.table_ref, ...), custom_call_target="tpu_custom_call" | custom-call | flops 201326592 | bytes 5242880 | tf_op jit(solution)/shard_map/transform/pallas_call | solution.py:85
  342.1 5.8 %collective-permute-start.32 = (bf16[8,16384]{1,0:T(8,128)(2,1)}, bf16[8,16384]{1,0:T(8,128)(2,1)}, u32[]{:S(2)}, u32[]{:S(2)}) collective-permute-start(bf16[8,16384]{1,0:T(8,128)(2,1)} %get-tuple-element.112), channel_id=1, source_target_pairs={{0,24},{4,28},{8,16},{12,20},{16,8},{20,12},{24,0},{28,4},{1,25},{... | collective-permute-start | bytes 786440 | tf_op jit(solution)/shard_map/ppermute | solution.py:279
  349.4 12.9 %collective-permute-done.30.refs_4_ = bf16[8,16384]{1,0:T(8,128)(2,1)} collective-permute-done((bf16[8,16384]{1,0:T(8,128)(2,1)}, bf16[8,16384]{1,0:T(8,128)(2,1)}, u32[]{:S(2)}, u32[]{:S(2)}) %collective-permute-start.30) | collective-permute-done | bytes 262176 | tf_op jit(solution)/shard_map/ppermute | solution.py:279
  362.3 5.6 %collective-permute-done.31.refs_5_ = bf16[8,16384]{1,0:T(8,128)(2,1)} collective-permute-done((bf16[8,16384]{1,0:T(8,128)(2,1)}, bf16[8,16384]{1,0:T(8,128)(2,1)}, u32[]{:S(2)}, u32[]{:S(2)}) %collective-permute-start.31) | collective-permute-done | bytes 262176 | tf_op jit(solution)/shard_map/ppermute | solution.py:279
  373.8 13.7 %collective-permute-done.33.refs_7_ = bf16[8,16384]{1,0:T(8,128)(2,1)} collective-permute-done((bf16[8,16384]{1,0:T(8,128)(2,1)}, bf16[8,16384]{1,0:T(8,128)(2,1)}, u32[]{:S(2)}, u32[]{:S(2)}) %collective-permute-start.33) | collective-permute-done | bytes 262176 | tf_op jit(solution)/shard_map/ppermute | solution.py:279
  393.2 5.3 %collective-permute-start.4 = (bf16[8,4096]{1,0:T(8,128)(2,1)}, bf16[8,4096]{1,0:T(8,128)(2,1)S(1)}, u32[]{:S(2)}, u32[]{:S(2)}) collective-permute-start(bf16[8,4096]{1,0:T(8,128)(2,1)} %get-tuple-element.85), channel_id=1, source_target_pairs={{0,8},{4,12},{8,0},{12,4},{16,24},{20,28},{24,16},{28,20},{1,9},{5... | collective-permute-start | bytes 196616 | tf_op jit(solution)/shard_map/ppermute | solution.py:279
  401.5 4.4 collective-permute-start.5
  408.0 3.4 collective-permute-start.6
  419.5 4.7 gram.9
  424.2 5.9 %gram.10 = (bf16[3,64,32768]{2,1,0:T(8,128)(2,1)}, f32[64,64]{1,0:T(8,128)}) custom-call(f32[1,32768]{1,0:T(1,128)} %bitcast.500, bf16[8,16384]{1,0:T(8,128)(2,1)} %get-tuple-element.122.refs_0_, bf16[8,16384]{1,0:T(8,128)(2,1)} %copy-done.3, bf16[8,16384]{1,0:T(8,128)(2,1)} %copy-done.4, ...), custom_call_target="tpu_custom_call", output_to_operand_aliasing={{0}: (10, {})} | custom-call | flops 134217728 | bytes 4194304 | tf_op jit(solution)/shard_map/gram/pallas_call | solution.py:120
  430.0 5.9 %gram.11 = (bf16[3,64,32768]{2,1,0:T(8,128)(2,1)}, f32[64,64]{1,0:T(8,128)}) custom-call(f32[1,32768]{1,0:T(1,128)} %bitcast.501, bf16[8,16384]{1,0:T(8,128)(2,1)} %copy-done.9, bf16[8,16384]{1,0:T(8,128)(2,1)} %get-tuple-element.115.refs_1_, bf16[8,16384]{1,0:T(8,128)(2,1)} %copy-done.11, ...), custom_call_target="tpu_custom_call", output_to_operand_aliasing={{0}: (10, {})} | custom-call | flops 134217728 | bytes 4194304 | tf_op jit(solution)/shard_map/gram/pallas_call | solution.py:120
  435.9 5.9 %gram.12 = (bf16[3,64,32768]{2,1,0:T(8,128)(2,1)}, f32[64,64]{1,0:T(8,128)}) custom-call(f32[1,32768]{1,0:T(1,128)} %bitcast.502, bf16[8,16384]{1,0:T(8,128)(2,1)} %get-tuple-element.106.refs_0_, bf16[8,16384]{1,0:T(8,128)(2,1)} %copy-done.12, bf16[8,16384]{1,0:T(8,128)(2,1)} %copy-done.14, ...), custom_call_target="tpu_custom_call", output_to_operand_aliasing={{0}: (10, {})} | custom-call | flops 134217728 | bytes 4194304 | tf_op jit(solution)/shard_map/gram/pallas_call | solution.py:120
  441.8 5.9 %gram.13 = (bf16[3,64,32768]{2,1,0:T(8,128)(2,1)}, f32[64,64]{1,0:T(8,128)}) custom-call(f32[1,32768]{1,0:T(1,128)} %bitcast.503, bf16[8,16384]{1,0:T(8,128)(2,1)} %collective-permute-done.19.refs_0_, bf16[8,16384]{1,0:T(8,128)(2,1)} %get-tuple-element.99.refs_1_, ...), custom_call_target="tpu_custom_call", output_to_operand_aliasing={{0}: (10, {})} | custom-call | flops 134217728 | bytes 4194304 | tf_op jit(solution)/shard_map/gram/pallas_call | solution.py:120
  447.6 4.7 gram.14
  474.8 18.1 %modes.1 = bf16[4,4,3,2,32768]{4,3,2,1,0:T(2,128)(2,1)} custom-call(bf16[32,64]{1,0:T(8,128)(2,1)} %convert_element_type.49.mix_ref, bf16[3,64,32768]{2,1,0:T(8,128)(2,1)} %get-tuple-element.161.held_ref), custom_call_target="tpu_custom_call" | custom-call | tf_op jit(solution)/shard_map/modes/pallas_call | solution.py:149
  (296 shorter events, 118.9 us)
Async XLA Ops:
  3.3 60.3 %collective-permute-start.51 = (bf16[32,12288]{1,0:T(8,128)(2,1)}, bf16[32,12288]{1,0:T(8,128)(2,1)}, u32[]{:S(2)}, u32[]{:S(2)}) collective-permute-start(bf16[32,12288]{1,0:T(8,128)(2,1)} %get-tuple-element.265), channel_id=1, source_target_pairs={{0,4},{4,0},{8,12},{12,8},{16,20},{20,16},{24,28},{28,24},{1,5},{5... | collective-permute-start | bytes 2359304 | tf_op jit(solution)/shard_map/ppermute | solution.py:270
  4.8 62.9 %collective-permute-start.52 = (bf16[32,12288]{1,0:T(8,128)(2,1)}, bf16[32,12288]{1,0:T(8,128)(2,1)}, u32[]{:S(2)}, u32[]{:S(2)}) collective-permute-start(bf16[32,12288]{1,0:T(8,128)(2,1)} %get-tuple-element.265), channel_id=1, source_target_pairs={{8,0},{20,28},{9,1},{21,29},{10,2},{22,30},{11,3},{23,31}} | collective-permute-start | bytes 2359304 | tf_op jit(solution)/shard_map/ppermute | solution.py:270
  9.1 33.7 %collective-permute-start = (bf16[32,4096]{1,0:T(8,128)(2,1)S(1)}, bf16[32,4096]{1,0:T(8,128)(2,1)S(1)}, u32[]{:S(2)}, u32[]{:S(2)}) collective-permute-start(bf16[32,4096]{1,0:T(8,128)(2,1)S(1)} %get-tuple-element.264), channel_id=1, source_target_pairs={{0,4},{4,0},{8,12},{12,8},{16,20},{20,16},{24,28},{28,24},{1,5},{5... | collective-permute-start | bytes 786440 | tf_op jit(solution)/shard_map/ppermute | solution.py:270
  9.2 33.7 %collective-permute-start.1 = (bf16[32,4096]{1,0:T(8,128)(2,1)S(1)}, bf16[32,4096]{1,0:T(8,128)(2,1)S(1)}, u32[]{:S(2)}, u32[]{:S(2)}) collective-permute-start(bf16[32,4096]{1,0:T(8,128)(2,1)S(1)} %get-tuple-element.264), channel_id=1, source_target_pairs={{8,0},{20,28},{9,1},{21,29},{10,2},{22,30},{11,3},{23,31}} | collective-permute-start | bytes 786440 | tf_op jit(solution)/shard_map/ppermute | solution.py:270
  10.5 24.6 %collective-permute-start.60 = (bf16[32,4096]{1,0:T(8,128)(2,1)S(1)}, bf16[32,4096]{1,0:T(8,128)(2,1)S(1)}, u32[]{:S(2)}, u32[]{:S(2)}) collective-permute-start(bf16[32,4096]{1,0:T(8,128)(2,1)S(1)} %get-tuple-element.263), channel_id=1, source_target_pairs={{4,0},{8,4},{12,8},{16,20},{20,24},{24,28},{5,1},{9,5},{13,9},{17,... | collective-permute-start | bytes 786440 | tf_op jit(solution)/shard_map/ppermute | solution.py:268
  35.1 74.9 %collective-permute-start.9 = (bf16[32,12288]{1,0:T(8,128)(2,1)}, bf16[32,12288]{1,0:T(8,128)(2,1)S(1)}, u32[]{:S(2)}, u32[]{:S(2)}) collective-permute-start(bf16[32,12288]{1,0:T(8,128)(2,1)} %get-tuple-element.266), channel_id=1, source_target_pairs={{4,0},{8,4},{12,8},{16,20},{20,24},{24,28},{5,1},{9,5},{13,9},{17,... | collective-permute-start | bytes 2359304 | tf_op jit(solution)/shard_map/ppermute | solution.py:268
  57.3 123.7 %collective-permute-start.43 = (bf16[32,16384]{1,0:T(8,128)(2,1)}, bf16[32,16384]{1,0:T(8,128)(2,1)S(1)}, u32[]{:S(2)}, u32[]{:S(2)}) collective-permute-start(bf16[32,16384]{1,0:T(8,128)(2,1)} %get-tuple-element.267), channel_id=1, source_target_pairs={{4,0},{8,4},{12,8},{16,20},{20,24},{24,28},{5,1},{9,5},{13,9},{17,... | collective-permute-start | bytes 3145736 | tf_op jit(solution)/shard_map/ppermute | solution.py:268
  63.5 26.7 %collective-permute-start.63 = (bf16[8,4096]{1,0:T(8,128)(2,1)}, bf16[8,4096]{1,0:T(8,128)(2,1)S(1)}, u32[]{:S(2)}, u32[]{:S(2)}) collective-permute-start(bf16[8,4096]{1,0:T(8,128)(2,1)} %get-tuple-element.141), channel_id=1, source_target_pairs={{0,12},{4,8},{8,4},{12,0},{16,28},{20,24},{24,20},{28,16},{1,13},{... | collective-permute-start | bytes 196616 | tf_op jit(solution)/shard_map/ppermute | solution.py:279
  63.6 26.7 %collective-permute-start.64 = (bf16[8,4096]{1,0:T(8,128)(2,1)}, bf16[8,4096]{1,0:T(8,128)(2,1)S(1)}, u32[]{:S(2)}, u32[]{:S(2)}) collective-permute-start(bf16[8,4096]{1,0:T(8,128)(2,1)} %get-tuple-element.142), channel_id=1, source_target_pairs={{0,16},{4,20},{8,24},{12,28},{16,0},{20,4},{24,8},{28,12},{1,17},{... | collective-permute-start | bytes 196616 | tf_op jit(solution)/shard_map/ppermute | solution.py:279
  67.7 25.4 %collective-permute-start.65 = (bf16[8,4096]{1,0:T(8,128)(2,1)}, bf16[8,4096]{1,0:T(8,128)(2,1)}, u32[]{:S(2)}, u32[]{:S(2)}) collective-permute-start(bf16[8,4096]{1,0:T(8,128)(2,1)} %get-tuple-element.143), channel_id=1, source_target_pairs={{0,20},{4,16},{8,28},{12,24},{16,4},{20,0},{24,12},{28,8},{1,21},{... | collective-permute-start | bytes 196616 | tf_op jit(solution)/shard_map/ppermute | solution.py:279
  110.6 25.6 %collective-permute-start.57 = (bf16[8,12288]{1,0:T(8,128)(2,1)}, bf16[8,12288]{1,0:T(8,128)(2,1)}, u32[]{:S(2)}, u32[]{:S(2)}) collective-permute-start(bf16[8,12288]{1,0:T(8,128)(2,1)} %get-tuple-element.135), channel_id=1, source_target_pairs={{0,16},{4,20},{8,24},{12,28},{16,0},{20,4},{24,8},{28,12},{1,17},{... | collective-permute-start | bytes 589832 | tf_op jit(solution)/shard_map/ppermute | solution.py:279
  120.4 29.7 %collective-permute-start.59 = (bf16[8,12288]{1,0:T(8,128)(2,1)}, bf16[8,12288]{1,0:T(8,128)(2,1)S(1)}, u32[]{:S(2)}, u32[]{:S(2)}) collective-permute-start(bf16[8,12288]{1,0:T(8,128)(2,1)} %get-tuple-element.137), channel_id=1, source_target_pairs={{0,24},{4,28},{8,16},{12,20},{16,8},{20,12},{24,0},{28,4},{1,25},{... | collective-permute-start | bytes 589832 | tf_op jit(solution)/shard_map/ppermute | solution.py:279
  151.7 39.5 %collective-permute-start.34 = (bf16[32,16384]{1,0:T(8,128)(2,1)}, bf16[32,16384]{1,0:T(8,128)(2,1)}, u32[]{:S(2)}, u32[]{:S(2)}) collective-permute-start(bf16[32,16384]{1,0:T(8,128)(2,1)} %get-tuple-element.268), channel_id=1, source_target_pairs={{0,4},{4,0},{8,12},{12,8},{16,20},{20,16},{24,28},{28,24},{1,5},{5... | collective-permute-start | bytes 3145736 | tf_op jit(solution)/shard_map/ppermute | solution.py:270
  162.1 32.2 %collective-permute-start.35 = (bf16[32,16384]{1,0:T(8,128)(2,1)}, bf16[32,16384]{1,0:T(8,128)(2,1)}, u32[]{:S(2)}, u32[]{:S(2)}) collective-permute-start(bf16[32,16384]{1,0:T(8,128)(2,1)} %get-tuple-element.268), channel_id=1, source_target_pairs={{8,0},{20,28},{9,1},{21,29},{10,2},{22,30},{11,3},{23,31}} | collective-permute-start | bytes 3145736 | tf_op jit(solution)/shard_map/ppermute | solution.py:270
  167.9 48.9 %collective-permute-start.26 = (bf16[32,16384]{1,0:T(8,128)(2,1)}, bf16[32,16384]{1,0:T(8,128)(2,1)S(1)}, u32[]{:S(2)}, u32[]{:S(2)}) collective-permute-start(bf16[32,16384]{1,0:T(8,128)(2,1)} %get-tuple-element.269), channel_id=1, source_target_pairs={{4,0},{8,4},{12,8},{16,20},{20,24},{24,28},{5,1},{9,5},{13,9},{17,... | collective-permute-start | bytes 3145736 | tf_op jit(solution)/shard_map/ppermute | solution.py:268
  179.3 53.5 %collective-permute-start.17 = (bf16[32,16384]{1,0:T(8,128)(2,1)S(1)}, bf16[32,16384]{1,0:T(8,128)(2,1)}, u32[]{:S(2)}, u32[]{:S(2)}) collective-permute-start(bf16[32,16384]{1,0:T(8,128)(2,1)S(1)} %get-tuple-element.270), channel_id=1, source_target_pairs={{0,4},{4,0},{8,12},{12,8},{16,20},{20,16},{24,28},{28,24},{1,5},{5... | collective-permute-start | bytes 3145736 | tf_op jit(solution)/shard_map/ppermute | solution.py:270
  181.0 68.6 %collective-permute-start.18 = (bf16[32,16384]{1,0:T(8,128)(2,1)S(1)}, bf16[32,16384]{1,0:T(8,128)(2,1)}, u32[]{:S(2)}, u32[]{:S(2)}) collective-permute-start(bf16[32,16384]{1,0:T(8,128)(2,1)S(1)} %get-tuple-element.270), channel_id=1, source_target_pairs={{8,0},{20,28},{9,1},{21,29},{10,2},{22,30},{11,3},{23,31}} | collective-permute-start | bytes 3145736 | tf_op jit(solution)/shard_map/ppermute | solution.py:270
  191.2 63.5 %collective-permute-start.44 = (bf16[8,16384]{1,0:T(8,128)(2,1)}, bf16[8,16384]{1,0:T(8,128)(2,1)S(1)}, u32[]{:S(2)}, u32[]{:S(2)}) collective-permute-start(bf16[8,16384]{1,0:T(8,128)(2,1)} %get-tuple-element.123), channel_id=1, source_target_pairs={{0,4},{4,0},{8,12},{12,8},{16,20},{20,16},{24,28},{28,24},{1,5},{5... | collective-permute-start | bytes 786440 | tf_op jit(solution)/shard_map/ppermute | solution.py:279
  194.3 71.4 %collective-permute-start.45 = (bf16[8,16384]{1,0:T(8,128)(2,1)}, bf16[8,16384]{1,0:T(8,128)(2,1)S(1)}, u32[]{:S(2)}, u32[]{:S(2)}) collective-permute-start(bf16[8,16384]{1,0:T(8,128)(2,1)} %get-tuple-element.124), channel_id=1, source_target_pairs={{0,8},{4,12},{8,0},{12,4},{16,24},{20,28},{24,16},{28,20},{1,9},{5... | collective-permute-start | bytes 786440 | tf_op jit(solution)/shard_map/ppermute | solution.py:279
  216.8 56.0 %collective-permute-start.46 = (bf16[8,16384]{1,0:T(8,128)(2,1)}, bf16[8,16384]{1,0:T(8,128)(2,1)S(1)}, u32[]{:S(2)}, u32[]{:S(2)}) collective-permute-start(bf16[8,16384]{1,0:T(8,128)(2,1)} %get-tuple-element.125), channel_id=1, source_target_pairs={{0,12},{4,8},{8,4},{12,0},{16,28},{20,24},{24,20},{28,16},{1,13},{... | collective-permute-start | bytes 786440 | tf_op jit(solution)/shard_map/ppermute | solution.py:279
  232.7 40.2 %collective-permute-start.47 = (bf16[8,16384]{1,0:T(8,128)(2,1)}, bf16[8,16384]{1,0:T(8,128)(2,1)S(1)}, u32[]{:S(2)}, u32[]{:S(2)}) collective-permute-start(bf16[8,16384]{1,0:T(8,128)(2,1)} %get-tuple-element.126), channel_id=1, source_target_pairs={{0,16},{4,20},{8,24},{12,28},{16,0},{20,4},{24,8},{28,12},{1,17},{... | collective-permute-start | bytes 786440 | tf_op jit(solution)/shard_map/ppermute | solution.py:279
  249.6 26.7 %collective-permute-start.48 = (bf16[8,16384]{1,0:T(8,128)(2,1)}, bf16[8,16384]{1,0:T(8,128)(2,1)S(1)}, u32[]{:S(2)}, u32[]{:S(2)}) collective-permute-start(bf16[8,16384]{1,0:T(8,128)(2,1)} %get-tuple-element.127), channel_id=1, source_target_pairs={{0,20},{4,16},{8,28},{12,24},{16,4},{20,0},{24,12},{28,8},{1,21},{... | collective-permute-start | bytes 786440 | tf_op jit(solution)/shard_map/ppermute | solution.py:279
  254.7 26.3 %collective-permute-start.49 = (bf16[8,16384]{1,0:T(8,128)(2,1)}, bf16[8,16384]{1,0:T(8,128)(2,1)S(1)}, u32[]{:S(2)}, u32[]{:S(2)}) collective-permute-start(bf16[8,16384]{1,0:T(8,128)(2,1)} %get-tuple-element.128), channel_id=1, source_target_pairs={{0,24},{4,28},{8,16},{12,20},{16,8},{20,12},{24,0},{28,4},{1,25},{... | collective-permute-start | bytes 786440 | tf_op jit(solution)/shard_map/ppermute | solution.py:279
  265.7 30.4 %collective-permute-start.50 = (bf16[8,16384]{1,0:T(8,128)(2,1)}, bf16[8,16384]{1,0:T(8,128)(2,1)S(1)}, u32[]{:S(2)}, u32[]{:S(2)}) collective-permute-start(bf16[8,16384]{1,0:T(8,128)(2,1)} %get-tuple-element.129), channel_id=1, source_target_pairs={{0,28},{4,24},{8,20},{12,16},{16,12},{20,8},{24,4},{28,0},{1,29},{... | collective-permute-start | bytes 786440 | tf_op jit(solution)/shard_map/ppermute | solution.py:279
  272.9 23.3 %collective-permute-start.36 = (bf16[8,16384]{1,0:T(8,128)(2,1)}, bf16[8,16384]{1,0:T(8,128)(2,1)S(1)}, u32[]{:S(2)}, u32[]{:S(2)}) collective-permute-start(bf16[8,16384]{1,0:T(8,128)(2,1)} %get-tuple-element.114), channel_id=1, source_target_pairs={{0,4},{4,0},{8,12},{12,8},{16,20},{20,16},{24,28},{28,24},{1,5},{5... | collective-permute-start | bytes 786440 | tf_op jit(solution)/shard_map/ppermute | solution.py:279
  272.9 33.3 %collective-permute-start.37 = (bf16[8,16384]{1,0:T(8,128)(2,1)}, bf16[8,16384]{1,0:T(8,128)(2,1)S(1)}, u32[]{:S(2)}, u32[]{:S(2)}) collective-permute-start(bf16[8,16384]{1,0:T(8,128)(2,1)} %get-tuple-element.116), channel_id=1, source_target_pairs={{0,12},{4,8},{8,4},{12,0},{16,28},{20,24},{24,20},{28,16},{1,13},{... | collective-permute-start | bytes 786440 | tf_op jit(solution)/shard_map/ppermute | solution.py:279
  276.2 30.1 %collective-permute-start.38 = (bf16[8,16384]{1,0:T(8,128)(2,1)}, bf16[8,16384]{1,0:T(8,128)(2,1)}, u32[]{:S(2)}, u32[]{:S(2)}) collective-permute-start(bf16[8,16384]{1,0:T(8,128)(2,1)} %get-tuple-element.117), channel_id=1, source_target_pairs={{0,8},{4,12},{8,0},{12,4},{16,24},{20,28},{24,16},{28,20},{1,9},{5... | collective-permute-start | bytes 786440 | tf_op jit(solution)/shard_map/ppermute | solution.py:279
  281.1 27.7 %collective-permute-start.39 = (bf16[8,16384]{1,0:T(8,128)(2,1)}, bf16[8,16384]{1,0:T(8,128)(2,1)}, u32[]{:S(2)}, u32[]{:S(2)}) collective-permute-start(bf16[8,16384]{1,0:T(8,128)(2,1)} %get-tuple-element.118), channel_id=1, source_target_pairs={{0,20},{4,16},{8,28},{12,24},{16,4},{20,0},{24,12},{28,8},{1,21},{... | collective-permute-start | bytes 786440 | tf_op jit(solution)/shard_map/ppermute | solution.py:279
  296.2 38.5 %collective-permute-start.41 = (bf16[8,16384]{1,0:T(8,128)(2,1)}, bf16[8,16384]{1,0:T(8,128)(2,1)}, u32[]{:S(2)}, u32[]{:S(2)}) collective-permute-start(bf16[8,16384]{1,0:T(8,128)(2,1)} %get-tuple-element.120), channel_id=1, source_target_pairs={{0,28},{4,24},{8,20},{12,16},{16,12},{20,8},{24,4},{28,0},{1,29},{... | collective-permute-start | bytes 786440 | tf_op jit(solution)/shard_map/ppermute | solution.py:279
  306.2 35.8 %collective-permute-start.42 = (bf16[8,16384]{1,0:T(8,128)(2,1)}, bf16[8,16384]{1,0:T(8,128)(2,1)S(1)}, u32[]{:S(2)}, u32[]{:S(2)}) collective-permute-start(bf16[8,16384]{1,0:T(8,128)(2,1)} %get-tuple-element.121), channel_id=1, source_target_pairs={{0,24},{4,28},{8,16},{12,20},{16,8},{20,12},{24,0},{28,4},{1,25},{... | collective-permute-start | bytes 786440 | tf_op jit(solution)/shard_map/ppermute | solution.py:279
  306.3 35.8 %collective-permute-start.27 = (bf16[8,16384]{1,0:T(8,128)(2,1)}, bf16[8,16384]{1,0:T(8,128)(2,1)S(1)}, u32[]{:S(2)}, u32[]{:S(2)}) collective-permute-start(bf16[8,16384]{1,0:T(8,128)(2,1)} %get-tuple-element.107), channel_id=1, source_target_pairs={{0,4},{4,0},{8,12},{12,8},{16,20},{20,16},{24,28},{28,24},{1,5},{5... | collective-permute-start | bytes 786440 | tf_op jit(solution)/shard_map/ppermute | solution.py:279
  308.8 39.1 %collective-permute-start.28 = (bf16[8,16384]{1,0:T(8,128)(2,1)}, bf16[8,16384]{1,0:T(8,128)(2,1)S(1)}, u32[]{:S(2)}, u32[]{:S(2)}) collective-permute-start(bf16[8,16384]{1,0:T(8,128)(2,1)} %get-tuple-element.108), channel_id=1, source_target_pairs={{0,8},{4,12},{8,0},{12,4},{16,24},{20,28},{24,16},{28,20},{1,9},{5... | collective-permute-start | bytes 786440 | tf_op jit(solution)/shard_map/ppermute | solution.py:279
  317.3 30.7 %collective-permute-start.29 = (bf16[8,16384]{1,0:T(8,128)(2,1)}, bf16[8,16384]{1,0:T(8,128)(2,1)S(1)}, u32[]{:S(2)}, u32[]{:S(2)}) collective-permute-start(bf16[8,16384]{1,0:T(8,128)(2,1)} %get-tuple-element.109), channel_id=1, source_target_pairs={{0,12},{4,8},{8,4},{12,0},{16,28},{20,24},{24,20},{28,16},{1,13},{... | collective-permute-start | bytes 786440 | tf_op jit(solution)/shard_map/ppermute | solution.py:279
  334.7 27.6 %collective-permute-start.30 = (bf16[8,16384]{1,0:T(8,128)(2,1)}, bf16[8,16384]{1,0:T(8,128)(2,1)}, u32[]{:S(2)}, u32[]{:S(2)}) collective-permute-start(bf16[8,16384]{1,0:T(8,128)(2,1)} %get-tuple-element.110), channel_id=1, source_target_pairs={{0,16},{4,20},{8,24},{12,28},{16,0},{20,4},{24,8},{28,12},{1,17},{... | collective-permute-start | bytes 786440 | tf_op jit(solution)/shard_map/ppermute | solution.py:279
  342.0 25.9 %collective-permute-start.31 = (bf16[8,16384]{1,0:T(8,128)(2,1)}, bf16[8,16384]{1,0:T(8,128)(2,1)}, u32[]{:S(2)}, u32[]{:S(2)}) collective-permute-start(bf16[8,16384]{1,0:T(8,128)(2,1)} %get-tuple-element.111), channel_id=1, source_target_pairs={{0,20},{4,16},{8,28},{12,24},{16,4},{20,0},{24,12},{28,8},{1,21},{... | collective-permute-start | bytes 786440 | tf_op jit(solution)/shard_map/ppermute | solution.py:279
  342.1 31.7 %collective-permute-start.32 = (bf16[8,16384]{1,0:T(8,128)(2,1)}, bf16[8,16384]{1,0:T(8,128)(2,1)}, u32[]{:S(2)}, u32[]{:S(2)}) collective-permute-start(bf16[8,16384]{1,0:T(8,128)(2,1)} %get-tuple-element.112), channel_id=1, source_target_pairs={{0,24},{4,28},{8,16},{12,20},{16,8},{20,12},{24,0},{28,4},{1,25},{... | collective-permute-start | bytes 786440 | tf_op jit(solution)/shard_map/ppermute | solution.py:279
  347.9 39.7 %collective-permute-start.33 = (bf16[8,16384]{1,0:T(8,128)(2,1)}, bf16[8,16384]{1,0:T(8,128)(2,1)}, u32[]{:S(2)}, u32[]{:S(2)}) collective-permute-start(bf16[8,16384]{1,0:T(8,128)(2,1)} %get-tuple-element.113), channel_id=1, source_target_pairs={{0,28},{4,24},{8,20},{12,16},{16,12},{20,8},{24,4},{28,0},{1,29},{... | collective-permute-start | bytes 786440 | tf_op jit(solution)/shard_map/ppermute | solution.py:279
  347.9 39.6 %collective-permute-start.19 = (bf16[8,16384]{1,0:T(8,128)(2,1)}, bf16[8,16384]{1,0:T(8,128)(2,1)}, u32[]{:S(2)}, u32[]{:S(2)}) collective-permute-start(bf16[8,16384]{1,0:T(8,128)(2,1)} %get-tuple-element.98), channel_id=1, source_target_pairs={{0,4},{4,0},{8,12},{12,8},{16,20},{20,16},{24,28},{28,24},{1,5},{5... | collective-permute-start | bytes 786440 | tf_op jit(solution)/shard_map/ppermute | solution.py:279
  362.3 28.0 %collective-permute-start.20 = (bf16[8,16384]{1,0:T(8,128)(2,1)}, bf16[8,16384]{1,0:T(8,128)(2,1)}, u32[]{:S(2)}, u32[]{:S(2)}) collective-permute-start(bf16[8,16384]{1,0:T(8,128)(2,1)} %get-tuple-element.100), channel_id=1, source_target_pairs={{0,12},{4,8},{8,4},{12,0},{16,28},{20,24},{24,20},{28,16},{1,13},{... | collective-permute-start | bytes 786440 | tf_op jit(solution)/shard_map/ppermute | solution.py:279
  367.9 25.3 %collective-permute-start.21 = (bf16[8,16384]{1,0:T(8,128)(2,1)}, bf16[8,16384]{1,0:T(8,128)(2,1)}, u32[]{:S(2)}, u32[]{:S(2)}) collective-permute-start(bf16[8,16384]{1,0:T(8,128)(2,1)} %get-tuple-element.101), channel_id=1, source_target_pairs={{0,8},{4,12},{8,0},{12,4},{16,24},{20,28},{24,16},{28,20},{1,9},{5... | collective-permute-start | bytes 786440 | tf_op jit(solution)/shard_map/ppermute | solution.py:279
  373.8 27.7 %collective-permute-start.22 = (bf16[8,16384]{1,0:T(8,128)(2,1)}, bf16[8,16384]{1,0:T(8,128)(2,1)}, u32[]{:S(2)}, u32[]{:S(2)}) collective-permute-start(bf16[8,16384]{1,0:T(8,128)(2,1)} %get-tuple-element.102), channel_id=1, source_target_pairs={{0,20},{4,16},{8,28},{12,24},{16,4},{20,0},{24,12},{28,8},{1,21},{... | collective-permute-start | bytes 786440 | tf_op jit(solution)/shard_map/ppermute | solution.py:279
  387.5 26.0 %collective-permute-start.24 = (bf16[8,16384]{1,0:T(8,128)(2,1)}, bf16[8,16384]{1,0:T(8,128)(2,1)}, u32[]{:S(2)}, u32[]{:S(2)}) collective-permute-start(bf16[8,16384]{1,0:T(8,128)(2,1)} %get-tuple-element.104), channel_id=1, source_target_pairs={{0,28},{4,24},{8,20},{12,16},{16,12},{20,8},{24,4},{28,0},{1,29},{... | collective-permute-start | bytes 786440 | tf_op jit(solution)/shard_map/ppermute | solution.py:279
  390.2 26.7 %collective-permute-start.25 = (bf16[8,16384]{1,0:T(8,128)(2,1)}, bf16[8,16384]{1,0:T(8,128)(2,1)}, u32[]{:S(2)}, u32[]{:S(2)}) collective-permute-start(bf16[8,16384]{1,0:T(8,128)(2,1)} %get-tuple-element.105), channel_id=1, source_target_pairs={{0,24},{4,28},{8,16},{12,20},{16,8},{20,12},{24,0},{28,4},{1,25},{... | collective-permute-start | bytes 786440 | tf_op jit(solution)/shard_map/ppermute | solution.py:279
  393.2 59.1 %collective-permute-start.4 = (bf16[8,4096]{1,0:T(8,128)(2,1)}, bf16[8,4096]{1,0:T(8,128)(2,1)S(1)}, u32[]{:S(2)}, u32[]{:S(2)}) collective-permute-start(bf16[8,4096]{1,0:T(8,128)(2,1)} %get-tuple-element.85), channel_id=1, source_target_pairs={{0,8},{4,12},{8,0},{12,4},{16,24},{20,28},{24,16},{28,20},{1,9},{5... | collective-permute-start | bytes 196616 | tf_op jit(solution)/shard_map/ppermute | solution.py:279
  401.5 50.9 %collective-permute-start.5 = (bf16[8,4096]{1,0:T(8,128)(2,1)}, bf16[8,4096]{1,0:T(8,128)(2,1)S(1)}, u32[]{:S(2)}, u32[]{:S(2)}) collective-permute-start(bf16[8,4096]{1,0:T(8,128)(2,1)} %get-tuple-element.86), channel_id=1, source_target_pairs={{0,20},{4,16},{8,28},{12,24},{16,4},{20,0},{24,12},{28,8},{1,21},{... | collective-permute-start | bytes 196616 | tf_op jit(solution)/shard_map/ppermute | solution.py:279
  408.0 44.4 %collective-permute-start.6 = (bf16[8,4096]{1,0:T(8,128)(2,1)}, bf16[8,4096]{1,0:T(8,128)(2,1)S(1)}, u32[]{:S(2)}, u32[]{:S(2)}) collective-permute-start(bf16[8,4096]{1,0:T(8,128)(2,1)} %get-tuple-element.87), channel_id=1, source_target_pairs={{0,16},{4,20},{8,24},{12,28},{16,0},{20,4},{24,8},{28,12},{1,17},{... | collective-permute-start | bytes 196616 | tf_op jit(solution)/shard_map/ppermute | solution.py:279
  413.5 38.9 %collective-permute-start.7 = (bf16[8,4096]{1,0:T(8,128)(2,1)}, bf16[8,4096]{1,0:T(8,128)(2,1)S(1)}, u32[]{:S(2)}, u32[]{:S(2)}) collective-permute-start(bf16[8,4096]{1,0:T(8,128)(2,1)} %get-tuple-element.88), channel_id=1, source_target_pairs={{0,28},{4,24},{8,20},{12,16},{16,12},{20,8},{24,4},{28,0},{1,29},{... | collective-permute-start | bytes 196616 | tf_op jit(solution)/shard_map/ppermute | solution.py:279
  417.0 35.4 %collective-permute-start.8 = (bf16[8,4096]{1,0:T(8,128)(2,1)}, bf16[8,4096]{1,0:T(8,128)(2,1)S(1)}, u32[]{:S(2)}, u32[]{:S(2)}) collective-permute-start(bf16[8,4096]{1,0:T(8,128)(2,1)} %get-tuple-element.89), channel_id=1, source_target_pairs={{0,24},{4,28},{8,16},{12,20},{16,8},{20,12},{24,0},{28,4},{1,25},{... | collective-permute-start | bytes 196616 | tf_op jit(solution)/shard_map/ppermute | solution.py:279
  (63 other events, 2386.3 us)

commit v2 on v0

v2 whole, which is shorter than its diff:
```python
import functools
import math

import jax
import jax.numpy as jnp
from jax import lax
from jax.experimental import pallas as pl
from jax.experimental.pallas import tpu as pltpu
from jax.sharding import PartitionSpec as P

NFFT = 64
HALF = NFFT // 2
MODES = 4
SWEEPS = 3
NF = 32
GROUPS = 2
PER_GROUP = NF // GROUPS

CHUNKS_IN = ((0, 0, 4), (1, 0, 4), (2, 0, 2), (2, 2, 2))
CHUNKS_OUT = (2, 0, 1, 3)
QUARTERS = 4

shift_rate = 0.61
BIG = 48 * 1024 * 1024


def hann_window():
    sample = jnp.arange(NFFT, dtype=jnp.int32)
    return 0.5 - 0.5 * jnp.cos(2.0 * math.pi * sample.astype(jnp.float32) / NFFT)


def window_basis(freqs):
    sample = jnp.arange(NFFT, dtype=jnp.int32)
    turn_index = (freqs[:, None] * sample[None, :] % NFFT).astype(jnp.float32)
    angle_grid = 2.0 * math.pi * turn_index / NFFT
    window = hann_window()
    return jnp.stack([window * jnp.cos(angle_grid), -window * jnp.sin(angle_grid)], 0).astype(jnp.bfloat16)


def band_table(freq_order, me, devices):
    basis = window_basis(freq_order).reshape(2, GROUPS, PER_GROUP, NFFT)
    basis = jnp.transpose(basis, (1, 0, 2, 3))
    half_of = jnp.bitwise_xor(me, jnp.arange(devices, dtype=jnp.int32))
    block = jnp.arange(devices - 1, dtype=jnp.int32)
    first = (half_of[None, :] == block[:, None])[None, :, None, None, :, None]
    second = (half_of[None, :] == block[:, None] + 1)[None, :, None, None, :, None]
    low = basis[:, None, :, :, None, :HALF]
    high = basis[:, None, :, :, None, HALF:]
    nothing = jnp.zeros((), jnp.bfloat16)
    band = jnp.where(first, low, jnp.where(second, high, nothing))
    return band.reshape(GROUPS, (devices - 1) * 2 * PER_GROUP, devices * HALF)


def pick_kernel(count, comp, start, size, sub, me_ref, own_ref, *refs):
    outs, sems = refs[-count - 1 : -1], refs[-1]
    me = me_ref[0]
    copies = []
    for place in range(count):
        there = pl.multiple_of(jnp.bitwise_xor(me, place + 1) * sub + start, 128)
        copies.append(
            pltpu.make_async_copy(own_ref.at[comp, :, pl.ds(there, size)], outs[place], sems.at[place])
        )
    for copy in copies:
        copy.start()
    for copy in copies:
        copy.wait()


def pick(me, own, after, devices, comp, start, size, sub):
    count = devices - 1
    return pl.pallas_call(
        functools.partial(pick_kernel, count, comp, start, size, sub),
        in_specs=[pl.BlockSpec(memory_space=pltpu.SMEM)] + [pl.BlockSpec(memory_space=pl.ANY)] * (1 + len(after)),
        out_specs=[pl.BlockSpec(memory_space=pl.ANY)] * count,
        out_shape=[jax.ShapeDtypeStruct((own.shape[1], size), own.dtype)] * count,
        scratch_shapes=[pltpu.SemaphoreType.DMA((count,))],
        name="pick",
    )(me, own, *after)


def gather_kernel(count, me_ref, band_ref, fold_ref, weight_ref, own_ref, *refs):
    landed = refs[:count]
    before_ref, spectra_ref, total_ref, sums = refs[count:]
    step = pl.program_id(0)

    @pl.when(step == 0)
    def _():
        sums[...] = jnp.zeros_like(sums)

    data = jnp.concatenate([own_ref[0]] + [ref[...] for ref in landed], 0)
    weight = weight_ref[...]
    for group in range(GROUPS):
        wide = jnp.dot(band_ref[group], data, preferred_element_type=jnp.float32)
        spectra = wide.astype(jnp.bfloat16)
        spectra_ref[group] = spectra
        weighted = (spectra.astype(jnp.float32) * weight).astype(jnp.bfloat16)
        sums[group] += lax.dot_general(
            weighted, spectra, (((1,), (1,)), ((), ())), preferred_element_type=jnp.float32
        )

    @pl.when(step == pl.num_programs(0) - 1)
    def _():
        rows = sums.shape[1]
        line = lax.broadcasted_iota(jnp.int32, (rows, rows), 0) % PER_GROUP
        column = lax.broadcasted_iota(jnp.int32, (rows, rows), 1) % PER_GROUP
        for group in range(GROUPS):
            kept = jnp.where(line == column, sums[group], 0.0)
            total_ref[group] = before_ref[group] + jnp.dot(
                fold_ref[...], kept, precision=lax.Precision.HIGHEST, preferred_element_type=jnp.float32
            )


def gather(me, band, fold, weights, own, landed, before, comp, start, size, sub, tile):
    count = len(landed)
    half = own.shape[1]
    rows = band.shape[1]
    whole = lambda shape: pl.BlockSpec(shape, lambda g, m: (0,) * len(shape))
    spot = lambda g, m: m[0] * (sub // tile) + start // tile + g
    return pl.pallas_call(
        functools.partial(gather_kernel, count),
        grid_spec=pltpu.PrefetchScalarGridSpec(
            num_scalar_prefetch=1,
            grid=(size // tile,),
            in_specs=[
                whole(band.shape),
                whole(fold.shape),
                pl.BlockSpec((1, tile), lambda g, m: (0, spot(g, m))),
                pl.BlockSpec((1, half, tile), lambda g, m: (comp, 0, spot(g, m))),
            ]
            + [pl.BlockSpec((half, tile), lambda g, m: (0, g))] * count
            + [whole(before.shape)],
            out_specs=[pl.BlockSpec((GROUPS, rows, tile), lambda g, m: (0, 0, g)), whole(before.shape)],
            scratch_shapes=[pltpu.VMEM((GROUPS, rows, rows), jnp.float32)],
        ),
        out_shape=[
            jax.ShapeDtypeStruct((GROUPS, rows, size), jnp.bfloat16),
            jax.ShapeDtypeStruct(before.shape, jnp.float32),
        ],
        compiler_params=pltpu.CompilerParams(vmem_limit_bytes=BIG),
        cost_estimate=pl.CostEstimate(
            flops=2 * GROUPS * size * rows * (band.shape[2] + rows), bytes_accessed=2 * size * (2 * rows + 256), transcendentals=0
        ),
        name="gather",
    )(me, band, fold, weights, own, *landed, before)


def solve_kernel(blocks, me_ref, scale_ref, sums_ref, start_ref, tile_ref, mix_ref, energy_ref):
    devices = mix_ref.shape[0]
    freqs = mix_ref.shape[1] // (2 * MODES)
    padded = sums_ref.shape[1] // 2
    gram_scale = scale_ref[0]
    factor = scale_ref[1]

    def lanes(block, part):
        place = (2 * block + part) * PER_GROUP
        return jnp.concatenate([sums_ref[g, :, place : place + PER_GROUP] for g in range(GROUPS)], 1)

    real, imag = [], []
    for block in range(blocks):
        cosine, sine = lanes(block, 0), lanes(block, 1)
        real.append((cosine[:padded] + sine[padded:]) * gram_scale)
        imag.append((sine[:padded] - cosine[padded:]) * gram_scale)

    def apply(vec_re, vec_im):
        out_re = jnp.zeros((padded, NF), jnp.float32)
        out_im = out_re
        for block in range(blocks):
            at_re = vec_re[block : block + 1]
            at_im = vec_im[block : block + 1]
            out_re = out_re + (real[block] * at_re - imag[block] * at_im)
            out_im = out_im + (real[block] * at_im + imag[block] * at_re)
        return out_re, out_im

    def inner(value):
        return jnp.sum(value, axis=0, keepdims=True)

    vectors = [(start_ref[k], jnp.zeros((padded, NF), jnp.float32)) for k in range(MODES)]
    for sweep in range(SWEEPS):
        images = [apply(*vector) for vector in vectors]
        vectors = []
        for col_re, col_im in images:
            for prev_re, prev_im in vectors:
                inner_re = inner(prev_re * col_re + prev_im * col_im)
                inner_im = inner(prev_re * col_im - prev_im * col_re)
                col_re, col_im = (
                    col_re - (inner_re * prev_re - inner_im * prev_im),
                    col_im - (inner_re * prev_im + inner_im * prev_re),
                )
            length = jnp.sqrt(inner(col_re * col_re + col_im * col_im))
            vectors.append((col_re / length, col_im / length))
    for k, (vec_re, vec_im) in enumerate(vectors):
        applied_re, applied_im = apply(vec_re, vec_im)
        energy_ref[k : k + 1] = inner(vec_re * applied_re + vec_im * applied_im)

    straight, turned = [], []
    for vec_re, vec_im in vectors:
        straight += [vec_re * factor, vec_im * factor]
        turned += [-vec_im * factor, vec_re * factor]
    straight = jnp.concatenate(straight, 0).astype(jnp.bfloat16)
    turned = jnp.concatenate(turned, 0).astype(jnp.bfloat16)
    rows = tile_ref.shape[2]
    place = lax.broadcasted_iota(jnp.int32, (2 * MODES, padded, rows), 2)
    mine = place // (2 * PER_GROUP) == lax.broadcasted_iota(jnp.int32, (2 * MODES, padded, rows), 1)
    lane = lax.broadcasted_iota(jnp.int32, (2 * MODES, rows), 1)
    cosine = lane // PER_GROUP % 2 == 0
    me = me_ref[0]

    def spread(value, group):
        wide = jnp.dot(value, tile_ref[group], preferred_element_type=jnp.float32)
        wide = wide.reshape(2 * MODES, padded, rows)
        return jnp.sum(jnp.where(mine, wide, 0.0), axis=1)

    for group in range(GROUPS):
        both = jnp.where(cosine, spread(straight, group), spread(turned, group))
        for near in range(devices // GROUPS):
            device = group * (devices // GROUPS) + near
            pieces = [
                jnp.where(lane % PER_GROUP == near * freqs + f, both, 0.0) for f in range(freqs)
            ]
            mix_ref[jnp.bitwise_xor(me, device)] = jnp.concatenate(pieces, 0).astype(jnp.bfloat16)


def solve(me, scales, sums, start, tiles, devices):
    freqs = NF // devices
    rows = sums.shape[2]
    return pl.pallas_call(
        functools.partial(solve_kernel, devices - 1),
        in_specs=[pl.BlockSpec(memory_space=pltpu.SMEM)] * 2 + [pl.BlockSpec(memory_space=pltpu.VMEM)] * 3,
        out_specs=[pl.BlockSpec(memory_space=pltpu.VMEM)] * 2,
        out_shape=[
            jax.ShapeDtypeStruct((devices, freqs * MODES * 2, rows), jnp.bfloat16),
            jax.ShapeDtypeStruct((MODES, NF), jnp.float32),
        ],
        compiler_params=pltpu.CompilerParams(vmem_limit_bytes=BIG),
        name="solve",
    )(me, scales, sums, start, tiles)


def modes_kernel(me_ref, mix_ref, spectra_ref, *outs):
    devices = mix_ref.shape[0]
    part = devices // GROUPS
    freqs = outs[0].shape[0]
    per = freqs * MODES * 2
    side = me_ref[0] // part
    for h in range(GROUPS):
        mix = mix_ref[h * part : (h + 1) * part].reshape(part * per, mix_ref.shape[2])
        wide = jnp.dot(mix, spectra_ref[jnp.bitwise_xor(side, h)], preferred_element_type=jnp.float32)
        for near in range(part):
            out = outs[h * part + near]
            for f in range(freqs):
                for k in range(MODES):
                    place = near * per + 2 * (f * MODES + k)
                    out[f, k] = wide[place : place + 2].astype(out.dtype)


def modes_of(me, mix, spectra, devices, tile):
    freqs = NF // devices
    groups, rows, size = spectra.shape
    return pl.pallas_call(
        modes_kernel,
        grid_spec=pltpu.PrefetchScalarGridSpec(
            num_scalar_prefetch=1,
            grid=(size // tile,),
            in_specs=[
                pl.BlockSpec(mix.shape, lambda g, m: (0, 0, 0)),
                pl.BlockSpec((groups, rows, tile), lambda g, m: (0, 0, g)),
            ],
            out_specs=[pl.BlockSpec((freqs, MODES, 2, tile), lambda g, m: (0, 0, 0, g))] * devices,
        ),
        out_shape=[jax.ShapeDtypeStruct((freqs, MODES, 2, size), jnp.bfloat16)] * devices,
        compiler_params=pltpu.CompilerParams(vmem_limit_bytes=BIG),
        name="modes",
    )(me, mix, spectra)


def place_kernel(count, comp, start, size, sub, me_ref, *refs):
    pieces, out_ref, sems = refs[:count], refs[-2], refs[-1]
    me = me_ref[0]
    copies = []
    for place in range(count):
        there = pl.multiple_of(jnp.bitwise_xor(me, place) * sub + start, 128)
        copies.append(
            pltpu.make_async_copy(pieces[place], out_ref.at[:, :, comp, :, pl.ds(there, size)], sems.at[place])
        )
    for copy in copies:
        copy.start()
    for copy in copies:
        copy.wait()


def place(me, pieces, out, comp, start, size, sub, shape):
    count = len(pieces)
    more = [] if out is None else [out]
    return pl.pallas_call(
        functools.partial(place_kernel, count, comp, start, size, sub),
        in_specs=[pl.BlockSpec(memory_space=pltpu.SMEM)]
        + [pl.BlockSpec(memory_space=pl.ANY)] * (count + len(more)),
        out_specs=pl.BlockSpec(memory_space=pl.ANY),
        out_shape=jax.ShapeDtypeStruct(shape, jnp.bfloat16),
        input_output_aliases={count + 1: 0} if more else {},
        scratch_shapes=[pltpu.SemaphoreType.DMA((count,))],
        name="place",
    )(me, *pieces, *more)


def exchange(pieces, devices):
    landed = [None] * (devices - 1)
    across = list(range(devices // 2, devices))
    inside = list(range(1, devices // 2)) + [0]
    for step in [s for pair in zip(across, inside) for s in pair]:
        if step:
            landed[step - 1] = lax.ppermute(pieces[step - 1], "tm", [(d, d ^ step) for d in range(devices)])
    return landed


def sum_over(value, axis):
    count = lax.axis_size(axis)
    step = 1
    while step < count:
        value = value + lax.ppermute(value, axis, [(d, d ^ step) for d in range(count)])
        step *= 2
    return value


def per_device(snapshots, cell_weights, freq_order):
    devices = lax.axis_size("tm")
    spaces = lax.axis_size("space")
    index = lax.axis_index("tm")
    me = index.astype(jnp.int32).reshape(1)
    half, comps, cells = snapshots.shape
    freqs = NF // devices
    blocks = devices - 1
    padded = -(-blocks // 8) * 8
    rows = blocks * 2 * PER_GROUP
    sub = cells // devices
    unit = sub // QUARTERS
    window = hann_window()
    energy_sum = jnp.sum(window * window)
    scales = jnp.stack([1.0 / (energy_sum * (comps * cells * spaces)), 1.0 / jnp.sqrt(energy_sum)])

    own = jnp.transpose(snapshots, (1, 0, 2))
    weights = cell_weights.reshape(1, cells)
    band = band_table(freq_order, index.astype(jnp.int32), devices)
    line = jnp.arange(rows, dtype=jnp.int32)
    target = line // PER_GROUP % 2 * padded + line // (2 * PER_GROUP)
    fold = (target[None, :] == jnp.arange(2 * padded, dtype=jnp.int32)[:, None]).astype(jnp.float32)
    freq_line = jnp.arange(NF, dtype=jnp.int32)
    tiles = jnp.stack(
        [freq_line[:, None] == g * PER_GROUP + line[None, :] % PER_GROUP for g in range(GROUPS)]
    ).astype(jnp.bfloat16)
    count_a = jnp.arange(padded, dtype=jnp.float32) + 1.0
    count_k = jnp.arange(MODES, dtype=jnp.float32) + 1.0
    start_table = jnp.cos(shift_rate * count_a[None, :] * count_k[:, None])
    start_table = jnp.where(jnp.arange(padded)[None, :] < blocks, start_table, 0.0)
    start_table = jnp.broadcast_to(start_table[:, :, None], (MODES, padded, NF))

    sums = jnp.zeros((GROUPS, 2 * padded, rows), jnp.float32)
    spectra = []
    history = []
    for comp, first, length in CHUNKS_IN:
        start, size = first * unit, length * unit
        pieces = pick(me, own, history[-2:-1], devices, comp, start, size, sub)
        landed = exchange(pieces, devices)
        made, sums = gather(me, band, fold, weights, own, landed, sums, comp, start, size, sub, unit)
        spectra.append(made)
        history.append(sums)
    sums = sum_over(sum_over(sums, "space"), "tm")
    mix, energies = solve(me, scales, sums, start_table, tiles, devices)
    out = None
    shape = (freqs, MODES, comps, 2, cells)
    for chunk in CHUNKS_OUT:
        comp, first, length = CHUNKS_IN[chunk]
        made = modes_of(me, mix, spectra[chunk], devices, unit)
        landed = [made[0]] + exchange(made[1:], devices)
        out = place(me, landed, out, comp, first * unit, length * unit, sub, shape)
    mine = lax.dynamic_slice_in_dim(energies, index * freqs, freqs, 1)
    return (jnp.transpose(mine), jnp.transpose(out, (0, 1, 3, 2, 4)))


def solution(mesh):
    return jax.shard_map(
        per_device,
        mesh=mesh,
        in_specs=(P("tm", None, "space"), P("space"), P()),
        out_specs=(P("tm", None), P("tm", None, None, None, "space")),
        check_vma=False,
    )
```

time: 611 us -> 628 us (1.028)
  Pallas kernels: 0 us -> 389 us
  waiting for transfers between devices: 403 us -> 125 us
  starting transfers between devices: 9.56 us -> 92.7 us
  local copies, waits for them, and re-layouts: 99.4 us -> 16.6 us
  matrix products: 60.7 us -> 0 us
  other arithmetic: 21.1 us -> 1.27 us
  blocking collectives: 11.4 us -> 0 us
    pallas_call x0 -> x17, Pallas kernels: none -> 389 us  [the longest x4 195 us: place(): pl.pallas_call(functools.partial(place_kernel, count, comp, start, size,...]
    all_to_all x1 -> x0, waiting for transfers between devices: 267 us -> none  [per_device(): lax.all_to_all(ordered[None], 'tm', split_axis=2, concat_axis=0, tiled=True)]
    ppermute x1 -> x61, starting transfers between devices: 3.29 us -> 92.7 us  [the longest x56 89.2 us: exchange(): lax.ppermute(pieces[step - 1], 'tm', [(d, d ^ step) for d in range(device...]
    dot_general x19 -> x0, matrix products: 60.7 us -> none  [the longest x1 38.4 us: gram_parts(): jnp.einsum('arfp,bsfp->frasb', weighted, spectra, preferred_element_type=...]
    reshape x3 -> x0, local copies, waits for them, and re-layouts: 36.7 us -> none  [the longest x1 23.6 us: per_device(): ordered = jnp.take(spectra.reshape(2, NF, -1), freq_order, axis=1)]
    gather x1 -> x0, local copies, waits for them, and re-layouts: 31.3 us -> none  [per_device(): ordered = jnp.take(spectra.reshape(2, NF, -1), freq_order, axis=1)]
    select_n x2 -> x3, other arithmetic: 15.1 us -> 0.16 us  [the longest x1 0.11 us: per_device(): jnp.where(jnp.arange(padded)[None, :] < blocks, start_table, 0.0)]
    all_to_all x1 -> x0, local copies, waits for them, and re-layouts: 14.5 us -> none  [per_device(): lax.all_to_all(ordered[None], 'tm', split_axis=2, concat_axis=0, tiled=True)]
  transfers between devices with their start and end apart: 2 -> 61, of which waited for: 2 -> 22; matrix products, arithmetic and copies ran while one was open for 0% -> 1% of each run, Pallas kernels for 0% -> 47%
where the time goes in v2:
time: 628 us; the launch traced here: 627 us
  Pallas kernels  389 us (62%)
  waiting for transfers between devices  125 us (20%)
  starting transfers between devices  92.7 us (15%)
  local copies, waits for them, and re-layouts  16.6 us (3%)
    pallas_call x4, Pallas kernels, place(): pl.pallas_call(functools.partial(place_kernel, count, comp, start, size,...  195 us
    pallas_call x4, Pallas kernels, pick(): pl.pallas_call(functools.partial(pick_kernel, count, comp, start, size, s...  171 us
    ppermute x56, waiting for transfers between devices, exchange(): lax.ppermute(pieces[step - 1], 'tm', [(d, d ^ step) for d in range(device...  113 us
    ppermute x56, starting transfers between devices, exchange(): lax.ppermute(pieces[step - 1], 'tm', [(d, d ^ step) for d in range(device...  89.2 us
    pallas_call x4, Pallas kernels, gather(): pl.pallas_call(functools.partial(gather_kernel, count), grid_spec=pltpu.P...  16.1 us
  transfers between devices with their start and end apart: 61, of which 22 were waited for; matrix products, arithmetic and copies ran while one was open for 1% of the time, Pallas kernels for 47%

profile of v2, /device:TPU:8, one launch (start us, length us, event | category | flops | bytes accessed | tf_op | source)
XLA Modules:
  0.0 627.5 jit_solution(11126233593600417155)
XLA Ops:
  0.6 56.8 %pick.5 = (bf16[32,4096]{1,0:T(8,128)(2,1)}, bf16[32,4096]{1,0:T(8,128)(2,1)}, bf16[32,4096]{1,0:T(8,128)(2,1)}, bf16[32,4096]{1,0:T(8,128)(2,1)}, bf16[32,4096]...) custom-call(s32[1]{0:T(128)} %bitcast.me_ref, bf16[3,32,32768]{2,1,0:T(8,128)(2,1)} %bitcast.22), custom_call_target="tpu_custom_call" | custom-call | tf_op jit(solution)/shard_map/pick/pallas_call | solution.py:71
  61.0 2.6 collective-permute-start.10
  65.2 56.8 %pick.4 = (bf16[32,4096]{1,0:T(8,128)(2,1)}, bf16[32,4096]{1,0:T(8,128)(2,1)}, bf16[32,4096]{1,0:T(8,128)(2,1)}, bf16[32,4096]{1,0:T(8,128)(2,1)}, bf16[32,4096]...) custom-call(s32[1]{0:T(128)} %bitcast.me_ref, bf16[3,32,32768]{2,1,0:T(8,128)(2,1)} %bitcast.23), custom_call_target="tpu_custom_call" | custom-call | tf_op jit(solution)/shard_map/pick/pallas_call | solution.py:71
  125.6 2.2 collective-permute-start.1
  129.9 1.9 broadcast_in_dim.99
  133.0 1.9 broadcast_in_dim.94
  135.0 6.4 %collective-permute-done.12.refs_5_ = bf16[32,4096]{1,0:T(8,128)(2,1)S(1)} collective-permute-done((bf16[32,4096]{1,0:T(8,128)(2,1)}, bf16[32,4096]{1,0:T(8,128)(2,1)S(1)}, u32[]{:S(2)}, u32[]{:S(2)}) %collective-permute-start.12) | collective-permute-done | bytes 262176 | tf_op jit(solution)/shard_map/ppermute | solution.py:312
  141.5 21.1 %collective-permute-done.13.refs_6_ = bf16[32,4096]{1,0:T(8,128)(2,1)S(1)} collective-permute-done((bf16[32,4096]{1,0:T(8,128)(2,1)}, bf16[32,4096]{1,0:T(8,128)(2,1)S(1)}, u32[]{:S(2)}, u32[]{:S(2)}) %collective-permute-start.13) | collective-permute-done | bytes 262176 | tf_op jit(solution)/shard_map/ppermute | solution.py:312
  164.5 5.0 gather.4
  169.5 1.8 copy-done
  172.0 29.0 %pick.7 = (bf16[32,2048]{1,0:T(8,128)(2,1)}, bf16[32,2048]{1,0:T(8,128)(2,1)}, bf16[32,2048]{1,0:T(8,128)(2,1)}, bf16[32,2048]{1,0:T(8,128)(2,1)}, bf16[32,2048]...) custom-call(s32[1]{0:T(128)} %bitcast.me_ref, bf16[3,32,32768]{2,1,0:T(8,128)(2,1)} %bitcast.25, ...), custom_call_target="tpu_custom_call" | custom-call | tf_op jit(solution)/shard_map/pick/pallas_call | solution.py:71
  202.6 4.5 collective-permute-start.22
  211.5 5.0 gather.5
  218.9 29.0 %pick.6 = (bf16[32,2048]{1,0:T(8,128)(2,1)}, bf16[32,2048]{1,0:T(8,128)(2,1)}, bf16[32,2048]{1,0:T(8,128)(2,1)}, bf16[32,2048]{1,0:T(8,128)(2,1)}, bf16[32,2048]...) custom-call(s32[1]{0:T(128)} %bitcast.me_ref, bf16[3,32,32768]{2,1,0:T(8,128)(2,1)} %bitcast.27, ...), custom_call_target="tpu_custom_call" | custom-call | tf_op jit(solution)/shard_map/pick/pallas_call | solution.py:71
  248.6 2.3 collective-permute-start.27
  251.5 3.3 collective-permute-start.15
  258.1 2.9 collective-permute-start.18
  262.7 3.1 gather.6
  266.5 4.5 collective-permute-done.19.refs_5_
  272.2 3.0 gather.7
  278.1 2.4 collective-permute-done.29
  282.3 2.2 collective-permute-done.30
  286.5 2.0 collective-permute-done.31
  288.8 4.5 collective-permute-done.32
  300.8 3.7 collective-permute-start.58
  309.3 1.9 modes.6
  312.1 3.4 collective-permute-done.58.refs_5_
  315.5 4.0 collective-permute-start.48
  319.8 3.8 collective-permute-done.60.refs_7_
  328.0 9.4 %collective-permute-done.34.refs_2_ = bf16[4,4,2,2048]{3,2,1,0:T(2,128)(2,1)S(1)} collective-permute-done((bf16[4,4,2,2048]{3,2,1,0:T(2,128)(2,1)S(1)}, bf16[4,4,2,2048]{3,2,1,0:T(2,128)(2,1)S(1)}, u32[]{:S(2)}, u32[]{:S(2)}) %collective-permute-start.34) | collective-permute-done | bytes 131104 | tf_op jit(solution)/shard_map/ppermute | solution.py:312
  338.0 3.2 collective-permute-start.51
  346.3 12.3 %collective-permute-done.51.refs_5_ = bf16[4,4,2,4096]{3,2,1,0:T(2,128)(2,1)S(1)} collective-permute-done((bf16[4,4,2,4096]{3,2,1,0:T(2,128)(2,1)S(1)}, bf16[4,4,2,4096]{3,2,1,0:T(2,128)(2,1)S(1)}, u32[]{:S(2)}, u32[]{:S(2)}) %collective-permute-start.51) | collective-permute-done | bytes 262176 | tf_op jit(solution)/shard_map/ppermute | solution.py:312
  358.6 3.2 collective-permute-start.42
  361.8 3.3 collective-permute-done.52.refs_6_
  365.0 13.0 %collective-permute-done.53.refs_7_ = bf16[4,4,2,4096]{3,2,1,0:T(2,128)(2,1)S(1)} collective-permute-done((bf16[4,4,2,4096]{3,2,1,0:T(2,128)(2,1)S(1)}, bf16[4,4,2,4096]{3,2,1,0:T(2,128)(2,1)S(1)}, u32[]{:S(2)}, u32[]{:S(2)}) %collective-permute-start.53) | collective-permute-done | bytes 262176 | tf_op jit(solution)/shard_map/ppermute | solution.py:312
  380.1 6.0 collective-permute-start.35
  386.1 14.3 %collective-permute-done.43.refs_4_ = bf16[4,4,2,4096]{3,2,1,0:T(2,128)(2,1)S(1)} collective-permute-done((bf16[4,4,2,4096]{3,2,1,0:T(2,128)(2,1)S(1)}, bf16[4,4,2,4096]{3,2,1,0:T(2,128)(2,1)S(1)}, u32[]{:S(2)}, u32[]{:S(2)}) %collective-permute-start.43) | collective-permute-done | bytes 262176 | tf_op jit(solution)/shard_map/ppermute | solution.py:312
  400.5 3.4 collective-permute-start.36
  403.9 3.6 collective-permute-done.44.refs_5_
  407.5 4.3 collective-permute-start.37
  411.8 9.9 %collective-permute-done.45.refs_6_ = bf16[4,4,2,4096]{3,2,1,0:T(2,128)(2,1)S(1)} collective-permute-done((bf16[4,4,2,4096]{3,2,1,0:T(2,128)(2,1)S(1)}, bf16[4,4,2,4096]{3,2,1,0:T(2,128)(2,1)S(1)}, u32[]{:S(2)}, u32[]{:S(2)}) %collective-permute-start.45) | collective-permute-done | bytes 262176 | tf_op jit(solution)/shard_map/ppermute | solution.py:312
  421.7 2.3 collective-permute-start.38
  424.0 4.6 collective-permute-done.46.refs_7_
  429.3 1.9 collective-permute-start.39
  432.0 32.9 %place.4.refs_8_ = bf16[4,4,3,2,32768]{4,3,2,1,0:T(2,128)(2,1)} custom-call(s32[1]{0:T(128)} %bitcast.me_ref, bf16[4,4,2,2048]{3,2,1,0:T(2,128)(2,1)} %copy-done.14, bf16[4,4,2,2048]{3,2,1,0:T(2,128)(2,1)} %copy-done.31, bf16[4,4,2,2048]{3,2,1,0:T(2,128)(2,1)} %copy-done.32, bf16[4,4,2,2048]{3,2,1,0:T(2,128)(2,1)} %copy-done.33, ...), custom_call_target="tpu_custom_call" | custom-call | tf_op jit(solution)/shard_map/place/pallas_call | solution.py:294
  465.0 64.7 %place.5.refs_8_ = bf16[4,4,3,2,32768]{4,3,2,1,0:T(2,128)(2,1)} custom-call(s32[1]{0:T(128)} %bitcast.me_ref, bf16[4,4,2,4096]{3,2,1,0:T(2,128)(2,1)} %copy-done.7, bf16[4,4,2,4096]{3,2,1,0:T(2,128)(2,1)} %copy-done.15, bf16[4,4,2,4096]{3,2,1,0:T(2,128)(2,1)} %copy-done.16, bf16[4,4,2,4096]{3,2,1,0:T(2,128)(2,1)} %copy-done.17, ...), custom_call_target="tpu_custom_call", output_to_operand_aliasing={{}: (9, {})} | custom-call | tf_op jit(solution)/shard_map/place/pallas_call | solution.py:294
  529.8 64.7 %place.6.refs_8_ = bf16[4,4,3,2,32768]{4,3,2,1,0:T(2,128)(2,1)} custom-call(s32[1]{0:T(128)} %bitcast.me_ref, bf16[4,4,2,4096]{3,2,1,0:T(2,128)(2,1)} %copy-done.8, bf16[4,4,2,4096]{3,2,1,0:T(2,128)(2,1)} %copy-done.22, bf16[4,4,2,4096]{3,2,1,0:T(2,128)(2,1)} %copy-done.23, bf16[4,4,2,4096]{3,2,1,0:T(2,128)(2,1)} %copy-done.24, ...), custom_call_target="tpu_custom_call", output_to_operand_aliasing={{}: (9, {})} | custom-call | tf_op jit(solution)/shard_map/place/pallas_call | solution.py:294
  594.5 32.9 %place.7 = bf16[4,4,3,2,32768]{4,3,2,1,0:T(2,128)(2,1)} custom-call(s32[1]{0:T(128)} %bitcast.me_ref, bf16[4,4,2,2048]{3,2,1,0:T(2,128)(2,1)} %copy-done.9, bf16[4,4,2,2048]{3,2,1,0:T(2,128)(2,1)} %copy-done.29, bf16[4,4,2,2048]{3,2,1,0:T(2,128)(2,1)} %copy-done.30, ...), custom_call_target="tpu_custom_call", output_to_operand_aliasing={{}: (9, {})} | custom-call | tf_op jit(solution)/shard_map/place/pallas_call | solution.py:294
  (211 shorter events, 63.7 us)
Async XLA Ops:
  57.4 64.7 %collective-permute-start.7 = (bf16[32,4096]{1,0:T(8,128)(2,1)}, bf16[32,4096]{1,0:T(8,128)(2,1)S(1)}, u32[]{:S(2)}, u32[]{:S(2)}) collective-permute-start(bf16[32,4096]{1,0:T(8,128)(2,1)} %get-tuple-element.79), channel_id=1, source_target_pairs={{0,4},{4,0},{8,12},{12,8},{16,20},{20,16},{24,28},{28,24},{1,5},{5... | collective-permute-start | bytes 786440 | tf_op jit(solution)/shard_map/ppermute | solution.py:312
  59.0 64.7 %collective-permute-start.8 = (bf16[32,4096]{1,0:T(8,128)(2,1)}, bf16[32,4096]{1,0:T(8,128)(2,1)S(1)}, u32[]{:S(2)}, u32[]{:S(2)}) collective-permute-start(bf16[32,4096]{1,0:T(8,128)(2,1)} %get-tuple-element.80), channel_id=1, source_target_pairs={{0,8},{4,12},{8,0},{12,4},{16,24},{20,28},{24,16},{28,20},{1,9},{5... | collective-permute-start | bytes 786440 | tf_op jit(solution)/shard_map/ppermute | solution.py:312
  59.4 64.7 %collective-permute-start.9 = (bf16[32,4096]{1,0:T(8,128)(2,1)}, bf16[32,4096]{1,0:T(8,128)(2,1)S(1)}, u32[]{:S(2)}, u32[]{:S(2)}) collective-permute-start(bf16[32,4096]{1,0:T(8,128)(2,1)} %get-tuple-element.81), channel_id=1, source_target_pairs={{0,12},{4,8},{8,4},{12,0},{16,28},{20,24},{24,20},{28,16},{1,13},{... | collective-permute-start | bytes 786440 | tf_op jit(solution)/shard_map/ppermute | solution.py:312
  61.0 64.6 %collective-permute-start.10 = (bf16[32,4096]{1,0:T(8,128)(2,1)}, bf16[32,4096]{1,0:T(8,128)(2,1)S(1)}, u32[]{:S(2)}, u32[]{:S(2)}) collective-permute-start(bf16[32,4096]{1,0:T(8,128)(2,1)} %get-tuple-element.82), channel_id=1, source_target_pairs={{0,16},{4,20},{8,24},{12,28},{16,0},{20,4},{24,8},{28,12},{1,17},{... | collective-permute-start | bytes 786440 | tf_op jit(solution)/shard_map/ppermute | solution.py:312
  63.6 71.4 %collective-permute-start.11 = (bf16[32,4096]{1,0:T(8,128)(2,1)}, bf16[32,4096]{1,0:T(8,128)(2,1)S(1)}, u32[]{:S(2)}, u32[]{:S(2)}) collective-permute-start(bf16[32,4096]{1,0:T(8,128)(2,1)} %get-tuple-element.83), channel_id=1, source_target_pairs={{0,20},{4,16},{8,28},{12,24},{16,4},{20,0},{24,12},{28,8},{1,21},{... | collective-permute-start | bytes 786440 | tf_op jit(solution)/shard_map/ppermute | solution.py:312
  122.1 19.4 %collective-permute-start.12 = (bf16[32,4096]{1,0:T(8,128)(2,1)}, bf16[32,4096]{1,0:T(8,128)(2,1)S(1)}, u32[]{:S(2)}, u32[]{:S(2)}) collective-permute-start(bf16[32,4096]{1,0:T(8,128)(2,1)} %get-tuple-element.84), channel_id=1, source_target_pairs={{0,24},{4,28},{8,16},{12,20},{16,8},{20,12},{24,0},{28,4},{1,25},{... | collective-permute-start | bytes 786440 | tf_op jit(solution)/shard_map/ppermute | solution.py:312
  123.7 38.9 %collective-permute-start.13 = (bf16[32,4096]{1,0:T(8,128)(2,1)}, bf16[32,4096]{1,0:T(8,128)(2,1)S(1)}, u32[]{:S(2)}, u32[]{:S(2)}) collective-permute-start(bf16[32,4096]{1,0:T(8,128)(2,1)} %get-tuple-element.85), channel_id=1, source_target_pairs={{0,28},{4,24},{8,20},{12,16},{16,12},{20,8},{24,4},{28,0},{1,29},{... | collective-permute-start | bytes 786440 | tf_op jit(solution)/shard_map/ppermute | solution.py:312
  124.1 38.5 %collective-permute-start = (bf16[32,4096]{1,0:T(8,128)(2,1)}, bf16[32,4096]{1,0:T(8,128)(2,1)S(1)}, u32[]{:S(2)}, u32[]{:S(2)}) collective-permute-start(bf16[32,4096]{1,0:T(8,128)(2,1)} %get-tuple-element.72), channel_id=1, source_target_pairs={{0,4},{4,0},{8,12},{12,8},{16,20},{20,16},{24,28},{28,24},{1,5},{5... | collective-permute-start | bytes 786440 | tf_op jit(solution)/shard_map/ppermute | solution.py:312
  125.6 38.7 %collective-permute-start.1 = (bf16[32,4096]{1,0:T(8,128)(2,1)}, bf16[32,4096]{1,0:T(8,128)(2,1)S(1)}, u32[]{:S(2)}, u32[]{:S(2)}) collective-permute-start(bf16[32,4096]{1,0:T(8,128)(2,1)} %get-tuple-element.73), channel_id=1, source_target_pairs={{0,8},{4,12},{8,0},{12,4},{16,24},{20,28},{24,16},{28,20},{1,9},{5... | collective-permute-start | bytes 786440 | tf_op jit(solution)/shard_map/ppermute | solution.py:312
  135.0 66.0 %collective-permute-start.2 = (bf16[32,4096]{1,0:T(8,128)(2,1)}, bf16[32,4096]{1,0:T(8,128)(2,1)S(1)}, u32[]{:S(2)}, u32[]{:S(2)}) collective-permute-start(bf16[32,4096]{1,0:T(8,128)(2,1)} %get-tuple-element.74), channel_id=1, source_target_pairs={{0,12},{4,8},{8,4},{12,0},{16,28},{20,24},{24,20},{28,16},{1,13},{... | collective-permute-start | bytes 786440 | tf_op jit(solution)/shard_map/ppermute | solution.py:312
  141.5 61.1 %collective-permute-start.3 = (bf16[32,4096]{1,0:T(8,128)(2,1)}, bf16[32,4096]{1,0:T(8,128)(2,1)S(1)}, u32[]{:S(2)}, u32[]{:S(2)}) collective-permute-start(bf16[32,4096]{1,0:T(8,128)(2,1)} %get-tuple-element.75), channel_id=1, source_target_pairs={{0,16},{4,20},{8,24},{12,28},{16,0},{20,4},{24,8},{28,12},{1,17},{... | collective-permute-start | bytes 786440 | tf_op jit(solution)/shard_map/ppermute | solution.py:312
  162.6 44.5 %collective-permute-start.4 = (bf16[32,4096]{1,0:T(8,128)(2,1)}, bf16[32,4096]{1,0:T(8,128)(2,1)S(1)}, u32[]{:S(2)}, u32[]{:S(2)}) collective-permute-start(bf16[32,4096]{1,0:T(8,128)(2,1)} %get-tuple-element.76), channel_id=1, source_target_pairs={{0,20},{4,16},{8,28},{12,24},{16,4},{20,0},{24,12},{28,8},{1,21},{... | collective-permute-start | bytes 786440 | tf_op jit(solution)/shard_map/ppermute | solution.py:312
  162.6 45.9 %collective-permute-start.5 = (bf16[32,4096]{1,0:T(8,128)(2,1)}, bf16[32,4096]{1,0:T(8,128)(2,1)}, u32[]{:S(2)}, u32[]{:S(2)}) collective-permute-start(bf16[32,4096]{1,0:T(8,128)(2,1)} %get-tuple-element.77), channel_id=1, source_target_pairs={{0,24},{4,28},{8,16},{12,20},{16,8},{20,12},{24,0},{28,4},{1,25},{... | collective-permute-start | bytes 786440 | tf_op jit(solution)/shard_map/ppermute | solution.py:312
  164.3 45.9 %collective-permute-start.6 = (bf16[32,4096]{1,0:T(8,128)(2,1)}, bf16[32,4096]{1,0:T(8,128)(2,1)}, u32[]{:S(2)}, u32[]{:S(2)}) collective-permute-start(bf16[32,4096]{1,0:T(8,128)(2,1)} %get-tuple-element.78), channel_id=1, source_target_pairs={{0,28},{4,24},{8,20},{12,16},{16,12},{20,8},{24,4},{28,0},{1,29},{... | collective-permute-start | bytes 786440 | tf_op jit(solution)/shard_map/ppermute | solution.py:312
  200.9 47.0 %collective-permute-start.21 = (bf16[32,2048]{1,0:T(8,128)(2,1)}, bf16[32,2048]{1,0:T(8,128)(2,1)S(1)}, u32[]{:S(2)}, u32[]{:S(2)}) collective-permute-start(bf16[32,2048]{1,0:T(8,128)(2,1)} %get-tuple-element.95), channel_id=1, source_target_pairs={{0,4},{4,0},{8,12},{12,8},{16,20},{20,16},{24,28},{28,24},{1,5},{5... | collective-permute-start | bytes 393224 | tf_op jit(solution)/shard_map/ppermute | solution.py:312
  202.6 46.0 %collective-permute-start.22 = (bf16[32,2048]{1,0:T(8,128)(2,1)}, bf16[32,2048]{1,0:T(8,128)(2,1)S(1)}, u32[]{:S(2)}, u32[]{:S(2)}) collective-permute-start(bf16[32,2048]{1,0:T(8,128)(2,1)} %get-tuple-element.96), channel_id=1, source_target_pairs={{0,8},{4,12},{8,0},{12,4},{16,24},{20,28},{24,16},{28,20},{1,9},{5... | collective-permute-start | bytes 393224 | tf_op jit(solution)/shard_map/ppermute | solution.py:312
  207.1 43.9 %collective-permute-start.23 = (bf16[32,2048]{1,0:T(8,128)(2,1)}, bf16[32,2048]{1,0:T(8,128)(2,1)S(1)}, u32[]{:S(2)}, u32[]{:S(2)}) collective-permute-start(bf16[32,2048]{1,0:T(8,128)(2,1)} %get-tuple-element.97), channel_id=1, source_target_pairs={{0,12},{4,8},{8,4},{12,0},{16,28},{20,24},{24,20},{28,16},{1,13},{... | collective-permute-start | bytes 393224 | tf_op jit(solution)/shard_map/ppermute | solution.py:312
  208.5 43.0 %collective-permute-start.24 = (bf16[32,2048]{1,0:T(8,128)(2,1)}, bf16[32,2048]{1,0:T(8,128)(2,1)S(1)}, u32[]{:S(2)}, u32[]{:S(2)}) collective-permute-start(bf16[32,2048]{1,0:T(8,128)(2,1)} %get-tuple-element.98), channel_id=1, source_target_pairs={{0,16},{4,20},{8,24},{12,28},{16,0},{20,4},{24,8},{28,12},{1,17},{... | collective-permute-start | bytes 393224 | tf_op jit(solution)/shard_map/ppermute | solution.py:312
  210.3 44.5 %collective-permute-start.25 = (bf16[32,2048]{1,0:T(8,128)(2,1)}, bf16[32,2048]{1,0:T(8,128)(2,1)S(1)}, u32[]{:S(2)}, u32[]{:S(2)}) collective-permute-start(bf16[32,2048]{1,0:T(8,128)(2,1)} %get-tuple-element.99), channel_id=1, source_target_pairs={{0,20},{4,16},{8,28},{12,24},{16,4},{20,0},{24,12},{28,8},{1,21},{... | collective-permute-start | bytes 393224 | tf_op jit(solution)/shard_map/ppermute | solution.py:312
  250.9 10.1 %collective-permute-start.14 = (bf16[32,2048]{1,0:T(8,128)(2,1)}, bf16[32,2048]{1,0:T(8,128)(2,1)S(1)}, u32[]{:S(2)}, u32[]{:S(2)}) collective-permute-start(bf16[32,2048]{1,0:T(8,128)(2,1)} %get-tuple-element.88), channel_id=1, source_target_pairs={{0,4},{4,0},{8,12},{12,8},{16,20},{20,16},{24,28},{28,24},{1,5},{5... | collective-permute-start | bytes 393224 | tf_op jit(solution)/shard_map/ppermute | solution.py:312
  254.8 10.9 %collective-permute-start.16 = (bf16[32,2048]{1,0:T(8,128)(2,1)}, bf16[32,2048]{1,0:T(8,128)(2,1)S(1)}, u32[]{:S(2)}, u32[]{:S(2)}) collective-permute-start(bf16[32,2048]{1,0:T(8,128)(2,1)} %get-tuple-element.90), channel_id=1, source_target_pairs={{0,12},{4,8},{8,4},{12,0},{16,28},{20,24},{24,20},{28,16},{1,13},{... | collective-permute-start | bytes 393224 | tf_op jit(solution)/shard_map/ppermute | solution.py:312
  261.0 10.0 %collective-permute-start.19 = (bf16[32,2048]{1,0:T(8,128)(2,1)}, bf16[32,2048]{1,0:T(8,128)(2,1)S(1)}, u32[]{:S(2)}, u32[]{:S(2)}) collective-permute-start(bf16[32,2048]{1,0:T(8,128)(2,1)} %get-tuple-element.93), channel_id=1, source_target_pairs={{0,24},{4,28},{8,16},{12,20},{16,8},{20,12},{24,0},{28,4},{1,25},{... | collective-permute-start | bytes 393224 | tf_op jit(solution)/shard_map/ppermute | solution.py:312
  261.3 10.9 %collective-permute-start.20 = (bf16[32,2048]{1,0:T(8,128)(2,1)}, bf16[32,2048]{1,0:T(8,128)(2,1)S(1)}, u32[]{:S(2)}, u32[]{:S(2)}) collective-permute-start(bf16[32,2048]{1,0:T(8,128)(2,1)} %get-tuple-element.94), channel_id=1, source_target_pairs={{0,28},{4,24},{8,20},{12,16},{16,12},{20,8},{24,4},{28,0},{1,29},{... | collective-permute-start | bytes 393224 | tf_op jit(solution)/shard_map/ppermute | solution.py:312
  300.6 10.7 %collective-permute-start.57 = (bf16[4,4,2,2048]{3,2,1,0:T(2,128)(2,1)S(1)}, bf16[4,4,2,2048]{3,2,1,0:T(2,128)(2,1)S(1)}, u32[]{:S(2)}, u32[]{:S(2)}) collective-permute-start(bf16[4,4,2,2048]{3,2,1,0:T(2,128)(2,1)S(1)} %get-tuple-element.138), channel_id=1, source_target_pairs={{0,16},{4,20},{8,24},{12,28},{16,0},{20,4},{24,8},{28,12},{1,17},{... | collective-permute-start | bytes 393224 | tf_op jit(solution)/shard_map/ppermute | solution.py:312
  300.8 14.7 %collective-permute-start.58 = (bf16[4,4,2,2048]{3,2,1,0:T(2,128)(2,1)S(1)}, bf16[4,4,2,2048]{3,2,1,0:T(2,128)(2,1)S(1)}, u32[]{:S(2)}, u32[]{:S(2)}) collective-permute-start(bf16[4,4,2,2048]{3,2,1,0:T(2,128)(2,1)S(1)} %get-tuple-element.139), channel_id=1, source_target_pairs={{0,20},{4,16},{8,28},{12,24},{16,4},{20,0},{24,12},{28,8},{1,21},{... | collective-permute-start | bytes 393224 | tf_op jit(solution)/shard_map/ppermute | solution.py:312
  304.6 15.0 %collective-permute-start.59 = (bf16[4,4,2,2048]{3,2,1,0:T(2,128)(2,1)S(1)}, bf16[4,4,2,2048]{3,2,1,0:T(2,128)(2,1)S(1)}, u32[]{:S(2)}, u32[]{:S(2)}) collective-permute-start(bf16[4,4,2,2048]{3,2,1,0:T(2,128)(2,1)S(1)} %get-tuple-element.140), channel_id=1, source_target_pairs={{0,24},{4,28},{8,16},{12,20},{16,8},{20,12},{24,0},{28,4},{1,25},{... | collective-permute-start | bytes 393224 | tf_op jit(solution)/shard_map/ppermute | solution.py:312
  305.1 18.4 %collective-permute-start.60 = (bf16[4,4,2,2048]{3,2,1,0:T(2,128)(2,1)S(1)}, bf16[4,4,2,2048]{3,2,1,0:T(2,128)(2,1)S(1)}, u32[]{:S(2)}, u32[]{:S(2)}) collective-permute-start(bf16[4,4,2,2048]{3,2,1,0:T(2,128)(2,1)S(1)} %get-tuple-element.141), channel_id=1, source_target_pairs={{0,28},{4,24},{8,20},{12,16},{16,12},{20,8},{24,4},{28,0},{1,29},{... | collective-permute-start | bytes 393224 | tf_op jit(solution)/shard_map/ppermute | solution.py:312
  308.1 15.5 %collective-permute-start.33 = (bf16[4,4,2,2048]{3,2,1,0:T(2,128)(2,1)S(1)}, bf16[4,4,2,2048]{3,2,1,0:T(2,128)(2,1)S(1)}, u32[]{:S(2)}, u32[]{:S(2)}) collective-permute-start(bf16[4,4,2,2048]{3,2,1,0:T(2,128)(2,1)S(1)} %get-tuple-element.108), channel_id=1, source_target_pairs={{0,4},{4,0},{8,12},{12,8},{16,20},{20,16},{24,28},{28,24},{1,5},{5... | collective-permute-start | bytes 393224 | tf_op jit(solution)/shard_map/ppermute | solution.py:312
  311.2 30.0 %collective-permute-start.47 = (bf16[4,4,2,4096]{3,2,1,0:T(2,128)(2,1)S(1)}, bf16[4,4,2,4096]{3,2,1,0:T(2,128)(2,1)S(1)}, u32[]{:S(2)}, u32[]{:S(2)}) collective-permute-start(bf16[4,4,2,4096]{3,2,1,0:T(2,128)(2,1)S(1)} %get-tuple-element.126), channel_id=1, source_target_pairs={{0,4},{4,0},{8,12},{12,8},{16,20},{20,16},{24,28},{28,24},{1,5},{5... | collective-permute-start | bytes 786440 | tf_op jit(solution)/shard_map/ppermute | solution.py:312
  315.5 25.7 %collective-permute-start.48 = (bf16[4,4,2,4096]{3,2,1,0:T(2,128)(2,1)S(1)}, bf16[4,4,2,4096]{3,2,1,0:T(2,128)(2,1)S(1)}, u32[]{:S(2)}, u32[]{:S(2)}) collective-permute-start(bf16[4,4,2,4096]{3,2,1,0:T(2,128)(2,1)S(1)} %get-tuple-element.127), channel_id=1, source_target_pairs={{0,8},{4,12},{8,0},{12,4},{16,24},{20,28},{24,16},{28,20},{1,9},{5... | collective-permute-start | bytes 786440 | tf_op jit(solution)/shard_map/ppermute | solution.py:312
  319.6 23.4 %collective-permute-start.49 = (bf16[4,4,2,4096]{3,2,1,0:T(2,128)(2,1)S(1)}, bf16[4,4,2,4096]{3,2,1,0:T(2,128)(2,1)S(1)}, u32[]{:S(2)}, u32[]{:S(2)}) collective-permute-start(bf16[4,4,2,4096]{3,2,1,0:T(2,128)(2,1)S(1)} %get-tuple-element.128), channel_id=1, source_target_pairs={{0,12},{4,8},{8,4},{12,0},{16,28},{20,24},{24,20},{28,16},{1,13},{... | collective-permute-start | bytes 786440 | tf_op jit(solution)/shard_map/ppermute | solution.py:312
  323.6 21.3 %collective-permute-start.50 = (bf16[4,4,2,4096]{3,2,1,0:T(2,128)(2,1)S(1)}, bf16[4,4,2,4096]{3,2,1,0:T(2,128)(2,1)S(1)}, u32[]{:S(2)}, u32[]{:S(2)}) collective-permute-start(bf16[4,4,2,4096]{3,2,1,0:T(2,128)(2,1)S(1)} %get-tuple-element.129), channel_id=1, source_target_pairs={{0,16},{4,20},{8,24},{12,28},{16,0},{20,4},{24,8},{28,12},{1,17},{... | collective-permute-start | bytes 786440 | tf_op jit(solution)/shard_map/ppermute | solution.py:312
  323.6 13.8 %collective-permute-start.34 = (bf16[4,4,2,2048]{3,2,1,0:T(2,128)(2,1)S(1)}, bf16[4,4,2,2048]{3,2,1,0:T(2,128)(2,1)S(1)}, u32[]{:S(2)}, u32[]{:S(2)}) collective-permute-start(bf16[4,4,2,2048]{3,2,1,0:T(2,128)(2,1)S(1)} %get-tuple-element.109), channel_id=1, source_target_pairs={{0,8},{4,12},{8,0},{12,4},{16,24},{20,28},{24,16},{28,20},{1,9},{5... | collective-permute-start | bytes 393224 | tf_op jit(solution)/shard_map/ppermute | solution.py:312
  338.0 20.5 %collective-permute-start.51 = (bf16[4,4,2,4096]{3,2,1,0:T(2,128)(2,1)S(1)}, bf16[4,4,2,4096]{3,2,1,0:T(2,128)(2,1)S(1)}, u32[]{:S(2)}, u32[]{:S(2)}) collective-permute-start(bf16[4,4,2,4096]{3,2,1,0:T(2,128)(2,1)S(1)} %get-tuple-element.130), channel_id=1, source_target_pairs={{0,20},{4,16},{8,28},{12,24},{16,4},{20,0},{24,12},{28,8},{1,21},{... | collective-permute-start | bytes 786440 | tf_op jit(solution)/shard_map/ppermute | solution.py:312
  341.3 23.8 %collective-permute-start.52 = (bf16[4,4,2,4096]{3,2,1,0:T(2,128)(2,1)S(1)}, bf16[4,4,2,4096]{3,2,1,0:T(2,128)(2,1)S(1)}, u32[]{:S(2)}, u32[]{:S(2)}) collective-permute-start(bf16[4,4,2,4096]{3,2,1,0:T(2,128)(2,1)S(1)} %get-tuple-element.131), channel_id=1, source_target_pairs={{0,24},{4,28},{8,16},{12,20},{16,8},{20,12},{24,0},{28,4},{1,25},{... | collective-permute-start | bytes 786440 | tf_op jit(solution)/shard_map/ppermute | solution.py:312
  341.3 36.7 %collective-permute-start.53 = (bf16[4,4,2,4096]{3,2,1,0:T(2,128)(2,1)S(1)}, bf16[4,4,2,4096]{3,2,1,0:T(2,128)(2,1)S(1)}, u32[]{:S(2)}, u32[]{:S(2)}) collective-permute-start(bf16[4,4,2,4096]{3,2,1,0:T(2,128)(2,1)S(1)} %get-tuple-element.132), channel_id=1, source_target_pairs={{0,28},{4,24},{8,20},{12,16},{16,12},{20,8},{24,4},{28,0},{1,29},{... | collective-permute-start | bytes 786440 | tf_op jit(solution)/shard_map/ppermute | solution.py:312
  343.0 35.0 %collective-permute-start.40 = (bf16[4,4,2,4096]{3,2,1,0:T(2,128)(2,1)S(1)}, bf16[4,4,2,4096]{3,2,1,0:T(2,128)(2,1)S(1)}, u32[]{:S(2)}, u32[]{:S(2)}) collective-permute-start(bf16[4,4,2,4096]{3,2,1,0:T(2,128)(2,1)S(1)} %get-tuple-element.117), channel_id=1, source_target_pairs={{0,4},{4,0},{8,12},{12,8},{16,20},{20,16},{24,28},{28,24},{1,5},{5... | collective-permute-start | bytes 786440 | tf_op jit(solution)/shard_map/ppermute | solution.py:312
  344.9 33.8 %collective-permute-start.41 = (bf16[4,4,2,4096]{3,2,1,0:T(2,128)(2,1)S(1)}, bf16[4,4,2,4096]{3,2,1,0:T(2,128)(2,1)S(1)}, u32[]{:S(2)}, u32[]{:S(2)}) collective-permute-start(bf16[4,4,2,4096]{3,2,1,0:T(2,128)(2,1)S(1)} %get-tuple-element.118), channel_id=1, source_target_pairs={{0,8},{4,12},{8,0},{12,4},{16,24},{20,28},{24,16},{28,20},{1,9},{5... | collective-permute-start | bytes 786440 | tf_op jit(solution)/shard_map/ppermute | solution.py:312
  358.6 21.5 %collective-permute-start.42 = (bf16[4,4,2,4096]{3,2,1,0:T(2,128)(2,1)S(1)}, bf16[4,4,2,4096]{3,2,1,0:T(2,128)(2,1)S(1)}, u32[]{:S(2)}, u32[]{:S(2)}) collective-permute-start(bf16[4,4,2,4096]{3,2,1,0:T(2,128)(2,1)S(1)} %get-tuple-element.119), channel_id=1, source_target_pairs={{0,12},{4,8},{8,4},{12,0},{16,28},{20,24},{24,20},{28,16},{1,13},{... | collective-permute-start | bytes 786440 | tf_op jit(solution)/shard_map/ppermute | solution.py:312
  365.0 35.4 %collective-permute-start.43 = (bf16[4,4,2,4096]{3,2,1,0:T(2,128)(2,1)S(1)}, bf16[4,4,2,4096]{3,2,1,0:T(2,128)(2,1)S(1)}, u32[]{:S(2)}, u32[]{:S(2)}) collective-permute-start(bf16[4,4,2,4096]{3,2,1,0:T(2,128)(2,1)S(1)} %get-tuple-element.120), channel_id=1, source_target_pairs={{0,16},{4,20},{8,24},{12,28},{16,0},{20,4},{24,8},{28,12},{1,17},{... | collective-permute-start | bytes 786440 | tf_op jit(solution)/shard_map/ppermute | solution.py:312
  378.0 29.5 %collective-permute-start.44 = (bf16[4,4,2,4096]{3,2,1,0:T(2,128)(2,1)S(1)}, bf16[4,4,2,4096]{3,2,1,0:T(2,128)(2,1)S(1)}, u32[]{:S(2)}, u32[]{:S(2)}) collective-permute-start(bf16[4,4,2,4096]{3,2,1,0:T(2,128)(2,1)S(1)} %get-tuple-element.121), channel_id=1, source_target_pairs={{0,20},{4,16},{8,28},{12,24},{16,4},{20,0},{24,12},{28,8},{1,21},{... | collective-permute-start | bytes 786440 | tf_op jit(solution)/shard_map/ppermute | solution.py:312
  378.0 43.6 %collective-permute-start.45 = (bf16[4,4,2,4096]{3,2,1,0:T(2,128)(2,1)S(1)}, bf16[4,4,2,4096]{3,2,1,0:T(2,128)(2,1)S(1)}, u32[]{:S(2)}, u32[]{:S(2)}) collective-permute-start(bf16[4,4,2,4096]{3,2,1,0:T(2,128)(2,1)S(1)} %get-tuple-element.122), channel_id=1, source_target_pairs={{0,24},{4,28},{8,16},{12,20},{16,8},{20,12},{24,0},{28,4},{1,25},{... | collective-permute-start | bytes 786440 | tf_op jit(solution)/shard_map/ppermute | solution.py:312
  378.7 49.9 %collective-permute-start.46 = (bf16[4,4,2,4096]{3,2,1,0:T(2,128)(2,1)S(1)}, bf16[4,4,2,4096]{3,2,1,0:T(2,128)(2,1)S(1)}, u32[]{:S(2)}, u32[]{:S(2)}) collective-permute-start(bf16[4,4,2,4096]{3,2,1,0:T(2,128)(2,1)S(1)} %get-tuple-element.123), channel_id=1, source_target_pairs={{0,28},{4,24},{8,20},{12,16},{16,12},{20,8},{24,4},{28,0},{1,29},{... | collective-permute-start | bytes 786440 | tf_op jit(solution)/shard_map/ppermute | solution.py:312
  380.1 214.4 %collective-permute-start.35 = (bf16[4,4,2,2048]{3,2,1,0:T(2,128)(2,1)S(1)}, bf16[4,4,2,2048]{3,2,1,0:T(2,128)(2,1)}, u32[]{:S(2)}, u32[]{:S(2)}) collective-permute-start(bf16[4,4,2,2048]{3,2,1,0:T(2,128)(2,1)S(1)} %get-tuple-element.110), channel_id=1, source_target_pairs={{0,12},{4,8},{8,4},{12,0},{16,28},{20,24},{24,20},{28,16},{1,13},{... | collective-permute-start | bytes 393224 | tf_op jit(solution)/shard_map/ppermute | solution.py:312
  400.5 194.0 %collective-permute-start.36 = (bf16[4,4,2,2048]{3,2,1,0:T(2,128)(2,1)S(1)}, bf16[4,4,2,2048]{3,2,1,0:T(2,128)(2,1)}, u32[]{:S(2)}, u32[]{:S(2)}) collective-permute-start(bf16[4,4,2,2048]{3,2,1,0:T(2,128)(2,1)S(1)} %get-tuple-element.111), channel_id=1, source_target_pairs={{0,16},{4,20},{8,24},{12,28},{16,0},{20,4},{24,8},{28,12},{1,17},{... | collective-permute-start | bytes 393224 | tf_op jit(solution)/shard_map/ppermute | solution.py:312
  407.5 187.0 %collective-permute-start.37 = (bf16[4,4,2,2048]{3,2,1,0:T(2,128)(2,1)S(1)}, bf16[4,4,2,2048]{3,2,1,0:T(2,128)(2,1)}, u32[]{:S(2)}, u32[]{:S(2)}) collective-permute-start(bf16[4,4,2,2048]{3,2,1,0:T(2,128)(2,1)S(1)} %get-tuple-element.112), channel_id=1, source_target_pairs={{0,20},{4,16},{8,28},{12,24},{16,4},{20,0},{24,12},{28,8},{1,21},{... | collective-permute-start | bytes 393224 | tf_op jit(solution)/shard_map/ppermute | solution.py:312
  421.7 172.8 %collective-permute-start.38 = (bf16[4,4,2,2048]{3,2,1,0:T(2,128)(2,1)S(1)}, bf16[4,4,2,2048]{3,2,1,0:T(2,128)(2,1)}, u32[]{:S(2)}, u32[]{:S(2)}) collective-permute-start(bf16[4,4,2,2048]{3,2,1,0:T(2,128)(2,1)S(1)} %get-tuple-element.113), channel_id=1, source_target_pairs={{0,24},{4,28},{8,16},{12,20},{16,8},{20,12},{24,0},{28,4},{1,25},{... | collective-permute-start | bytes 393224 | tf_op jit(solution)/shard_map/ppermute | solution.py:312
  429.3 165.2 %collective-permute-start.39 = (bf16[4,4,2,2048]{3,2,1,0:T(2,128)(2,1)S(1)}, bf16[4,4,2,2048]{3,2,1,0:T(2,128)(2,1)}, u32[]{:S(2)}, u32[]{:S(2)}) collective-permute-start(bf16[4,4,2,2048]{3,2,1,0:T(2,128)(2,1)S(1)} %get-tuple-element.114), channel_id=1, source_target_pairs={{0,28},{4,24},{8,20},{12,16},{16,12},{20,8},{24,4},{28,0},{1,29},{... | collective-permute-start | bytes 393224 | tf_op jit(solution)/shard_map/ppermute | solution.py:312
  (54 other events, 2324.7 us)

commit v3 on v2

--- a/solution.py
+++ b/solution.py
@@ -21,7 +21,8 @@
 QUARTERS = 4
 
 shift_rate = 0.61
-BIG = 48 * 1024 * 1024
+SMALL = 8 * 1024 * 1024
+BIG = 32 * 1024 * 1024
 
 
 def hann_window():
@@ -71,9 +72,10 @@
     return pl.pallas_call(
         functools.partial(pick_kernel, count, comp, start, size, sub),
         in_specs=[pl.BlockSpec(memory_space=pltpu.SMEM)] + [pl.BlockSpec(memory_space=pl.ANY)] * (1 + len(after)),
-        out_specs=[pl.BlockSpec(memory_space=pl.ANY)] * count,
+        out_specs=[pl.BlockSpec(memory_space=pltpu.VMEM)] * count,
         out_shape=[jax.ShapeDtypeStruct((own.shape[1], size), own.dtype)] * count,
         scratch_shapes=[pltpu.SemaphoreType.DMA((count,))],
+        compiler_params=pltpu.CompilerParams(vmem_limit_bytes=SMALL),
         name="pick",
     )(me, own, *after)
 
@@ -236,7 +238,8 @@
     )(me, scales, sums, start, tiles)
 
 
-def modes_kernel(me_ref, mix_ref, spectra_ref, *outs):
+def modes_kernel(after, me_ref, mix_ref, spectra_ref, *refs):
+    outs = refs[after:]
     devices = mix_ref.shape[0]
     part = devices // GROUPS
     freqs = outs[0].shape[0]
@@ -253,24 +256,25 @@
                     out[f, k] = wide[place : place + 2].astype(out.dtype)
 
 
-def modes_of(me, mix, spectra, devices, tile):
+def modes_of(me, mix, spectra, after, devices, tile):
     freqs = NF // devices
     groups, rows, size = spectra.shape
     return pl.pallas_call(
-        modes_kernel,
+        functools.partial(modes_kernel, len(after)),
         grid_spec=pltpu.PrefetchScalarGridSpec(
             num_scalar_prefetch=1,
             grid=(size // tile,),
             in_specs=[
                 pl.BlockSpec(mix.shape, lambda g, m: (0, 0, 0)),
                 pl.BlockSpec((groups, rows, tile), lambda g, m: (0, 0, g)),
-            ],
+            ]
+            + [pl.BlockSpec(memory_space=pl.ANY)] * len(after),
             out_specs=[pl.BlockSpec((freqs, MODES, 2, tile), lambda g, m: (0, 0, 0, g))] * devices,
         ),
         out_shape=[jax.ShapeDtypeStruct((freqs, MODES, 2, size), jnp.bfloat16)] * devices,
         compiler_params=pltpu.CompilerParams(vmem_limit_bytes=BIG),
         name="modes",
-    )(me, mix, spectra)
+    )(me, mix, spectra, *after)
 
 
 def place_kernel(count, comp, start, size, sub, me_ref, *refs):
@@ -294,11 +298,13 @@
     return pl.pallas_call(
         functools.partial(place_kernel, count, comp, start, size, sub),
         in_specs=[pl.BlockSpec(memory_space=pltpu.SMEM)]
-        + [pl.BlockSpec(memory_space=pl.ANY)] * (count + len(more)),
+        + [pl.BlockSpec(memory_space=pltpu.VMEM)] * count
+        + [pl.BlockSpec(memory_space=pl.ANY)] * len(more),
         out_specs=pl.BlockSpec(memory_space=pl.ANY),
         out_shape=jax.ShapeDtypeStruct(shape, jnp.bfloat16),
         input_output_aliases={count + 1: 0} if more else {},
         scratch_shapes=[pltpu.SemaphoreType.DMA((count,))],
+        compiler_params=pltpu.CompilerParams(vmem_limit_bytes=SMALL),
         name="place",
     )(me, *pieces, *more)
 
@@ -366,15 +372,16 @@
         history.append(sums)
     sums = sum_over(sum_over(sums, "space"), "tm")
     mix, energies = solve(me, scales, sums, start_table, tiles, devices)
-    out = None
+    placed = [None]
     shape = (freqs, MODES, comps, 2, cells)
     for chunk in CHUNKS_OUT:
         comp, first, length = CHUNKS_IN[chunk]
-        made = modes_of(me, mix, spectra[chunk], devices, unit)
+        after = [] if len(placed) < 3 else placed[-2:-1]
+        made = modes_of(me, mix, spectra[chunk], after, devices, unit)
         landed = [made[0]] + exchange(made[1:], devices)
-        out = place(me, landed, out, comp, first * unit, length * unit, sub, shape)
+        placed.append(place(me, landed, placed[-1], comp, first * unit, length * unit, sub, shape))
     mine = lax.dynamic_slice_in_dim(energies, index * freqs, freqs, 1)
-    return (jnp.transpose(mine), jnp.transpose(out, (0, 1, 3, 2, 4)))
+    return (jnp.transpose(mine), jnp.transpose(placed[-1], (0, 1, 3, 2, 4)))
 
 
 def solution(mesh):

time: 628 us -> 324 us (0.52)
  Pallas kernels: 389 us -> 28.3 us
  waiting for transfers between devices: 125 us -> 171 us
  local copies, waits for them, and re-layouts: 16.6 us -> 37.1 us
  starting transfers between devices: 92.7 us -> 80.9 us
    pallas_call x4, Pallas kernels: 195 us -> 4.79 us  [place(): pl.pallas_call(functools.partial(place_kernel, count, comp, start, size,...]
    pallas_call x4, Pallas kernels: 171 us -> 2.93 us  [pick(): pl.pallas_call(functools.partial(pick_kernel, count, comp, start, size, s...]
    ppermute x56, waiting for transfers between devices: 113 us -> 159 us  [exchange(): lax.ppermute(pieces[step - 1], 'tm', [(d, d ^ step) for d in range(device...]
    unnamed x83 -> x31, local copies, waits for them, and re-layouts: 9.25 us -> 21.3 us
    ppermute x56, starting transfers between devices: 89.2 us -> 77.2 us  [exchange(): lax.ppermute(pieces[step - 1], 'tm', [(d, d ^ step) for d in range(device...]
    broadcast_in_dim x8, local copies, waits for them, and re-layouts: 7.01 us -> 14.9 us  [band_table(): band = jnp.where(first, low, jnp.where(second, high, nothing))]
  transfers between devices with their start and end apart: 61 -> 61, of which waited for: 22 -> 32; matrix products, arithmetic and copies ran while one was open for 1% -> 6% of each run, Pallas kernels for 47% -> 7%
where the time goes in v3:
time: 324 us; the launch traced here: 323 us
  waiting for transfers between devices  171 us (53%)
  starting transfers between devices  80.9 us (25%)
  local copies, waits for them, and re-layouts  37.1 us (11%)
  Pallas kernels  28.3 us (9%)
  other arithmetic  3.43 us (1%)
    ppermute x56, waiting for transfers between devices, exchange(): lax.ppermute(pieces[step - 1], 'tm', [(d, d ^ step) for d in range(device...  159 us
    ppermute x56, starting transfers between devices, exchange(): lax.ppermute(pieces[step - 1], 'tm', [(d, d ^ step) for d in range(device...  77.2 us
    unnamed x31, local copies, waits for them, and re-layouts  21.3 us
    broadcast_in_dim x8, local copies, waits for them, and re-layouts, band_table(): band = jnp.where(first, low, jnp.where(second, high, nothing))  14.9 us
    pallas_call x4, Pallas kernels, gather(): pl.pallas_call(functools.partial(gather_kernel, count), grid_spec=pltpu.P...  13.1 us
    ppermute x5, waiting for transfers between devices, sum_over(): lax.ppermute(value, axis, [(d, d ^ step) for d in range(count)])  11.8 us
  transfers between devices with their start and end apart: 61, of which 32 were waited for; matrix products, arithmetic and copies ran while one was open for 6% of the time, Pallas kernels for 7%

profile of v3, /device:TPU:8, one launch (start us, length us, event | category | flops | bytes accessed | tf_op | source)
XLA Modules:
  0.0 322.9 jit_solution(18027535906135480299)
XLA Ops:
  0.7 2.8 copy-done
  8.2 2.6 collective-permute-start.10
  13.0 2.8 copy-done.1
  19.8 4.0 %collective-permute-done.8.refs_1_ = bf16[32,4096]{1,0:T(8,128)(2,1)S(1)} collective-permute-done((bf16[32,4096]{1,0:T(8,128)(2,1)S(1)}, bf16[32,4096]{1,0:T(8,128)(2,1)S(1)}, u32[]{:S(2)}, u32[]{:S(2)}) %collective-permute-start.8) | collective-permute-done | bytes 262176 | tf_op jit(solution)/shard_map/ppermute | solution.py:318
  23.8 4.2 %collective-permute-done.9.refs_2_ = bf16[32,4096]{1,0:T(8,128)(2,1)S(1)} collective-permute-done((bf16[32,4096]{1,0:T(8,128)(2,1)}, bf16[32,4096]{1,0:T(8,128)(2,1)S(1)}, u32[]{:S(2)}, u32[]{:S(2)}) %collective-permute-start.9) | collective-permute-done | bytes 262176 | tf_op jit(solution)/shard_map/ppermute | solution.py:318
  28.0 3.8 %collective-permute-start.1 = (bf16[32,4096]{1,0:T(8,128)(2,1)}, bf16[32,4096]{1,0:T(8,128)(2,1)S(1)}, u32[]{:S(2)}, u32[]{:S(2)}) collective-permute-start(bf16[32,4096]{1,0:T(8,128)(2,1)} %get-tuple-element.73), channel_id=1, source_target_pairs={{0,8},{4,12},{8,0},{12,4},{16,24},{20,28},{24,16},{28,20},{1,9},{5... | collective-permute-start | bytes 786440 | tf_op jit(solution)/shard_map/ppermute | solution.py:318
  40.3 2.5 broadcast_in_dim.99
  44.7 2.5 broadcast_in_dim.94
  48.4 2.9 collective-permute-done.12.refs_5_
  51.4 21.5 %collective-permute-done.13.refs_6_ = bf16[32,4096]{1,0:T(8,128)(2,1)S(1)} collective-permute-done((bf16[32,4096]{1,0:T(8,128)(2,1)}, bf16[32,4096]{1,0:T(8,128)(2,1)S(1)}, u32[]{:S(2)}, u32[]{:S(2)}) %collective-permute-start.13) | collective-permute-done | bytes 262176 | tf_op jit(solution)/shard_map/ppermute | solution.py:318
  72.9 2.4 collective-permute-start.5
  75.5 2.8 copy-done.2
  78.2 4.2 %gather.4 = (bf16[2,224,4096]{2,1,0:T(8,128)(2,1)S(1)}, f32[2,16,224]{2,1,0:T(8,128)S(1)}) custom-call(s32[1]{0:T(128)} %bitcast.me_ref, bf16[2,224,256]{2,1,0:T(8,128)(2,1)S(1)} %select_select_fusion.band_ref, f32[16,224]{1,0:T(8,128)S(1)} %fusion.6.fold_ref, f32[1,32768]{1,0:T(1,128)S(1)} %bitcast.27, bf16[3,32,32768]{2,1,0:T(8,128)(2,1)S(1)} %bitcast.20, ...), custom_call_target="tpu_custom_call" | custom-call | flops 1761607680 | bytes 5767168 | tf_op jit(solution)/shard_map/gather/pallas_call | solution.py:121
  84.4 5.3 %collective-permute-start.22 = (bf16[32,2048]{1,0:T(8,128)(2,1)S(1)}, bf16[32,2048]{1,0:T(8,128)(2,1)S(1)}, u32[]{:S(2)}, u32[]{:S(2)}) collective-permute-start(bf16[32,2048]{1,0:T(8,128)(2,1)S(1)} %get-tuple-element.96), channel_id=1, source_target_pairs={{0,8},{4,12},{8,0},{12,4},{16,24},{20,28},{24,16},{28,20},{1,9},{5... | collective-permute-start | bytes 393224 | tf_op jit(solution)/shard_map/ppermute | solution.py:318
  91.6 2.4 collective-permute-start.23
  94.0 3.3 %collective-permute-done.5.refs_5_ = bf16[32,4096]{1,0:T(8,128)(2,1)S(1)} collective-permute-done((bf16[32,4096]{1,0:T(8,128)(2,1)S(1)}, bf16[32,4096]{1,0:T(8,128)(2,1)S(1)}, u32[]{:S(2)}, u32[]{:S(2)}) %collective-permute-start.5) | collective-permute-done | bytes 262176 | tf_op jit(solution)/shard_map/ppermute | solution.py:318
  97.3 10.7 %collective-permute-done.6.refs_6_ = bf16[32,4096]{1,0:T(8,128)(2,1)S(1)} collective-permute-done((bf16[32,4096]{1,0:T(8,128)(2,1)S(1)}, bf16[32,4096]{1,0:T(8,128)(2,1)S(1)}, u32[]{:S(2)}, u32[]{:S(2)}) %collective-permute-start.6) | collective-permute-done | bytes 262176 | tf_op jit(solution)/shard_map/ppermute | solution.py:318
  108.0 4.3 %gather.5 = (bf16[2,224,4096]{2,1,0:T(8,128)(2,1)S(1)}, f32[2,16,224]{2,1,0:T(8,128)S(1)}) custom-call(s32[1]{0:T(128)} %bitcast.me_ref, bf16[2,224,256]{2,1,0:T(8,128)(2,1)S(1)} %select_select_fusion.band_ref, f32[16,224]{1,0:T(8,128)S(1)} %fusion.6.fold_ref, f32[1,32768]{1,0:T(1,128)S(1)} %bitcast.28, bf16[3,32,32768]{2,1,0:T(8,128)(2,1)S(1)} %bitcast.22, ...), custom_call_target="tpu_custom_call" | custom-call | flops 1761607680 | bytes 5767168 | tf_op jit(solution)/shard_map/gather/pallas_call | solution.py:121
  114.5 2.5 collective-permute-start.26
  118.5 5.2 %collective-permute-start.15 = (bf16[32,2048]{1,0:T(8,128)(2,1)S(1)}, bf16[32,2048]{1,0:T(8,128)(2,1)S(1)}, u32[]{:S(2)}, u32[]{:S(2)}) collective-permute-start(bf16[32,2048]{1,0:T(8,128)(2,1)S(1)} %get-tuple-element.89), channel_id=1, source_target_pairs={{0,8},{4,12},{8,0},{12,4},{16,24},{20,28},{24,16},{28,20},{1,9},{5... | collective-permute-start | bytes 393224 | tf_op jit(solution)/shard_map/ppermute | solution.py:318
  126.5 7.9 %collective-permute-done.27.refs_6_ = bf16[32,2048]{1,0:T(8,128)(2,1)S(1)} collective-permute-done((bf16[32,2048]{1,0:T(8,128)(2,1)S(1)}, bf16[32,2048]{1,0:T(8,128)(2,1)S(1)}, u32[]{:S(2)}, u32[]{:S(2)}) %collective-permute-start.27) | collective-permute-done | bytes 131104 | tf_op jit(solution)/shard_map/ppermute | solution.py:318
  137.1 2.3 gather.6
  141.3 4.9 %collective-permute-done.19.refs_5_ = bf16[32,2048]{1,0:T(8,128)(2,1)S(1)} collective-permute-done((bf16[32,2048]{1,0:T(8,128)(2,1)S(1)}, bf16[32,2048]{1,0:T(8,128)(2,1)S(1)}, u32[]{:S(2)}, u32[]{:S(2)}) %collective-permute-start.19) | collective-permute-done | bytes 131104 | tf_op jit(solution)/shard_map/ppermute | solution.py:318
  147.9 2.3 gather.7
  154.2 2.4 collective-permute-done.29
  158.0 2.6 collective-permute-done.30
  165.5 3.8 %collective-permute-done.32 = f32[2,16,224]{2,1,0:T(8,128)S(1)} collective-permute-done((f32[2,16,224]{2,1,0:T(8,128)S(1)}, f32[2,16,224]{2,1,0:T(8,128)S(1)}, u32[]{:S(2)}, u32[]{:S(2)}) %collective-permute-start.32) | collective-permute-done | bytes 28704 | tf_op jit(solution)/shard_map/ppermute | solution.py:326
  176.2 2.0 copy-done.8
  186.7 7.2 %collective-permute-done.44.refs_5_ = bf16[4,4,2,2048]{3,2,1,0:T(2,128)(2,1)S(1)} collective-permute-done((bf16[4,4,2,2048]{3,2,1,0:T(2,128)(2,1)S(1)}, bf16[4,4,2,2048]{3,2,1,0:T(2,128)(2,1)S(1)}, u32[]{:S(2)}, u32[]{:S(2)}) %collective-permute-start.44) | collective-permute-done | bytes 131104 | tf_op jit(solution)/shard_map/ppermute | solution.py:318
  194.8 5.3 %collective-permute-done.45.refs_6_ = bf16[4,4,2,2048]{3,2,1,0:T(2,128)(2,1)S(1)} collective-permute-done((bf16[4,4,2,2048]{3,2,1,0:T(2,128)(2,1)S(1)}, bf16[4,4,2,2048]{3,2,1,0:T(2,128)(2,1)S(1)}, u32[]{:S(2)}, u32[]{:S(2)}) %collective-permute-start.45) | collective-permute-done | bytes 131104 | tf_op jit(solution)/shard_map/ppermute | solution.py:318
  200.1 15.6 %collective-permute-done.46.refs_7_ = bf16[4,4,2,2048]{3,2,1,0:T(2,128)(2,1)S(1)} collective-permute-done((bf16[4,4,2,2048]{3,2,1,0:T(2,128)(2,1)S(1)}, bf16[4,4,2,2048]{3,2,1,0:T(2,128)(2,1)S(1)}, u32[]{:S(2)}, u32[]{:S(2)}) %collective-permute-start.46) | collective-permute-done | bytes 131104 | tf_op jit(solution)/shard_map/ppermute | solution.py:318
  219.5 2.8 copy-done.3
  225.0 2.5 collective-permute-done.36.refs_4_
  228.9 4.3 %collective-permute-done.37.refs_5_ = bf16[4,4,2,4096]{3,2,1,0:T(2,128)(2,1)S(1)} collective-permute-done((bf16[4,4,2,4096]{3,2,1,0:T(2,128)(2,1)S(1)}, bf16[4,4,2,4096]{3,2,1,0:T(2,128)(2,1)S(1)}, u32[]{:S(2)}, u32[]{:S(2)}) %collective-permute-start.37) | collective-permute-done | bytes 262176 | tf_op jit(solution)/shard_map/ppermute | solution.py:318
  233.2 7.7 %collective-permute-done.38.refs_6_ = bf16[4,4,2,4096]{3,2,1,0:T(2,128)(2,1)S(1)} collective-permute-done((bf16[4,4,2,4096]{3,2,1,0:T(2,128)(2,1)S(1)}, bf16[4,4,2,4096]{3,2,1,0:T(2,128)(2,1)S(1)}, u32[]{:S(2)}, u32[]{:S(2)}) %collective-permute-start.38) | collective-permute-done | bytes 262176 | tf_op jit(solution)/shard_map/ppermute | solution.py:318
  240.8 3.2 collective-permute-done.39.refs_7_
  246.3 2.8 copy-done.4
  251.7 2.4 collective-permute-start.56
  254.1 3.4 %collective-permute-done.47.refs_1_ = bf16[4,4,2,2048]{3,2,1,0:T(2,128)(2,1)S(1)} collective-permute-done((bf16[4,4,2,2048]{3,2,1,0:T(2,128)(2,1)S(1)}, bf16[4,4,2,2048]{3,2,1,0:T(2,128)(2,1)S(1)}, u32[]{:S(2)}, u32[]{:S(2)}) %collective-permute-start.47) | collective-permute-done | bytes 131104 | tf_op jit(solution)/shard_map/ppermute | solution.py:318
  257.5 2.2 collective-permute-done.48.refs_2_
  259.7 4.5 %collective-permute-start.58 = (bf16[4,4,2,4096]{3,2,1,0:T(2,128)(2,1)S(1)}, bf16[4,4,2,4096]{3,2,1,0:T(2,128)(2,1)S(1)}, u32[]{:S(2)}, u32[]{:S(2)}) collective-permute-start(bf16[4,4,2,4096]{3,2,1,0:T(2,128)(2,1)S(1)} %get-tuple-element.139), channel_id=1, source_target_pairs={{0,20},{4,16},{8,28},{12,24},{16,4},{20,0},{24,12},{28,8},{1,21},{... | collective-permute-start | bytes 786440 | tf_op jit(solution)/shard_map/ppermute | solution.py:318
  265.3 3.1 collective-permute-start.49
  268.4 17.9 %collective-permute-done.57.refs_4_ = bf16[4,4,2,4096]{3,2,1,0:T(2,128)(2,1)S(1)} collective-permute-done((bf16[4,4,2,4096]{3,2,1,0:T(2,128)(2,1)S(1)}, bf16[4,4,2,4096]{3,2,1,0:T(2,128)(2,1)S(1)}, u32[]{:S(2)}, u32[]{:S(2)}) %collective-permute-start.57) | collective-permute-done | bytes 262176 | tf_op jit(solution)/shard_map/ppermute | solution.py:318
  286.2 3.4 %collective-permute-start.50 = (bf16[4,4,2,2048]{3,2,1,0:T(2,128)(2,1)}, bf16[4,4,2,2048]{3,2,1,0:T(2,128)(2,1)S(1)}, u32[]{:S(2)}, u32[]{:S(2)}) collective-permute-start(bf16[4,4,2,2048]{3,2,1,0:T(2,128)(2,1)} %get-tuple-element.129), channel_id=1, source_target_pairs={{0,16},{4,20},{8,24},{12,28},{16,0},{20,4},{24,8},{28,12},{1,17},{... | collective-permute-start | bytes 393224 | tf_op jit(solution)/shard_map/ppermute | solution.py:318
  289.6 7.9 %collective-permute-done.58.refs_5_ = bf16[4,4,2,4096]{3,2,1,0:T(2,128)(2,1)S(1)} collective-permute-done((bf16[4,4,2,4096]{3,2,1,0:T(2,128)(2,1)S(1)}, bf16[4,4,2,4096]{3,2,1,0:T(2,128)(2,1)S(1)}, u32[]{:S(2)}, u32[]{:S(2)}) %collective-permute-start.58) | collective-permute-done | bytes 262176 | tf_op jit(solution)/shard_map/ppermute | solution.py:318
  297.5 4.3 %collective-permute-start.51 = (bf16[4,4,2,2048]{3,2,1,0:T(2,128)(2,1)S(1)}, bf16[4,4,2,2048]{3,2,1,0:T(2,128)(2,1)S(1)}, u32[]{:S(2)}, u32[]{:S(2)}) collective-permute-start(bf16[4,4,2,2048]{3,2,1,0:T(2,128)(2,1)S(1)} %get-tuple-element.130), channel_id=1, source_target_pairs={{0,20},{4,16},{8,28},{12,24},{16,4},{20,0},{24,12},{28,8},{1,21},{... | collective-permute-start | bytes 393224 | tf_op jit(solution)/shard_map/ppermute | solution.py:318
  301.7 7.0 %collective-permute-done.59.refs_6_ = bf16[4,4,2,4096]{3,2,1,0:T(2,128)(2,1)S(1)} collective-permute-done((bf16[4,4,2,4096]{3,2,1,0:T(2,128)(2,1)S(1)}, bf16[4,4,2,4096]{3,2,1,0:T(2,128)(2,1)S(1)}, u32[]{:S(2)}, u32[]{:S(2)}) %collective-permute-start.59) | collective-permute-done | bytes 262176 | tf_op jit(solution)/shard_map/ppermute | solution.py:318
  309.8 4.6 %collective-permute-done.60.refs_7_ = bf16[4,4,2,4096]{3,2,1,0:T(2,128)(2,1)S(1)} collective-permute-done((bf16[4,4,2,4096]{3,2,1,0:T(2,128)(2,1)S(1)}, bf16[4,4,2,4096]{3,2,1,0:T(2,128)(2,1)S(1)}, u32[]{:S(2)}, u32[]{:S(2)}) %collective-permute-start.60) | collective-permute-done | bytes 262176 | tf_op jit(solution)/shard_map/ppermute | solution.py:318
  (159 shorter events, 87.6 us)
Async XLA Ops:
  4.6 13.6 %collective-permute-start.7 = (bf16[32,4096]{1,0:T(8,128)(2,1)S(1)}, bf16[32,4096]{1,0:T(8,128)(2,1)S(1)}, u32[]{:S(2)}, u32[]{:S(2)}) collective-permute-start(bf16[32,4096]{1,0:T(8,128)(2,1)S(1)} %get-tuple-element.79), channel_id=1, source_target_pairs={{0,4},{4,0},{8,12},{12,8},{16,20},{20,16},{24,28},{28,24},{1,5},{5... | collective-permute-start | bytes 786440 | tf_op jit(solution)/shard_map/ppermute | solution.py:318
  6.2 17.6 %collective-permute-start.8 = (bf16[32,4096]{1,0:T(8,128)(2,1)S(1)}, bf16[32,4096]{1,0:T(8,128)(2,1)S(1)}, u32[]{:S(2)}, u32[]{:S(2)}) collective-permute-start(bf16[32,4096]{1,0:T(8,128)(2,1)S(1)} %get-tuple-element.80), channel_id=1, source_target_pairs={{0,8},{4,12},{8,0},{12,4},{16,24},{20,28},{24,16},{28,20},{1,9},{5... | collective-permute-start | bytes 786440 | tf_op jit(solution)/shard_map/ppermute | solution.py:318
  6.6 21.4 %collective-permute-start.9 = (bf16[32,4096]{1,0:T(8,128)(2,1)}, bf16[32,4096]{1,0:T(8,128)(2,1)S(1)}, u32[]{:S(2)}, u32[]{:S(2)}) collective-permute-start(bf16[32,4096]{1,0:T(8,128)(2,1)} %get-tuple-element.81), channel_id=1, source_target_pairs={{0,12},{4,8},{8,4},{12,0},{16,28},{20,24},{24,20},{28,16},{1,13},{... | collective-permute-start | bytes 786440 | tf_op jit(solution)/shard_map/ppermute | solution.py:318
  8.2 19.8 %collective-permute-start.10 = (bf16[32,4096]{1,0:T(8,128)(2,1)S(1)}, bf16[32,4096]{1,0:T(8,128)(2,1)S(1)}, u32[]{:S(2)}, u32[]{:S(2)}) collective-permute-start(bf16[32,4096]{1,0:T(8,128)(2,1)S(1)} %get-tuple-element.82), channel_id=1, source_target_pairs={{0,16},{4,20},{8,24},{12,28},{16,0},{20,4},{24,8},{28,12},{1,17},{... | collective-permute-start | bytes 786440 | tf_op jit(solution)/shard_map/ppermute | solution.py:318
  10.8 37.6 %collective-permute-start.11 = (bf16[32,4096]{1,0:T(8,128)(2,1)}, bf16[32,4096]{1,0:T(8,128)(2,1)S(1)}, u32[]{:S(2)}, u32[]{:S(2)}) collective-permute-start(bf16[32,4096]{1,0:T(8,128)(2,1)} %get-tuple-element.83), channel_id=1, source_target_pairs={{0,20},{4,16},{8,28},{12,24},{16,4},{20,0},{24,12},{28,8},{1,21},{... | collective-permute-start | bytes 786440 | tf_op jit(solution)/shard_map/ppermute | solution.py:318
  18.2 33.2 %collective-permute-start.12 = (bf16[32,4096]{1,0:T(8,128)(2,1)}, bf16[32,4096]{1,0:T(8,128)(2,1)S(1)}, u32[]{:S(2)}, u32[]{:S(2)}) collective-permute-start(bf16[32,4096]{1,0:T(8,128)(2,1)} %get-tuple-element.84), channel_id=1, source_target_pairs={{0,24},{4,28},{8,16},{12,20},{16,8},{20,12},{24,0},{28,4},{1,25},{... | collective-permute-start | bytes 786440 | tf_op jit(solution)/shard_map/ppermute | solution.py:318
  23.7 49.2 %collective-permute-start.13 = (bf16[32,4096]{1,0:T(8,128)(2,1)}, bf16[32,4096]{1,0:T(8,128)(2,1)S(1)}, u32[]{:S(2)}, u32[]{:S(2)}) collective-permute-start(bf16[32,4096]{1,0:T(8,128)(2,1)} %get-tuple-element.85), channel_id=1, source_target_pairs={{0,28},{4,24},{8,20},{12,16},{16,12},{20,8},{24,4},{28,0},{1,29},{... | collective-permute-start | bytes 786440 | tf_op jit(solution)/shard_map/ppermute | solution.py:318
  28.0 44.9 %collective-permute-start = (bf16[32,4096]{1,0:T(8,128)(2,1)}, bf16[32,4096]{1,0:T(8,128)(2,1)S(1)}, u32[]{:S(2)}, u32[]{:S(2)}) collective-permute-start(bf16[32,4096]{1,0:T(8,128)(2,1)} %get-tuple-element.72), channel_id=1, source_target_pairs={{0,4},{4,0},{8,12},{12,8},{16,20},{20,16},{24,28},{28,24},{1,5},{5... | collective-permute-start | bytes 786440 | tf_op jit(solution)/shard_map/ppermute | solution.py:318
  28.0 47.3 %collective-permute-start.1 = (bf16[32,4096]{1,0:T(8,128)(2,1)}, bf16[32,4096]{1,0:T(8,128)(2,1)S(1)}, u32[]{:S(2)}, u32[]{:S(2)}) collective-permute-start(bf16[32,4096]{1,0:T(8,128)(2,1)} %get-tuple-element.73), channel_id=1, source_target_pairs={{0,8},{4,12},{8,0},{12,4},{16,24},{20,28},{24,16},{28,20},{1,9},{5... | collective-permute-start | bytes 786440 | tf_op jit(solution)/shard_map/ppermute | solution.py:318
  48.4 34.5 %collective-permute-start.2 = (bf16[32,4096]{1,0:T(8,128)(2,1)}, bf16[32,4096]{1,0:T(8,128)(2,1)S(1)}, u32[]{:S(2)}, u32[]{:S(2)}) collective-permute-start(bf16[32,4096]{1,0:T(8,128)(2,1)} %copy-done.12), channel_id=1, source_target_pairs={{0,12},{4,8},{8,4},{12,0},{16,28},{20,24},{24,20},{28,16},{1,13},{... | collective-permute-start | bytes 786440 | tf_op jit(solution)/shard_map/ppermute | solution.py:318
  51.4 33.0 %collective-permute-start.3 = (bf16[32,4096]{1,0:T(8,128)(2,1)S(1)}, bf16[32,4096]{1,0:T(8,128)(2,1)S(1)}, u32[]{:S(2)}, u32[]{:S(2)}) collective-permute-start(bf16[32,4096]{1,0:T(8,128)(2,1)S(1)} %get-tuple-element.75), channel_id=1, source_target_pairs={{0,16},{4,20},{8,24},{12,28},{16,0},{20,4},{24,8},{28,12},{1,17},{... | collective-permute-start | bytes 786440 | tf_op jit(solution)/shard_map/ppermute | solution.py:318
  72.9 18.7 %collective-permute-start.4 = (bf16[32,4096]{1,0:T(8,128)(2,1)S(1)}, bf16[32,4096]{1,0:T(8,128)(2,1)S(1)}, u32[]{:S(2)}, u32[]{:S(2)}) collective-permute-start(bf16[32,4096]{1,0:T(8,128)(2,1)S(1)} %get-tuple-element.76), channel_id=1, source_target_pairs={{0,20},{4,16},{8,28},{12,24},{16,4},{20,0},{24,12},{28,8},{1,21},{... | collective-permute-start | bytes 786440 | tf_op jit(solution)/shard_map/ppermute | solution.py:318
  72.9 24.4 %collective-permute-start.5 = (bf16[32,4096]{1,0:T(8,128)(2,1)S(1)}, bf16[32,4096]{1,0:T(8,128)(2,1)S(1)}, u32[]{:S(2)}, u32[]{:S(2)}) collective-permute-start(bf16[32,4096]{1,0:T(8,128)(2,1)S(1)} %get-tuple-element.77), channel_id=1, source_target_pairs={{0,24},{4,28},{8,16},{12,20},{16,8},{20,12},{24,0},{28,4},{1,25},{... | collective-permute-start | bytes 786440 | tf_op jit(solution)/shard_map/ppermute | solution.py:318
  75.3 32.7 %collective-permute-start.6 = (bf16[32,4096]{1,0:T(8,128)(2,1)S(1)}, bf16[32,4096]{1,0:T(8,128)(2,1)S(1)}, u32[]{:S(2)}, u32[]{:S(2)}) collective-permute-start(bf16[32,4096]{1,0:T(8,128)(2,1)S(1)} %get-tuple-element.78), channel_id=1, source_target_pairs={{0,28},{4,24},{8,20},{12,16},{16,12},{20,8},{24,4},{28,0},{1,29},{... | collective-permute-start | bytes 786440 | tf_op jit(solution)/shard_map/ppermute | solution.py:318
  82.9 31.6 %collective-permute-start.21 = (bf16[32,2048]{1,0:T(8,128)(2,1)S(1)}, bf16[32,2048]{1,0:T(8,128)(2,1)S(1)}, u32[]{:S(2)}, u32[]{:S(2)}) collective-permute-start(bf16[32,2048]{1,0:T(8,128)(2,1)S(1)} %get-tuple-element.95), channel_id=1, source_target_pairs={{0,4},{4,0},{8,12},{12,8},{16,20},{20,16},{24,28},{28,24},{1,5},{5... | collective-permute-start | bytes 393224 | tf_op jit(solution)/shard_map/ppermute | solution.py:318
  84.4 32.6 %collective-permute-start.22 = (bf16[32,2048]{1,0:T(8,128)(2,1)S(1)}, bf16[32,2048]{1,0:T(8,128)(2,1)S(1)}, u32[]{:S(2)}, u32[]{:S(2)}) collective-permute-start(bf16[32,2048]{1,0:T(8,128)(2,1)S(1)} %get-tuple-element.96), channel_id=1, source_target_pairs={{0,8},{4,12},{8,0},{12,4},{16,24},{20,28},{24,16},{28,20},{1,9},{5... | collective-permute-start | bytes 393224 | tf_op jit(solution)/shard_map/ppermute | solution.py:318
  91.6 25.5 %collective-permute-start.23 = (bf16[32,2048]{1,0:T(8,128)(2,1)S(1)}, bf16[32,2048]{1,0:T(8,128)(2,1)S(1)}, u32[]{:S(2)}, u32[]{:S(2)}) collective-permute-start(bf16[32,2048]{1,0:T(8,128)(2,1)S(1)} %get-tuple-element.97), channel_id=1, source_target_pairs={{0,12},{4,8},{8,4},{12,0},{16,28},{20,24},{24,20},{28,16},{1,13},{... | collective-permute-start | bytes 393224 | tf_op jit(solution)/shard_map/ppermute | solution.py:318
  97.3 21.3 %collective-permute-start.24 = (bf16[32,2048]{1,0:T(8,128)(2,1)S(1)}, bf16[32,2048]{1,0:T(8,128)(2,1)S(1)}, u32[]{:S(2)}, u32[]{:S(2)}) collective-permute-start(bf16[32,2048]{1,0:T(8,128)(2,1)S(1)} %get-tuple-element.98), channel_id=1, source_target_pairs={{0,16},{4,20},{8,24},{12,28},{16,0},{20,4},{24,8},{28,12},{1,17},{... | collective-permute-start | bytes 393224 | tf_op jit(solution)/shard_map/ppermute | solution.py:318
  108.0 15.8 %collective-permute-start.25 = (bf16[32,2048]{1,0:T(8,128)(2,1)S(1)}, bf16[32,2048]{1,0:T(8,128)(2,1)S(1)}, u32[]{:S(2)}, u32[]{:S(2)}) collective-permute-start(bf16[32,2048]{1,0:T(8,128)(2,1)S(1)} %get-tuple-element.99), channel_id=1, source_target_pairs={{0,20},{4,16},{8,28},{12,24},{16,4},{20,0},{24,12},{28,8},{1,21},{... | collective-permute-start | bytes 393224 | tf_op jit(solution)/shard_map/ppermute | solution.py:318
  114.5 12.0 %collective-permute-start.26 = (bf16[32,2048]{1,0:T(8,128)(2,1)S(1)}, bf16[32,2048]{1,0:T(8,128)(2,1)S(1)}, u32[]{:S(2)}, u32[]{:S(2)}) collective-permute-start(bf16[32,2048]{1,0:T(8,128)(2,1)S(1)} %get-tuple-element.100), channel_id=1, source_target_pairs={{0,24},{4,28},{8,16},{12,20},{16,8},{20,12},{24,0},{28,4},{1,25},{... | collective-permute-start | bytes 393224 | tf_op jit(solution)/shard_map/ppermute | solution.py:318
  117.0 17.5 %collective-permute-start.27 = (bf16[32,2048]{1,0:T(8,128)(2,1)S(1)}, bf16[32,2048]{1,0:T(8,128)(2,1)S(1)}, u32[]{:S(2)}, u32[]{:S(2)}) collective-permute-start(bf16[32,2048]{1,0:T(8,128)(2,1)S(1)} %get-tuple-element.101), channel_id=1, source_target_pairs={{0,28},{4,24},{8,20},{12,16},{16,12},{20,8},{24,4},{28,0},{1,29},{... | collective-permute-start | bytes 393224 | tf_op jit(solution)/shard_map/ppermute | solution.py:318
  117.1 17.3 %collective-permute-start.14 = (bf16[32,2048]{1,0:T(8,128)(2,1)S(1)}, bf16[32,2048]{1,0:T(8,128)(2,1)S(1)}, u32[]{:S(2)}, u32[]{:S(2)}) collective-permute-start(bf16[32,2048]{1,0:T(8,128)(2,1)S(1)} %get-tuple-element.88), channel_id=1, source_target_pairs={{0,4},{4,0},{8,12},{12,8},{16,20},{20,16},{24,28},{28,24},{1,5},{5... | collective-permute-start | bytes 393224 | tf_op jit(solution)/shard_map/ppermute | solution.py:318
  118.5 17.6 %collective-permute-start.15 = (bf16[32,2048]{1,0:T(8,128)(2,1)S(1)}, bf16[32,2048]{1,0:T(8,128)(2,1)S(1)}, u32[]{:S(2)}, u32[]{:S(2)}) collective-permute-start(bf16[32,2048]{1,0:T(8,128)(2,1)S(1)} %get-tuple-element.89), channel_id=1, source_target_pairs={{0,8},{4,12},{8,0},{12,4},{16,24},{20,28},{24,16},{28,20},{1,9},{5... | collective-permute-start | bytes 393224 | tf_op jit(solution)/shard_map/ppermute | solution.py:318
  123.8 15.6 %collective-permute-start.16 = (bf16[32,2048]{1,0:T(8,128)(2,1)S(1)}, bf16[32,2048]{1,0:T(8,128)(2,1)S(1)}, u32[]{:S(2)}, u32[]{:S(2)}) collective-permute-start(bf16[32,2048]{1,0:T(8,128)(2,1)S(1)} %get-tuple-element.90), channel_id=1, source_target_pairs={{0,12},{4,8},{8,4},{12,0},{16,28},{20,24},{24,20},{28,16},{1,13},{... | collective-permute-start | bytes 393224 | tf_op jit(solution)/shard_map/ppermute | solution.py:318
  126.5 12.9 %collective-permute-start.17 = (bf16[32,2048]{1,0:T(8,128)(2,1)S(1)}, bf16[32,2048]{1,0:T(8,128)(2,1)S(1)}, u32[]{:S(2)}, u32[]{:S(2)}) collective-permute-start(bf16[32,2048]{1,0:T(8,128)(2,1)S(1)} %get-tuple-element.91), channel_id=1, source_target_pairs={{0,16},{4,20},{8,24},{12,28},{16,0},{20,4},{24,8},{28,12},{1,17},{... | collective-permute-start | bytes 393224 | tf_op jit(solution)/shard_map/ppermute | solution.py:318
  134.4 11.8 %collective-permute-start.19 = (bf16[32,2048]{1,0:T(8,128)(2,1)S(1)}, bf16[32,2048]{1,0:T(8,128)(2,1)S(1)}, u32[]{:S(2)}, u32[]{:S(2)}) collective-permute-start(bf16[32,2048]{1,0:T(8,128)(2,1)S(1)} %get-tuple-element.93), channel_id=1, source_target_pairs={{0,24},{4,28},{8,16},{12,20},{16,8},{20,12},{24,0},{28,4},{1,25},{... | collective-permute-start | bytes 393224 | tf_op jit(solution)/shard_map/ppermute | solution.py:318
  136.1 11.8 %collective-permute-start.20 = (bf16[32,2048]{1,0:T(8,128)(2,1)S(1)}, bf16[32,2048]{1,0:T(8,128)(2,1)S(1)}, u32[]{:S(2)}, u32[]{:S(2)}) collective-permute-start(bf16[32,2048]{1,0:T(8,128)(2,1)S(1)} %get-tuple-element.94), channel_id=1, source_target_pairs={{0,28},{4,24},{8,20},{12,16},{16,12},{20,8},{24,4},{28,0},{1,29},{... | collective-permute-start | bytes 393224 | tf_op jit(solution)/shard_map/ppermute | solution.py:318
  180.1 35.6 %collective-permute-start.33 = (bf16[4,4,2,4096]{3,2,1,0:T(2,128)(2,1)S(1)}, bf16[4,4,2,4096]{3,2,1,0:T(2,128)(2,1)S(1)}, u32[]{:S(2)}, u32[]{:S(2)}) collective-permute-start(bf16[4,4,2,4096]{3,2,1,0:T(2,128)(2,1)S(1)} %get-tuple-element.109), channel_id=1, source_target_pairs={{0,4},{4,0},{8,12},{12,8},{16,20},{20,16},{24,28},{28,24},{1,5},{5... | collective-permute-start | bytes 786440 | tf_op jit(solution)/shard_map/ppermute | solution.py:318
  181.1 35.8 %collective-permute-start.34 = (bf16[4,4,2,4096]{3,2,1,0:T(2,128)(2,1)S(1)}, bf16[4,4,2,4096]{3,2,1,0:T(2,128)(2,1)S(1)}, u32[]{:S(2)}, u32[]{:S(2)}) collective-permute-start(bf16[4,4,2,4096]{3,2,1,0:T(2,128)(2,1)S(1)} %get-tuple-element.110), channel_id=1, source_target_pairs={{0,8},{4,12},{8,0},{12,4},{16,24},{20,28},{24,16},{28,20},{1,9},{5... | collective-permute-start | bytes 786440 | tf_op jit(solution)/shard_map/ppermute | solution.py:318
  183.1 10.8 %collective-permute-start.44 = (bf16[4,4,2,2048]{3,2,1,0:T(2,128)(2,1)S(1)}, bf16[4,4,2,2048]{3,2,1,0:T(2,128)(2,1)S(1)}, u32[]{:S(2)}, u32[]{:S(2)}) collective-permute-start(bf16[4,4,2,2048]{3,2,1,0:T(2,128)(2,1)S(1)} %get-tuple-element.122), channel_id=1, source_target_pairs={{0,20},{4,16},{8,28},{12,24},{16,4},{20,0},{24,12},{28,8},{1,21},{... | collective-permute-start | bytes 393224 | tf_op jit(solution)/shard_map/ppermute | solution.py:318
  183.8 16.3 %collective-permute-start.45 = (bf16[4,4,2,2048]{3,2,1,0:T(2,128)(2,1)S(1)}, bf16[4,4,2,2048]{3,2,1,0:T(2,128)(2,1)S(1)}, u32[]{:S(2)}, u32[]{:S(2)}) collective-permute-start(bf16[4,4,2,2048]{3,2,1,0:T(2,128)(2,1)S(1)} %get-tuple-element.123), channel_id=1, source_target_pairs={{0,24},{4,28},{8,16},{12,20},{16,8},{20,12},{24,0},{28,4},{1,25},{... | collective-permute-start | bytes 393224 | tf_op jit(solution)/shard_map/ppermute | solution.py:318
  185.2 30.6 %collective-permute-start.46 = (bf16[4,4,2,2048]{3,2,1,0:T(2,128)(2,1)S(1)}, bf16[4,4,2,2048]{3,2,1,0:T(2,128)(2,1)S(1)}, u32[]{:S(2)}, u32[]{:S(2)}) collective-permute-start(bf16[4,4,2,2048]{3,2,1,0:T(2,128)(2,1)S(1)} %get-tuple-element.124), channel_id=1, source_target_pairs={{0,28},{4,24},{8,20},{12,16},{16,12},{20,8},{24,4},{28,0},{1,29},{... | collective-permute-start | bytes 393224 | tf_op jit(solution)/shard_map/ppermute | solution.py:318
  193.9 30.2 %collective-permute-start.35 = (bf16[4,4,2,4096]{3,2,1,0:T(2,128)(2,1)S(1)}, bf16[4,4,2,4096]{3,2,1,0:T(2,128)(2,1)S(1)}, u32[]{:S(2)}, u32[]{:S(2)}) collective-permute-start(bf16[4,4,2,4096]{3,2,1,0:T(2,128)(2,1)S(1)} %get-tuple-element.111), channel_id=1, source_target_pairs={{0,12},{4,8},{8,4},{12,0},{16,28},{20,24},{24,20},{28,16},{1,13},{... | collective-permute-start | bytes 786440 | tf_op jit(solution)/shard_map/ppermute | solution.py:318
  200.1 27.3 %collective-permute-start.36 = (bf16[4,4,2,4096]{3,2,1,0:T(2,128)(2,1)S(1)}, bf16[4,4,2,4096]{3,2,1,0:T(2,128)(2,1)S(1)}, u32[]{:S(2)}, u32[]{:S(2)}) collective-permute-start(bf16[4,4,2,4096]{3,2,1,0:T(2,128)(2,1)S(1)} %get-tuple-element.112), channel_id=1, source_target_pairs={{0,16},{4,20},{8,24},{12,28},{16,0},{20,4},{24,8},{28,12},{1,17},{... | collective-permute-start | bytes 786440 | tf_op jit(solution)/shard_map/ppermute | solution.py:318
  215.7 17.5 %collective-permute-start.37 = (bf16[4,4,2,4096]{3,2,1,0:T(2,128)(2,1)S(1)}, bf16[4,4,2,4096]{3,2,1,0:T(2,128)(2,1)S(1)}, u32[]{:S(2)}, u32[]{:S(2)}) collective-permute-start(bf16[4,4,2,4096]{3,2,1,0:T(2,128)(2,1)S(1)} %get-tuple-element.113), channel_id=1, source_target_pairs={{0,20},{4,16},{8,28},{12,24},{16,4},{20,0},{24,12},{28,8},{1,21},{... | collective-permute-start | bytes 786440 | tf_op jit(solution)/shard_map/ppermute | solution.py:318
  215.7 25.1 %collective-permute-start.38 = (bf16[4,4,2,4096]{3,2,1,0:T(2,128)(2,1)S(1)}, bf16[4,4,2,4096]{3,2,1,0:T(2,128)(2,1)S(1)}, u32[]{:S(2)}, u32[]{:S(2)}) collective-permute-start(bf16[4,4,2,4096]{3,2,1,0:T(2,128)(2,1)S(1)} %get-tuple-element.114), channel_id=1, source_target_pairs={{0,24},{4,28},{8,16},{12,20},{16,8},{20,12},{24,0},{28,4},{1,25},{... | collective-permute-start | bytes 786440 | tf_op jit(solution)/shard_map/ppermute | solution.py:318
  216.9 27.2 %collective-permute-start.39 = (bf16[4,4,2,4096]{3,2,1,0:T(2,128)(2,1)S(1)}, bf16[4,4,2,4096]{3,2,1,0:T(2,128)(2,1)S(1)}, u32[]{:S(2)}, u32[]{:S(2)}) collective-permute-start(bf16[4,4,2,4096]{3,2,1,0:T(2,128)(2,1)S(1)} %get-tuple-element.115), channel_id=1, source_target_pairs={{0,28},{4,24},{8,20},{12,16},{16,12},{20,8},{24,4},{28,0},{1,29},{... | collective-permute-start | bytes 786440 | tf_op jit(solution)/shard_map/ppermute | solution.py:318
  224.1 40.1 %collective-permute-start.54 = (bf16[4,4,2,4096]{3,2,1,0:T(2,128)(2,1)S(1)}, bf16[4,4,2,4096]{3,2,1,0:T(2,128)(2,1)S(1)}, u32[]{:S(2)}, u32[]{:S(2)}) collective-permute-start(bf16[4,4,2,4096]{3,2,1,0:T(2,128)(2,1)S(1)} %get-tuple-element.135), channel_id=1, source_target_pairs={{0,4},{4,0},{8,12},{12,8},{16,20},{20,16},{24,28},{28,24},{1,5},{5... | collective-permute-start | bytes 786440 | tf_op jit(solution)/shard_map/ppermute | solution.py:318
  227.4 36.8 %collective-permute-start.55 = (bf16[4,4,2,4096]{3,2,1,0:T(2,128)(2,1)S(1)}, bf16[4,4,2,4096]{3,2,1,0:T(2,128)(2,1)S(1)}, u32[]{:S(2)}, u32[]{:S(2)}) collective-permute-start(bf16[4,4,2,4096]{3,2,1,0:T(2,128)(2,1)S(1)} %get-tuple-element.136), channel_id=1, source_target_pairs={{0,8},{4,12},{8,0},{12,4},{16,24},{20,28},{24,16},{28,20},{1,9},{5... | collective-permute-start | bytes 786440 | tf_op jit(solution)/shard_map/ppermute | solution.py:318
  251.7 13.5 %collective-permute-start.56 = (bf16[4,4,2,4096]{3,2,1,0:T(2,128)(2,1)S(1)}, bf16[4,4,2,4096]{3,2,1,0:T(2,128)(2,1)S(1)}, u32[]{:S(2)}, u32[]{:S(2)}) collective-permute-start(bf16[4,4,2,4096]{3,2,1,0:T(2,128)(2,1)S(1)} %get-tuple-element.137), channel_id=1, source_target_pairs={{0,12},{4,8},{8,4},{12,0},{16,28},{20,24},{24,20},{28,16},{1,13},{... | collective-permute-start | bytes 786440 | tf_op jit(solution)/shard_map/ppermute | solution.py:318
  257.5 28.7 %collective-permute-start.57 = (bf16[4,4,2,4096]{3,2,1,0:T(2,128)(2,1)S(1)}, bf16[4,4,2,4096]{3,2,1,0:T(2,128)(2,1)S(1)}, u32[]{:S(2)}, u32[]{:S(2)}) collective-permute-start(bf16[4,4,2,4096]{3,2,1,0:T(2,128)(2,1)S(1)} %get-tuple-element.138), channel_id=1, source_target_pairs={{0,16},{4,20},{8,24},{12,28},{16,0},{20,4},{24,8},{28,12},{1,17},{... | collective-permute-start | bytes 786440 | tf_op jit(solution)/shard_map/ppermute | solution.py:318
  259.7 37.7 %collective-permute-start.58 = (bf16[4,4,2,4096]{3,2,1,0:T(2,128)(2,1)S(1)}, bf16[4,4,2,4096]{3,2,1,0:T(2,128)(2,1)S(1)}, u32[]{:S(2)}, u32[]{:S(2)}) collective-permute-start(bf16[4,4,2,4096]{3,2,1,0:T(2,128)(2,1)S(1)} %get-tuple-element.139), channel_id=1, source_target_pairs={{0,20},{4,16},{8,28},{12,24},{16,4},{20,0},{24,12},{28,8},{1,21},{... | collective-permute-start | bytes 786440 | tf_op jit(solution)/shard_map/ppermute | solution.py:318
  264.2 44.5 %collective-permute-start.59 = (bf16[4,4,2,4096]{3,2,1,0:T(2,128)(2,1)S(1)}, bf16[4,4,2,4096]{3,2,1,0:T(2,128)(2,1)S(1)}, u32[]{:S(2)}, u32[]{:S(2)}) collective-permute-start(bf16[4,4,2,4096]{3,2,1,0:T(2,128)(2,1)S(1)} %get-tuple-element.140), channel_id=1, source_target_pairs={{0,24},{4,28},{8,16},{12,20},{16,8},{20,12},{24,0},{28,4},{1,25},{... | collective-permute-start | bytes 786440 | tf_op jit(solution)/shard_map/ppermute | solution.py:318
  264.2 50.1 %collective-permute-start.60 = (bf16[4,4,2,4096]{3,2,1,0:T(2,128)(2,1)S(1)}, bf16[4,4,2,4096]{3,2,1,0:T(2,128)(2,1)S(1)}, u32[]{:S(2)}, u32[]{:S(2)}) collective-permute-start(bf16[4,4,2,4096]{3,2,1,0:T(2,128)(2,1)S(1)} %get-tuple-element.141), channel_id=1, source_target_pairs={{0,28},{4,24},{8,20},{12,16},{16,12},{20,8},{24,4},{28,0},{1,29},{... | collective-permute-start | bytes 786440 | tf_op jit(solution)/shard_map/ppermute | solution.py:318
  265.3 53.1 %collective-permute-start.49 = (bf16[4,4,2,2048]{3,2,1,0:T(2,128)(2,1)}, bf16[4,4,2,2048]{3,2,1,0:T(2,128)(2,1)S(1)}, u32[]{:S(2)}, u32[]{:S(2)}) collective-permute-start(bf16[4,4,2,2048]{3,2,1,0:T(2,128)(2,1)} %get-tuple-element.128), channel_id=1, source_target_pairs={{0,12},{4,8},{8,4},{12,0},{16,28},{20,24},{24,20},{28,16},{1,13},{... | collective-permute-start | bytes 393224 | tf_op jit(solution)/shard_map/ppermute | solution.py:318
  286.2 32.2 %collective-permute-start.50 = (bf16[4,4,2,2048]{3,2,1,0:T(2,128)(2,1)}, bf16[4,4,2,2048]{3,2,1,0:T(2,128)(2,1)S(1)}, u32[]{:S(2)}, u32[]{:S(2)}) collective-permute-start(bf16[4,4,2,2048]{3,2,1,0:T(2,128)(2,1)} %get-tuple-element.129), channel_id=1, source_target_pairs={{0,16},{4,20},{8,24},{12,28},{16,0},{20,4},{24,8},{28,12},{1,17},{... | collective-permute-start | bytes 393224 | tf_op jit(solution)/shard_map/ppermute | solution.py:318
  297.5 21.0 %collective-permute-start.51 = (bf16[4,4,2,2048]{3,2,1,0:T(2,128)(2,1)S(1)}, bf16[4,4,2,2048]{3,2,1,0:T(2,128)(2,1)S(1)}, u32[]{:S(2)}, u32[]{:S(2)}) collective-permute-start(bf16[4,4,2,2048]{3,2,1,0:T(2,128)(2,1)S(1)} %get-tuple-element.130), channel_id=1, source_target_pairs={{0,20},{4,16},{8,28},{12,24},{16,4},{20,0},{24,12},{28,8},{1,21},{... | collective-permute-start | bytes 393224 | tf_op jit(solution)/shard_map/ppermute | solution.py:318
  308.7 11.2 %collective-permute-start.52 = (bf16[4,4,2,2048]{3,2,1,0:T(2,128)(2,1)S(1)}, bf16[4,4,2,2048]{3,2,1,0:T(2,128)(2,1)S(1)}, u32[]{:S(2)}, u32[]{:S(2)}) collective-permute-start(bf16[4,4,2,2048]{3,2,1,0:T(2,128)(2,1)S(1)} %get-tuple-element.131), channel_id=1, source_target_pairs={{0,24},{4,28},{8,16},{12,20},{16,8},{20,12},{24,0},{28,4},{1,25},{... | collective-permute-start | bytes 393224 | tf_op jit(solution)/shard_map/ppermute | solution.py:318
  (28 other events, 282.2 us)

commit v4 on v3

--- a/solution.py
+++ b/solution.py
@@ -16,13 +16,23 @@
 GROUPS = 2
 PER_GROUP = NF // GROUPS
 
-CHUNKS_IN = ((0, 0, 4), (1, 0, 4), (2, 0, 2), (2, 2, 2))
-CHUNKS_OUT = (2, 0, 1, 3)
+CHUNKS_IN = ((0, 0, 4), (1, 0, 4), (2, 0, 4))
+CHUNKS_OUT = (0, 1, 2)
 QUARTERS = 4
+EARLY = 0
 
 shift_rate = 0.61
-SMALL = 8 * 1024 * 1024
-BIG = 32 * 1024 * 1024
+MIB = 1024 * 1024
+
+
+def vmem(devices):
+    return (16 if devices <= 8 else 60) * MIB
+
+
+def turns(devices):
+    across = list(range(devices // 2, devices))
+    inside = list(range(1, devices // 2)) + [0]
+    return [0] + [t for pair in zip(across, inside) for t in pair][:-1]
 
 
 def hann_window():
@@ -41,7 +51,7 @@
 def band_table(freq_order, me, devices):
     basis = window_basis(freq_order).reshape(2, GROUPS, PER_GROUP, NFFT)
     basis = jnp.transpose(basis, (1, 0, 2, 3))
-    half_of = jnp.bitwise_xor(me, jnp.arange(devices, dtype=jnp.int32))
+    half_of = jnp.bitwise_xor(me, jnp.array(turns(devices), jnp.int32))
     block = jnp.arange(devices - 1, dtype=jnp.int32)
     first = (half_of[None, :] == block[:, None])[None, :, None, None, :, None]
     second = (half_of[None, :] == block[:, None] + 1)[None, :, None, None, :, None]
@@ -52,12 +62,13 @@
     return band.reshape(GROUPS, (devices - 1) * 2 * PER_GROUP, devices * HALF)
 
 
-def pick_kernel(count, comp, start, size, sub, me_ref, own_ref, *refs):
+def pick_kernel(wanted, comp, start, size, sub, me_ref, own_ref, *refs):
+    count = len(wanted)
     outs, sems = refs[-count - 1 : -1], refs[-1]
     me = me_ref[0]
     copies = []
-    for place in range(count):
-        there = pl.multiple_of(jnp.bitwise_xor(me, place + 1) * sub + start, 128)
+    for place, turn in enumerate(wanted):
+        there = pl.multiple_of(jnp.bitwise_xor(me, turn) * sub + start, 128)
         copies.append(
             pltpu.make_async_copy(own_ref.at[comp, :, pl.ds(there, size)], outs[place], sems.at[place])
         )
@@ -67,22 +78,23 @@
         copy.wait()
 
 
-def pick(me, own, after, devices, comp, start, size, sub):
-    count = devices - 1
-    return pl.pallas_call(
-        functools.partial(pick_kernel, count, comp, start, size, sub),
+def pick(me, own, after, devices, wanted, comp, start, size, sub):
+    count = len(wanted)
+    return pl.pallas_call(
+        functools.partial(pick_kernel, wanted, comp, start, size, sub),
         in_specs=[pl.BlockSpec(memory_space=pltpu.SMEM)] + [pl.BlockSpec(memory_space=pl.ANY)] * (1 + len(after)),
         out_specs=[pl.BlockSpec(memory_space=pltpu.VMEM)] * count,
         out_shape=[jax.ShapeDtypeStruct((own.shape[1], size), own.dtype)] * count,
         scratch_shapes=[pltpu.SemaphoreType.DMA((count,))],
-        compiler_params=pltpu.CompilerParams(vmem_limit_bytes=SMALL),
+        compiler_params=pltpu.CompilerParams(vmem_limit_bytes=vmem(devices)),
         name="pick",
     )(me, own, *after)
 
 
 def gather_kernel(count, me_ref, band_ref, fold_ref, weight_ref, own_ref, *refs):
     landed = refs[:count]
-    before_ref, spectra_ref, total_ref, sums = refs[count:]
+    before_ref, total_ref, sums = refs[count], refs[-2], refs[-1]
+    spectra_ref = refs[count + 1] if len(refs) > count + 3 else None
     step = pl.program_id(0)
 
     @pl.when(step == 0)
@@ -94,7 +106,8 @@
     for group in range(GROUPS):
         wide = jnp.dot(band_ref[group], data, preferred_element_type=jnp.float32)
         spectra = wide.astype(jnp.bfloat16)
-        spectra_ref[group] = spectra
+        if spectra_ref is not None:
+            spectra_ref[group] = spectra
         weighted = (spectra.astype(jnp.float32) * weight).astype(jnp.bfloat16)
         sums[group] += lax.dot_general(
             weighted, spectra, (((1,), (1,)), ((), ())), preferred_element_type=jnp.float32
@@ -112,8 +125,9 @@
             )
 
 
-def gather(me, band, fold, weights, own, landed, before, comp, start, size, sub, tile):
+def gather(me, band, fold, weights, own, landed, before, keep, comp, start, size, sub, tile):
     count = len(landed)
+    devices = count + 1
     half = own.shape[1]
     rows = band.shape[1]
     whole = lambda shape: pl.BlockSpec(shape, lambda g, m: (0,) * len(shape))
@@ -131,14 +145,15 @@
             ]
             + [pl.BlockSpec((half, tile), lambda g, m: (0, g))] * count
             + [whole(before.shape)],
-            out_specs=[pl.BlockSpec((GROUPS, rows, tile), lambda g, m: (0, 0, g)), whole(before.shape)],
+            out_specs=[pl.BlockSpec((GROUPS, rows, tile), lambda g, m: (0, 0, g))] * keep + [whole(before.shape)],
             scratch_shapes=[pltpu.VMEM((GROUPS, rows, rows), jnp.float32)],
         ),
         out_shape=[
             jax.ShapeDtypeStruct((GROUPS, rows, size), jnp.bfloat16),
-            jax.ShapeDtypeStruct(before.shape, jnp.float32),
-        ],
-        compiler_params=pltpu.CompilerParams(vmem_limit_bytes=BIG),
+        ]
+        * keep
+        + [jax.ShapeDtypeStruct(before.shape, jnp.float32)],
+        compiler_params=pltpu.CompilerParams(vmem_limit_bytes=vmem(devices)),
         cost_estimate=pl.CostEstimate(
             flops=2 * GROUPS * size * rows * (band.shape[2] + rows), bytes_accessed=2 * size * (2 * rows + 256), transcendentals=0
         ),
@@ -233,58 +248,192 @@
             jax.ShapeDtypeStruct((devices, freqs * MODES * 2, rows), jnp.bfloat16),
             jax.ShapeDtypeStruct((MODES, NF), jnp.float32),
         ],
-        compiler_params=pltpu.CompilerParams(vmem_limit_bytes=BIG),
+        compiler_params=pltpu.CompilerParams(vmem_limit_bytes=vmem(devices)),
         name="solve",
     )(me, scales, sums, start, tiles)
 
 
-def modes_kernel(after, me_ref, mix_ref, spectra_ref, *refs):
+def fetch_kernel(me_ref, spectra_ref, after_ref, out_ref, sem):
+    side = jnp.bitwise_xor(me_ref[0], 1)
+    copy = pltpu.make_async_copy(spectra_ref.at[pl.ds(side, 1)], out_ref, sem)
+    copy.start()
+    copy.wait()
+
+
+def fetch(side, spectra, after, devices):
+    return pl.pallas_call(
+        fetch_kernel,
+        in_specs=[pl.BlockSpec(memory_space=pltpu.SMEM)] + [pl.BlockSpec(memory_space=pl.ANY)] * 2,
+        out_specs=pl.BlockSpec(memory_space=pltpu.VMEM),
+        out_shape=jax.ShapeDtypeStruct((1,) + spectra.shape[1:], spectra.dtype),
+        scratch_shapes=[pltpu.SemaphoreType.DMA(())],
+        compiler_params=pltpu.CompilerParams(vmem_limit_bytes=vmem(devices)),
+        name="fetch",
+    )(side, spectra, after)
+
+
+def modes_kernel(after, sides, me_ref, mix_ref, spectra_ref, *refs):
     outs = refs[after:]
     devices = mix_ref.shape[0]
     part = devices // GROUPS
     freqs = outs[0].shape[0]
     per = freqs * MODES * 2
-    side = me_ref[0] // part
-    for h in range(GROUPS):
-        mix = mix_ref[h * part : (h + 1) * part].reshape(part * per, mix_ref.shape[2])
-        wide = jnp.dot(mix, spectra_ref[jnp.bitwise_xor(side, h)], preferred_element_type=jnp.float32)
+    mine = me_ref[0] // part
+    for number, side in enumerate(sides):
+        mix = mix_ref[side * part : (side + 1) * part].reshape(part * per, mix_ref.shape[2])
+        group = jnp.bitwise_xor(mine, side) if len(sides) > 1 else 0
+        wide = jnp.dot(mix, spectra_ref[group], preferred_element_type=jnp.float32)
         for near in range(part):
-            out = outs[h * part + near]
-            for f in range(freqs):
-                for k in range(MODES):
-                    place = near * per + 2 * (f * MODES + k)
-                    out[f, k] = wide[place : place + 2].astype(out.dtype)
-
-
-def modes_of(me, mix, spectra, after, devices, tile):
+            split_rows(wide[near * per : (near + 1) * per], outs[number * part + near])
+
+
+def split_rows(wide, out):
+    freqs, modes = out.shape[:2]
+    for f in range(freqs):
+        for k in range(modes):
+            place = 2 * (f * modes + k)
+            out[f, k] = wide[place : place + 2].astype(out.dtype)
+
+
+def modes_of(me, mix, spectra, after, devices, sides, skip, tile):
     freqs = NF // devices
+    part = devices // GROUPS
     groups, rows, size = spectra.shape
-    return pl.pallas_call(
-        functools.partial(modes_kernel, len(after)),
+    count = part * len(sides)
+    if groups == 1:
+        source = pl.BlockSpec((1, rows, tile), lambda g, m: (0, 0, skip // tile + g))
+    elif len(sides) == 1:
+        source = pl.BlockSpec(
+            (1, rows, tile), lambda g, m: (jnp.bitwise_xor(m[0] // part, sides[0]), 0, skip // tile + g)
+        )
+    else:
+        source = pl.BlockSpec((groups, rows, tile), lambda g, m: (0, 0, skip // tile + g))
+    made = pl.pallas_call(
+        functools.partial(modes_kernel, len(after), sides),
+        grid_spec=pltpu.PrefetchScalarGridSpec(
+            num_scalar_prefetch=1,
+            grid=((size - skip) // tile,),
+            in_specs=[
+                pl.BlockSpec(mix.shape, lambda g, m: (0, 0, 0)),
+                source,
+            ]
+            + [pl.BlockSpec(memory_space=pl.ANY)] * len(after),
+            out_specs=[pl.BlockSpec((freqs, MODES, 2, tile), lambda g, m: (0, 0, 0, g))] * count,
+        ),
+        out_shape=[jax.ShapeDtypeStruct((freqs, MODES, 2, size - skip), jnp.bfloat16)] * count,
+        compiler_params=pltpu.CompilerParams(vmem_limit_bytes=vmem(devices)),
+        name="modes",
+    )(me, mix, spectra, *after)
+    return {side * part + near: made[n * part + near] for n, side in enumerate(sides) for near in range(part)}
+
+
+def again_kernel(count, after, me_ref, band_ref, mix_ref, own_ref, *refs):
+    landed, outs = refs[:count], refs[count + after :]
+    devices = mix_ref.shape[0]
+    part = devices // GROUPS
+    freqs = outs[0].shape[0]
+    per = freqs * MODES * 2
+    mine = me_ref[0] // part
+    data = jnp.concatenate([own_ref[0]] + [ref[...] for ref in landed], 0)
+    for side in (0, 1):
+        band = band_ref[jnp.bitwise_xor(mine, side)]
+        spectra = jnp.dot(band, data, preferred_element_type=jnp.float32).astype(jnp.bfloat16)
+        mix = mix_ref[side * part : (side + 1) * part].reshape(part * per, mix_ref.shape[2])
+        wide = jnp.dot(mix, spectra, preferred_element_type=jnp.float32)
+        for near in range(part):
+            split_rows(wide[near * per : (near + 1) * per], outs[side * part + near])
+
+
+def modes_again(me, band, mix, own, landed, after, devices, comp, start, size, sub, tile):
+    freqs = NF // devices
+    count = len(landed)
+    half = own.shape[1]
+    made = pl.pallas_call(
+        functools.partial(again_kernel, count, len(after)),
         grid_spec=pltpu.PrefetchScalarGridSpec(
             num_scalar_prefetch=1,
             grid=(size // tile,),
             in_specs=[
+                pl.BlockSpec(band.shape, lambda g, m: (0, 0, 0)),
                 pl.BlockSpec(mix.shape, lambda g, m: (0, 0, 0)),
-                pl.BlockSpec((groups, rows, tile), lambda g, m: (0, 0, g)),
+                pl.BlockSpec((1, half, tile), lambda g, m: (comp, 0, m[0] * (sub // tile) + start // tile + g)),
             ]
+            + [pl.BlockSpec((half, tile), lambda g, m: (0, g))] * count
             + [pl.BlockSpec(memory_space=pl.ANY)] * len(after),
             out_specs=[pl.BlockSpec((freqs, MODES, 2, tile), lambda g, m: (0, 0, 0, g))] * devices,
         ),
         out_shape=[jax.ShapeDtypeStruct((freqs, MODES, 2, size), jnp.bfloat16)] * devices,
-        compiler_params=pltpu.CompilerParams(vmem_limit_bytes=BIG),
-        name="modes",
-    )(me, mix, spectra, *after)
-
-
-def place_kernel(count, comp, start, size, sub, me_ref, *refs):
+        compiler_params=pltpu.CompilerParams(vmem_limit_bytes=vmem(devices)),
+        name="again",
+    )(me, band, mix, own, *landed, *after)
+    return dict(enumerate(made))
+
+
+def choose_kernel(me_ref, table_ref, spectra_ref, after_ref, *outs):
+    part = len(outs)
+    other = jnp.bitwise_xor(me_ref[0] // part, 1)
+    for near, out in enumerate(outs):
+        out[...] = jnp.dot(table_ref[near], spectra_ref[other], preferred_element_type=jnp.float32).astype(out.dtype)
+
+
+def choose(me, table, spectra, after, devices, size, tile):
+    groups, rows, _ = spectra.shape
+    part = devices // GROUPS
+    return pl.pallas_call(
+        choose_kernel,
+        grid_spec=pltpu.PrefetchScalarGridSpec(
+            num_scalar_prefetch=1,
+            grid=(size // tile,),
+            in_specs=[
+                pl.BlockSpec(table.shape, lambda g, m: (0, 0, 0)),
+                pl.BlockSpec((groups, rows, tile), lambda g, m: (0, 0, g)),
+                pl.BlockSpec(memory_space=pl.ANY),
+            ],
+            out_specs=[pl.BlockSpec((table.shape[1], tile), lambda g, m: (0, g))] * part,
+        ),
+        out_shape=[jax.ShapeDtypeStruct((table.shape[1], size), jnp.bfloat16)] * part,
+        compiler_params=pltpu.CompilerParams(vmem_limit_bytes=vmem(devices)),
+        name="choose",
+    )(me, table, spectra, after)
+
+
+def finish_kernel(count, mix_ref, table_ref, *refs):
+    mix = lax.dot_general(
+        mix_ref[0], table_ref[...], (((1,), (1,)), ((), ())), preferred_element_type=jnp.float32
+    ).astype(jnp.bfloat16)
+    for landed, out in zip(refs[:count], refs[count:]):
+        split_rows(jnp.dot(mix, landed[...], preferred_element_type=jnp.float32), out)
+
+
+def finish(mix, table, landed, devices, freqs, tile):
+    count = len(landed)
+    rows, size = landed[0].shape
+    return pl.pallas_call(
+        functools.partial(finish_kernel, count),
+        grid=(size // tile,),
+        in_specs=[
+            pl.BlockSpec((1,) + mix.shape[1:], lambda g: (0, 0, 0)),
+            pl.BlockSpec(table.shape, lambda g: (0, 0)),
+        ]
+        + [pl.BlockSpec((rows, tile), lambda g: (0, g))] * count,
+        out_specs=[pl.BlockSpec((freqs, MODES, 2, tile), lambda g: (0, 0, 0, g))] * count,
+        out_shape=[jax.ShapeDtypeStruct((freqs, MODES, 2, size), jnp.bfloat16)] * count,
+        compiler_params=pltpu.CompilerParams(vmem_limit_bytes=vmem(devices)),
+        name="finish",
+    )(mix, table, *landed)
+
+
+def place_kernel(spots, comp, sub, me_ref, *refs):
+    count = len(spots)
     pieces, out_ref, sems = refs[:count], refs[-2], refs[-1]
     me = me_ref[0]
     copies = []
-    for place in range(count):
-        there = pl.multiple_of(jnp.bitwise_xor(me, place) * sub + start, 128)
+    for n, (turn, start) in enumerate(spots):
+        there = pl.multiple_of(jnp.bitwise_xor(me, turn) * sub + start, 128)
         copies.append(
-            pltpu.make_async_copy(pieces[place], out_ref.at[:, :, comp, :, pl.ds(there, size)], sems.at[place])
+            pltpu.make_async_copy(
+                pieces[n], out_ref.at[:, :, comp, :, pl.ds(there, pieces[n].shape[3])], sems.at[n]
+            )
         )
     for copy in copies:
         copy.start()
@@ -292,11 +441,12 @@
         copy.wait()
 
 
-def place(me, pieces, out, comp, start, size, sub, shape):
+def place(me, pieces, out, devices, comp, sub, shape):
+    arrays = [piece[0] for piece in pieces]
     count = len(pieces)
     more = [] if out is None else [out]
     return pl.pallas_call(
-        functools.partial(place_kernel, count, comp, start, size, sub),
+        functools.partial(place_kernel, [piece[1:] for piece in pieces], comp, sub),
         in_specs=[pl.BlockSpec(memory_space=pltpu.SMEM)]
         + [pl.BlockSpec(memory_space=pltpu.VMEM)] * count
         + [pl.BlockSpec(memory_space=pl.ANY)] * len(more),
@@ -304,19 +454,17 @@
         out_shape=jax.ShapeDtypeStruct(shape, jnp.bfloat16),
         input_output_aliases={count + 1: 0} if more else {},
         scratch_shapes=[pltpu.SemaphoreType.DMA((count,))],
-        compiler_params=pltpu.CompilerParams(vmem_limit_bytes=SMALL),
+        compiler_params=pltpu.CompilerParams(vmem_limit_bytes=vmem(devices)),
         name="place",
-    )(me, *pieces, *more)
+    )(me, *arrays, *more)
+
+
+def send(value, turn, devices):
+    return lax.ppermute(value, "tm", [(d, d ^ turn) for d in range(devices)])
 
 
 def exchange(pieces, devices):
-    landed = [None] * (devices - 1)
-    across = list(range(devices // 2, devices))
-    inside = list(range(1, devices // 2)) + [0]
-    for step in [s for pair in zip(across, inside) for s in pair]:
-        if step:
-            landed[step - 1] = lax.ppermute(pieces[step - 1], "tm", [(d, d ^ step) for d in range(devices)])
-    return landed
+    return [send(piece, turn, devices) for piece, turn in zip(pieces, turns(devices)[1:])]
 
 
 def sum_over(value, axis):
@@ -365,21 +513,58 @@
     history = []
     for comp, first, length in CHUNKS_IN:
         start, size = first * unit, length * unit
-        pieces = pick(me, own, history[-2:-1], devices, comp, start, size, sub)
+        order = turns(devices)[1:]
+        cut = 0 if history else 1
+        pieces = []
+        for wanted in (order[:cut], order[cut:]):
+            if wanted:
+                pieces += pick(me, own, history[-2:-1], devices, wanted, comp, start, size, sub)
         landed = exchange(pieces, devices)
-        made, sums = gather(me, band, fold, weights, own, landed, sums, comp, start, size, sub, unit)
-        spectra.append(made)
+        keep = len(history) < len(CHUNKS_IN) - 1
+        *made, sums = gather(me, band, fold, weights, own, landed, sums, keep, comp, start, size, sub, unit if keep else 4 * unit)
+        spectra += made
         history.append(sums)
-    sums = sum_over(sum_over(sums, "space"), "tm")
+    part = devices // GROUPS
+    early = EARLY * unit // 2
+    lines = jnp.arange(blocks * 2 * freqs, dtype=jnp.int32)
+    near = jnp.bitwise_xor(index.astype(jnp.int32), jnp.arange(part, dtype=jnp.int32)) % part
+    same_part = (lines // freqs)[:, None] == (line // PER_GROUP)[None, :]
+    wanted = (near[:, None] * freqs + lines % freqs)[:, :, None] == (line % PER_GROUP)[None, None, :]
+    table = (same_part[None] & wanted).astype(jnp.bfloat16)
+    crossed = []
+    if early:
+        chosen = choose(me, table, spectra[0], history[-2], devices, early, unit // 2)
+        crossed = [send(value, part + n, devices) for n, value in enumerate(chosen)]
+
+    sums = sum_over(sums, "space")
+    ready = fetch(me // part, spectra[0], sums, devices)
+    sums = sum_over(sums, "tm")
     mix, energies = solve(me, scales, sums, start_table, tiles, devices)
     placed = [None]
     shape = (freqs, MODES, comps, 2, cells)
     for chunk in CHUNKS_OUT:
         comp, first, length = CHUNKS_IN[chunk]
         after = [] if len(placed) < 3 else placed[-2:-1]
-        made = modes_of(me, mix, spectra[chunk], after, devices, unit)
-        landed = [made[0]] + exchange(made[1:], devices)
-        placed.append(place(me, landed, placed[-1], comp, first * unit, length * unit, sub, shape))
+        pieces = []
+        if chunk == 0:
+            made = modes_of(me, mix, ready, after, devices, (1,), early, 4 * unit)
+            made.update(modes_of(me, mix, spectra[0], after, devices, (0,), 0, unit))
+        elif chunk == len(CHUNKS_IN) - 1:
+            made = modes_again(
+                me, band, mix, own, landed, after, devices, comp, first * unit, length * unit, sub, unit
+            )
+        else:
+            made = modes_of(me, mix, spectra[chunk], after, devices, (0, 1), 0, unit)
+        for turn in turns(devices):
+            skip = early if chunk == 0 and turn >= part else 0
+            value = send(made[turn], turn, devices) if turn else made[turn]
+            pieces.append((value, turn, first * unit + skip))
+        if chunk == 0 and early:
+            late = finish(mix, table[0], crossed, devices, freqs, unit // 2)
+            pieces += [(value, part + n, first * unit) for n, value in enumerate(late)]
+        soon = pieces[:5] if chunk == CHUNKS_OUT[-1] else []
+        done = place(me, soon, placed[-1], devices, comp, sub, shape) if soon else placed[-1]
+        placed.append(place(me, pieces[len(soon) :], done, devices, comp, sub, shape))
     mine = lax.dynamic_slice_in_dim(energies, index * freqs, freqs, 1)
     return (jnp.transpose(mine), jnp.transpose(placed[-1], (0, 1, 3, 2, 4)))
 

time: 324 us -> 302 us (0.932)
  waiting for transfers between devices: 171 us -> 154 us
  local copies, waits for them, and re-layouts: 37.1 us -> 27.8 us
  starting transfers between devices: 80.9 us -> 87.9 us
    ppermute x56 -> x42, waiting for transfers between devices: 159 us -> 145 us  [send(): return lax.ppermute(value, 'tm', [(d, d ^ turn) for d in range(devices)])]
    ppermute x56 -> x42, starting transfers between devices: 77.2 us -> 83.5 us  [send(): return lax.ppermute(value, 'tm', [(d, d ^ turn) for d in range(devices)])]
    broadcast_in_dim x8, local copies, waits for them, and re-layouts: 14.9 us -> 9.46 us  [band_table(): band = jnp.where(first, low, jnp.where(second, high, nothing))]
    unnamed x31 -> x35, local copies, waits for them, and re-layouts: 21.3 us -> 18 us
    pallas_call x4 -> x3, Pallas kernels: 13.1 us -> 11 us  [gather(): pl.pallas_call(functools.partial(gather_kernel, count), grid_spec=pltpu.P...]
    pallas_call x12 -> x13, Pallas kernels: 14 us -> 14.7 us  [the longest x4 5.76 us: place(): pl.pallas_call(functools.partial(place_kernel, [piece[1:] for piece in pi...]
  transfers between devices with their start and end apart: 61 -> 47, of which waited for: 32 -> 25; matrix products, arithmetic and copies ran while one was open for 6% -> 4% of each run, Pallas kernels for 7% -> 7%
where the time goes in v4:
time: 302 us; the launch traced here: 301 us
  waiting for transfers between devices  154 us (51%)
  starting transfers between devices  87.9 us (29%)
  local copies, waits for them, and re-layouts  27.8 us (9%)
  Pallas kernels  27 us (9%)
    ppermute x42, waiting for transfers between devices, send(): return lax.ppermute(value, 'tm', [(d, d ^ turn) for d in range(devices)])  145 us
    ppermute x42, starting transfers between devices, send(): return lax.ppermute(value, 'tm', [(d, d ^ turn) for d in range(devices)])  83.5 us
    unnamed x35, local copies, waits for them, and re-layouts  18 us
    pallas_call x3, Pallas kernels, gather(): pl.pallas_call(functools.partial(gather_kernel, count), grid_spec=pltpu.P...  11 us
    broadcast_in_dim x8, local copies, waits for them, and re-layouts, band_table(): band = jnp.where(first, low, jnp.where(second, high, nothing))  9.46 us
    ppermute x5, waiting for transfers between devices, sum_over(): lax.ppermute(value, axis, [(d, d ^ step) for d in range(count)])  8.89 us
  transfers between devices with their start and end apart: 47, of which 25 were waited for; matrix products, arithmetic and copies ran while one was open for 4% of the time, Pallas kernels for 7%

profile of v4, /device:TPU:8, one launch (start us, length us, event | category | flops | bytes accessed | tf_op | source)
XLA Modules:
  0.0 301.1 jit_solution(9170964956351724514)
XLA Ops:
  0.6 2.8 copy-done
  3.5 2.7 collective-permute-start
  8.3 3.0 collective-permute-start.4
  12.9 2.5 broadcast_in_dim.94
  16.5 2.5 broadcast_in_dim.99
  23.8 3.6 %collective-permute-start.5 = (bf16[32,4096]{1,0:T(8,128)(2,1)S(1)}, bf16[32,4096]{1,0:T(8,128)(2,1)S(1)}, u32[]{:S(2)}, u32[]{:S(2)}) collective-permute-start(bf16[32,4096]{1,0:T(8,128)(2,1)S(1)} %get-tuple-element.56), channel_id=1, source_target_pairs={{0,12},{4,8},{8,4},{12,0},{16,28},{20,24},{24,20},{28,16},{1,13},{... | collective-permute-start | bytes 786440 | tf_op jit(solution)/shard_map/ppermute | solution.py:463
  27.3 2.8 copy-done.1
  32.0 3.1 %collective-permute-done.2.refs_2_ = bf16[32,4096]{1,0:T(8,128)(2,1)S(1)} collective-permute-done((bf16[32,4096]{1,0:T(8,128)(2,1)S(1)}, bf16[32,4096]{1,0:T(8,128)(2,1)S(1)}, u32[]{:S(2)}, u32[]{:S(2)}) %collective-permute-start.2) | collective-permute-done | bytes 262176 | tf_op jit(solution)/shard_map/ppermute | solution.py:463
  35.0 4.6 %collective-permute-start.14 = (bf16[32,4096]{1,0:T(8,128)(2,1)S(1)}, bf16[32,4096]{1,0:T(8,128)(2,1)S(1)}, u32[]{:S(2)}, u32[]{:S(2)}) collective-permute-start(bf16[32,4096]{1,0:T(8,128)(2,1)S(1)} %get-tuple-element.66), channel_id=1, source_target_pairs={{0,16},{4,20},{8,24},{12,28},{16,0},{20,4},{24,8},{28,12},{1,17},{... | collective-permute-start | bytes 786440 | tf_op jit(solution)/shard_map/ppermute | solution.py:463
  40.2 11.4 %collective-permute-done.4.refs_4_ = bf16[32,4096]{1,0:T(8,128)(2,1)S(1)} collective-permute-done((bf16[32,4096]{1,0:T(8,128)(2,1)S(1)}, bf16[32,4096]{1,0:T(8,128)(2,1)S(1)}, u32[]{:S(2)}, u32[]{:S(2)}) %collective-permute-start.4) | collective-permute-done | bytes 262176 | tf_op jit(solution)/shard_map/ppermute | solution.py:463
  51.6 4.3 %collective-permute-start.17 = (bf16[32,4096]{1,0:T(8,128)(2,1)S(1)}, bf16[32,4096]{1,0:T(8,128)(2,1)S(1)}, u32[]{:S(2)}, u32[]{:S(2)}) collective-permute-start(bf16[32,4096]{1,0:T(8,128)(2,1)S(1)} %get-tuple-element.69), channel_id=1, source_target_pairs={{0,8},{4,12},{8,0},{12,4},{16,24},{20,28},{24,16},{28,20},{1,9},{5... | collective-permute-start | bytes 786440 | tf_op jit(solution)/shard_map/ppermute | solution.py:463
  55.9 8.2 %collective-permute-done.6.refs_6_ = bf16[32,4096]{1,0:T(8,128)(2,1)S(1)} collective-permute-done((bf16[32,4096]{1,0:T(8,128)(2,1)S(1)}, bf16[32,4096]{1,0:T(8,128)(2,1)S(1)}, u32[]{:S(2)}, u32[]{:S(2)}) %collective-permute-start.6) | collective-permute-done | bytes 262176 | tf_op jit(solution)/shard_map/ppermute | solution.py:463
  65.7 4.2 %gather.3 = (bf16[2,224,4096]{2,1,0:T(8,128)(2,1)S(1)}, f32[2,16,224]{2,1,0:T(8,128)S(1)}) custom-call(s32[1]{0:T(128)} %bitcast.me_ref, bf16[2,224,256]{2,1,0:T(8,128)(2,1)S(1)} %select_select_fusion.band_ref, f32[16,224]{1,0:T(8,128)S(1)} %fusion.6.fold_ref, f32[1,32768]{1,0:T(1,128)S(1)} %bitcast.29, bf16[3,32,32768]{2,1,0:T(8,128)(2,1)S(1)} %bitcast.21, ...), custom_call_target="tpu_custom_call" | custom-call | flops 1761607680 | bytes 5767168 | tf_op jit(solution)/shard_map/gather/pallas_call | solution.py:135
  73.5 3.3 %collective-permute-start.19 = (bf16[32,4096]{1,0:T(8,128)(2,1)S(1)}, bf16[32,4096]{1,0:T(8,128)(2,1)S(1)}, u32[]{:S(2)}, u32[]{:S(2)}) collective-permute-start(bf16[32,4096]{1,0:T(8,128)(2,1)S(1)} %get-tuple-element.71), channel_id=1, source_target_pairs={{0,12},{4,8},{8,4},{12,0},{16,28},{20,24},{24,20},{28,16},{1,13},{... | collective-permute-start | bytes 786440 | tf_op jit(solution)/shard_map/ppermute | solution.py:463
  79.2 4.4 %collective-permute-start.7 = (bf16[32,4096]{1,0:T(8,128)(2,1)S(1)}, bf16[32,4096]{1,0:T(8,128)(2,1)S(1)}, u32[]{:S(2)}, u32[]{:S(2)}) collective-permute-start(bf16[32,4096]{1,0:T(8,128)(2,1)S(1)} %get-tuple-element.59), channel_id=1, source_target_pairs={{0,16},{4,20},{8,24},{12,28},{16,0},{20,4},{24,8},{28,12},{1,17},{... | collective-permute-start | bytes 786440 | tf_op jit(solution)/shard_map/ppermute | solution.py:463
  84.0 12.6 %collective-permute-done.18.refs_4_ = bf16[32,4096]{1,0:T(8,128)(2,1)S(1)} collective-permute-done((bf16[32,4096]{1,0:T(8,128)(2,1)S(1)}, bf16[32,4096]{1,0:T(8,128)(2,1)S(1)}, u32[]{:S(2)}, u32[]{:S(2)}) %collective-permute-start.18) | collective-permute-done | bytes 262176 | tf_op jit(solution)/shard_map/ppermute | solution.py:463
  96.6 4.3 %collective-permute-start.10 = (bf16[32,4096]{1,0:T(8,128)(2,1)S(1)}, bf16[32,4096]{1,0:T(8,128)(2,1)S(1)}, u32[]{:S(2)}, u32[]{:S(2)}) collective-permute-start(bf16[32,4096]{1,0:T(8,128)(2,1)S(1)} %get-tuple-element.62), channel_id=1, source_target_pairs={{0,8},{4,12},{8,0},{12,4},{16,24},{20,28},{24,16},{28,20},{1,9},{5... | collective-permute-start | bytes 786440 | tf_op jit(solution)/shard_map/ppermute | solution.py:463
  100.9 8.2 %collective-permute-done.20.refs_6_ = bf16[32,4096]{1,0:T(8,128)(2,1)S(1)} collective-permute-done((bf16[32,4096]{1,0:T(8,128)(2,1)S(1)}, bf16[32,4096]{1,0:T(8,128)(2,1)S(1)}, u32[]{:S(2)}, u32[]{:S(2)}) %collective-permute-start.20) | collective-permute-done | bytes 262176 | tf_op jit(solution)/shard_map/ppermute | solution.py:463
  110.7 7.8 %collective-permute-done.7.refs_0_ = bf16[32,4096]{1,0:T(8,128)(2,1)S(1)} collective-permute-done((bf16[32,4096]{1,0:T(8,128)(2,1)S(1)}, bf16[32,4096]{1,0:T(8,128)(2,1)S(1)}, u32[]{:S(2)}, u32[]{:S(2)}) %collective-permute-start.7) | collective-permute-done | bytes 262176 | tf_op jit(solution)/shard_map/ppermute | solution.py:463
  118.5 3.3 %collective-permute-start.12 = (bf16[32,4096]{1,0:T(8,128)(2,1)S(1)}, bf16[32,4096]{1,0:T(8,128)(2,1)S(1)}, u32[]{:S(2)}, u32[]{:S(2)}) collective-permute-start(bf16[32,4096]{1,0:T(8,128)(2,1)S(1)} %get-tuple-element.64), channel_id=1, source_target_pairs={{0,12},{4,8},{8,4},{12,0},{16,28},{20,24},{24,20},{28,16},{1,13},{... | collective-permute-start | bytes 786440 | tf_op jit(solution)/shard_map/ppermute | solution.py:463
  123.3 4.2 %gather.4 = (bf16[2,224,4096]{2,1,0:T(8,128)(2,1)S(1)}, f32[2,16,224]{2,1,0:T(8,128)S(1)}) custom-call(s32[1]{0:T(128)} %bitcast.me_ref, bf16[2,224,256]{2,1,0:T(8,128)(2,1)S(1)} %select_select_fusion.band_ref, f32[16,224]{1,0:T(8,128)S(1)} %fusion.6.fold_ref, f32[1,32768]{1,0:T(1,128)S(1)} %bitcast.30, bf16[3,32,32768]{2,1,0:T(8,128)(2,1)S(1)} %bitcast.23, ...), custom_call_target="tpu_custom_call" | custom-call | flops 1761607680 | bytes 5767168 | tf_op jit(solution)/shard_map/gather/pallas_call | solution.py:135
  129.4 6.6 %collective-permute-done.11.refs_4_ = bf16[32,4096]{1,0:T(8,128)(2,1)S(1)} collective-permute-done((bf16[32,4096]{1,0:T(8,128)(2,1)S(1)}, bf16[32,4096]{1,0:T(8,128)(2,1)S(1)}, u32[]{:S(2)}, u32[]{:S(2)}) %collective-permute-start.11) | collective-permute-done | bytes 262176 | tf_op jit(solution)/shard_map/ppermute | solution.py:463
  136.0 5.8 %collective-permute-done.13.refs_6_ = bf16[32,4096]{1,0:T(8,128)(2,1)S(1)} collective-permute-done((bf16[32,4096]{1,0:T(8,128)(2,1)S(1)}, bf16[32,4096]{1,0:T(8,128)(2,1)S(1)}, u32[]{:S(2)}, u32[]{:S(2)}) %collective-permute-start.13) | collective-permute-done | bytes 262176 | tf_op jit(solution)/shard_map/ppermute | solution.py:463
  141.7 2.6 gather.5
  147.0 2.4 collective-permute-done.22
  150.2 3.1 %collective-permute-done.23 = f32[2,16,224]{2,1,0:T(8,128)S(1)} collective-permute-done((f32[2,16,224]{2,1,0:T(8,128)S(1)}, f32[2,16,224]{2,1,0:T(8,128)S(1)}, u32[]{:S(2)}, u32[]{:S(2)}) %collective-permute-start.23) | collective-permute-done | bytes 28704 | tf_op jit(solution)/shard_map/ppermute | solution.py:474
  157.3 2.3 collective-permute-start.25
  159.6 2.0 copy-done.4
  163.9 2.3 collective-permute-start.26
  172.7 11.1 %collective-permute-done.26.refs_1_ = bf16[4,4,2,4096]{3,2,1,0:T(2,128)(2,1)S(1)} collective-permute-done((bf16[4,4,2,4096]{3,2,1,0:T(2,128)(2,1)S(1)}, bf16[4,4,2,4096]{3,2,1,0:T(2,128)(2,1)S(1)}, u32[]{:S(2)}, u32[]{:S(2)}) %collective-permute-start.26) | collective-permute-done | bytes 262176 | tf_op jit(solution)/shard_map/ppermute | solution.py:463
  183.8 3.0 %collective-permute-start.31 = (bf16[4,4,2,4096]{3,2,1,0:T(2,128)(2,1)S(1)}, bf16[4,4,2,4096]{3,2,1,0:T(2,128)(2,1)S(1)}, u32[]{:S(2)}, u32[]{:S(2)}) collective-permute-start(bf16[4,4,2,4096]{3,2,1,0:T(2,128)(2,1)S(1)} %get-tuple-element.83), channel_id=1, source_target_pairs={{0,12},{4,8},{8,4},{12,0},{16,28},{20,24},{24,20},{28,16},{1,13},{... | collective-permute-start | bytes 786440 | tf_op jit(solution)/shard_map/ppermute | solution.py:463
  186.9 1.9 collective-permute-start.32
  190.7 5.8 %collective-permute-done.28.refs_3_ = bf16[4,4,2,4096]{3,2,1,0:T(2,128)(2,1)S(1)} collective-permute-done((bf16[4,4,2,4096]{3,2,1,0:T(2,128)(2,1)S(1)}, bf16[4,4,2,4096]{3,2,1,0:T(2,128)(2,1)S(1)}, u32[]{:S(2)}, u32[]{:S(2)}) %collective-permute-start.28) | collective-permute-done | bytes 262176 | tf_op jit(solution)/shard_map/ppermute | solution.py:463
  196.4 7.7 %collective-permute-start.40 = (bf16[4,4,2,4096]{3,2,1,0:T(2,128)(2,1)S(1)}, bf16[4,4,2,4096]{3,2,1,0:T(2,128)(2,1)S(1)}, u32[]{:S(2)}, u32[]{:S(2)}) collective-permute-start(bf16[4,4,2,4096]{3,2,1,0:T(2,128)(2,1)S(1)} %get-tuple-element.95), channel_id=1, source_target_pairs={{0,16},{4,20},{8,24},{12,28},{16,0},{20,4},{24,8},{28,12},{1,17},{... | collective-permute-start | bytes 786440 | tf_op jit(solution)/shard_map/ppermute | solution.py:463
  204.1 4.3 %collective-permute-start.41 = (bf16[4,4,2,4096]{3,2,1,0:T(2,128)(2,1)S(1)}, bf16[4,4,2,4096]{3,2,1,0:T(2,128)(2,1)S(1)}, u32[]{:S(2)}, u32[]{:S(2)}) collective-permute-start(bf16[4,4,2,4096]{3,2,1,0:T(2,128)(2,1)S(1)} %get-tuple-element.96), channel_id=1, source_target_pairs={{0,4},{4,0},{8,12},{12,8},{16,20},{20,16},{24,28},{28,24},{1,5},{5... | collective-permute-start | bytes 786440 | tf_op jit(solution)/shard_map/ppermute | solution.py:463
  208.4 5.1 %collective-permute-done.30.refs_5_ = bf16[4,4,2,4096]{3,2,1,0:T(2,128)(2,1)S(1)} collective-permute-done((bf16[4,4,2,4096]{3,2,1,0:T(2,128)(2,1)S(1)}, bf16[4,4,2,4096]{3,2,1,0:T(2,128)(2,1)S(1)}, u32[]{:S(2)}, u32[]{:S(2)}) %collective-permute-start.30) | collective-permute-done | bytes 262176 | tf_op jit(solution)/shard_map/ppermute | solution.py:463
  213.5 12.5 %collective-permute-done.32.refs_7_ = bf16[4,4,2,4096]{3,2,1,0:T(2,128)(2,1)S(1)} collective-permute-done((bf16[4,4,2,4096]{3,2,1,0:T(2,128)(2,1)S(1)}, bf16[4,4,2,4096]{3,2,1,0:T(2,128)(2,1)S(1)}, u32[]{:S(2)}, u32[]{:S(2)}) %collective-permute-start.32) | collective-permute-done | bytes 262176 | tf_op jit(solution)/shard_map/ppermute | solution.py:463
  229.5 2.8 copy-done.2
  232.2 4.5 %again.1 = (bf16[4,4,2,4096]{3,2,1,0:T(2,128)(2,1)S(1)}, bf16[4,4,2,4096]{3,2,1,0:T(2,128)(2,1)S(1)}, bf16[4,4,2,4096]{3,2,1,0:T(2,128)(2,1)}, bf16[4,4,2,4096]{...) custom-call(s32[1]{0:T(128)} %bitcast.me_ref, ...), custom_call_target="tpu_custom_call" | custom-call | tf_op jit(solution)/shard_map/again/pallas_call | solution.py:351
  237.4 3.4 %collective-permute-start.46 = (bf16[4,4,2,4096]{3,2,1,0:T(2,128)(2,1)S(1)}, bf16[4,4,2,4096]{3,2,1,0:T(2,128)(2,1)S(1)}, u32[]{:S(2)}, u32[]{:S(2)}) collective-permute-start(bf16[4,4,2,4096]{3,2,1,0:T(2,128)(2,1)S(1)} %get-tuple-element.101), channel_id=1, source_target_pairs={{0,28},{4,24},{8,20},{12,16},{16,12},{20,8},{24,4},{28,0},{1,29},{... | collective-permute-start | bytes 786440 | tf_op jit(solution)/shard_map/ppermute | solution.py:463
  242.7 2.9 collective-permute-start.37
  245.6 18.5 %collective-permute-done.44.refs_5_ = bf16[4,4,2,4096]{3,2,1,0:T(2,128)(2,1)S(1)} collective-permute-done((bf16[4,4,2,4096]{3,2,1,0:T(2,128)(2,1)S(1)}, bf16[4,4,2,4096]{3,2,1,0:T(2,128)(2,1)S(1)}, u32[]{:S(2)}, u32[]{:S(2)}) %collective-permute-start.44) | collective-permute-done | bytes 262176 | tf_op jit(solution)/shard_map/ppermute | solution.py:463
  265.8 3.9 %collective-permute-done.46.refs_7_ = bf16[4,4,2,4096]{3,2,1,0:T(2,128)(2,1)S(1)} collective-permute-done((bf16[4,4,2,4096]{3,2,1,0:T(2,128)(2,1)S(1)}, bf16[4,4,2,4096]{3,2,1,0:T(2,128)(2,1)S(1)}, u32[]{:S(2)}, u32[]{:S(2)}) %collective-permute-start.46) | collective-permute-done | bytes 262176 | tf_op jit(solution)/shard_map/ppermute | solution.py:463
  269.7 6.9 %collective-permute-done.36.refs_1_ = bf16[4,4,2,4096]{3,2,1,0:T(2,128)(2,1)S(1)} collective-permute-done((bf16[4,4,2,4096]{3,2,1,0:T(2,128)(2,1)S(1)}, bf16[4,4,2,4096]{3,2,1,0:T(2,128)(2,1)S(1)}, u32[]{:S(2)}, u32[]{:S(2)}) %collective-permute-start.36) | collective-permute-done | bytes 262176 | tf_op jit(solution)/shard_map/ppermute | solution.py:463
  276.6 3.0 %collective-permute-start.34 = (bf16[4,4,2,4096]{3,2,1,0:T(2,128)(2,1)}, bf16[4,4,2,4096]{3,2,1,0:T(2,128)(2,1)}, u32[]{:S(2)}, u32[]{:S(2)}) collective-permute-start(bf16[4,4,2,4096]{3,2,1,0:T(2,128)(2,1)} %get-tuple-element.86), channel_id=1, source_target_pairs={{0,12},{4,8},{8,4},{12,0},{16,28},{20,24},{24,20},{28,16},{1,13},{... | collective-permute-start | bytes 786440 | tf_op jit(solution)/shard_map/ppermute | solution.py:463
  284.5 9.0 %collective-permute-done.38.refs_3_ = bf16[4,4,2,4096]{3,2,1,0:T(2,128)(2,1)S(1)} collective-permute-done((bf16[4,4,2,4096]{3,2,1,0:T(2,128)(2,1)}, bf16[4,4,2,4096]{3,2,1,0:T(2,128)(2,1)S(1)}, u32[]{:S(2)}, u32[]{:S(2)}) %collective-permute-start.38) | collective-permute-done | bytes 262176 | tf_op jit(solution)/shard_map/ppermute | solution.py:463
  294.7 4.3 %collective-permute-done.35.refs_2_ = bf16[4,4,2,4096]{3,2,1,0:T(2,128)(2,1)} collective-permute-done((bf16[4,4,2,4096]{3,2,1,0:T(2,128)(2,1)}, bf16[4,4,2,4096]{3,2,1,0:T(2,128)(2,1)}, u32[]{:S(2)}, u32[]{:S(2)}) %collective-permute-start.35) | collective-permute-done | bytes 262176 | tf_op jit(solution)/shard_map/ppermute | solution.py:463
  299.0 1.9 place.7
  (136 shorter events, 55.1 us)
Async XLA Ops:
  3.5 20.3 %collective-permute-start = (bf16[32,4096]{1,0:T(8,128)(2,1)S(1)}, bf16[32,4096]{1,0:T(8,128)(2,1)S(1)}, u32[]{:S(2)}, u32[]{:S(2)}) collective-permute-start(bf16[32,4096]{1,0:T(8,128)(2,1)S(1)} %pick.4), channel_id=1, source_target_pairs={{0,16},{4,20},{8,24},{12,28},{16,0},{20,4},{24,8},{28,12},{1,17},{... | collective-permute-start | bytes 786440 | tf_op jit(solution)/shard_map/ppermute | solution.py:463
  6.3 24.0 %collective-permute-start.1 = (bf16[32,4096]{1,0:T(8,128)(2,1)S(1)}, bf16[32,4096]{1,0:T(8,128)(2,1)S(1)}, u32[]{:S(2)}, u32[]{:S(2)}) collective-permute-start(bf16[32,4096]{1,0:T(8,128)(2,1)S(1)} %get-tuple-element.52), channel_id=1, source_target_pairs={{0,4},{4,0},{8,12},{12,8},{16,20},{20,16},{24,28},{28,24},{1,5},{5... | collective-permute-start | bytes 786440 | tf_op jit(solution)/shard_map/ppermute | solution.py:463
  7.9 27.2 %collective-permute-start.2 = (bf16[32,4096]{1,0:T(8,128)(2,1)S(1)}, bf16[32,4096]{1,0:T(8,128)(2,1)S(1)}, u32[]{:S(2)}, u32[]{:S(2)}) collective-permute-start(bf16[32,4096]{1,0:T(8,128)(2,1)S(1)} %get-tuple-element.53), channel_id=1, source_target_pairs={{0,20},{4,16},{8,28},{12,24},{16,4},{20,0},{24,12},{28,8},{1,21},{... | collective-permute-start | bytes 786440 | tf_op jit(solution)/shard_map/ppermute | solution.py:463
  8.2 31.5 %collective-permute-start.3 = (bf16[32,4096]{1,0:T(8,128)(2,1)S(1)}, bf16[32,4096]{1,0:T(8,128)(2,1)S(1)}, u32[]{:S(2)}, u32[]{:S(2)}) collective-permute-start(bf16[32,4096]{1,0:T(8,128)(2,1)S(1)} %get-tuple-element.54), channel_id=1, source_target_pairs={{0,8},{4,12},{8,0},{12,4},{16,24},{20,28},{24,16},{28,20},{1,9},{5... | collective-permute-start | bytes 786440 | tf_op jit(solution)/shard_map/ppermute | solution.py:463
  8.3 43.3 %collective-permute-start.4 = (bf16[32,4096]{1,0:T(8,128)(2,1)S(1)}, bf16[32,4096]{1,0:T(8,128)(2,1)S(1)}, u32[]{:S(2)}, u32[]{:S(2)}) collective-permute-start(bf16[32,4096]{1,0:T(8,128)(2,1)S(1)} %get-tuple-element.55), channel_id=1, source_target_pairs={{0,24},{4,28},{8,16},{12,20},{16,8},{20,12},{24,0},{28,4},{1,25},{... | collective-permute-start | bytes 786440 | tf_op jit(solution)/shard_map/ppermute | solution.py:463
  23.8 27.8 %collective-permute-start.5 = (bf16[32,4096]{1,0:T(8,128)(2,1)S(1)}, bf16[32,4096]{1,0:T(8,128)(2,1)S(1)}, u32[]{:S(2)}, u32[]{:S(2)}) collective-permute-start(bf16[32,4096]{1,0:T(8,128)(2,1)S(1)} %get-tuple-element.56), channel_id=1, source_target_pairs={{0,12},{4,8},{8,4},{12,0},{16,28},{20,24},{24,20},{28,16},{1,13},{... | collective-permute-start | bytes 786440 | tf_op jit(solution)/shard_map/ppermute | solution.py:463
  30.4 33.8 %collective-permute-start.6 = (bf16[32,4096]{1,0:T(8,128)(2,1)S(1)}, bf16[32,4096]{1,0:T(8,128)(2,1)S(1)}, u32[]{:S(2)}, u32[]{:S(2)}) collective-permute-start(bf16[32,4096]{1,0:T(8,128)(2,1)S(1)} %get-tuple-element.57), channel_id=1, source_target_pairs={{0,28},{4,24},{8,20},{12,16},{16,12},{20,8},{24,4},{28,0},{1,29},{... | collective-permute-start | bytes 786440 | tf_op jit(solution)/shard_map/ppermute | solution.py:463
  35.0 38.5 %collective-permute-start.14 = (bf16[32,4096]{1,0:T(8,128)(2,1)S(1)}, bf16[32,4096]{1,0:T(8,128)(2,1)S(1)}, u32[]{:S(2)}, u32[]{:S(2)}) collective-permute-start(bf16[32,4096]{1,0:T(8,128)(2,1)S(1)} %get-tuple-element.66), channel_id=1, source_target_pairs={{0,16},{4,20},{8,24},{12,28},{16,0},{20,4},{24,8},{28,12},{1,17},{... | collective-permute-start | bytes 786440 | tf_op jit(solution)/shard_map/ppermute | solution.py:463
  39.6 37.2 %collective-permute-start.15 = (bf16[32,4096]{1,0:T(8,128)(2,1)S(1)}, bf16[32,4096]{1,0:T(8,128)(2,1)S(1)}, u32[]{:S(2)}, u32[]{:S(2)}) collective-permute-start(bf16[32,4096]{1,0:T(8,128)(2,1)S(1)} %get-tuple-element.67), channel_id=1, source_target_pairs={{0,4},{4,0},{8,12},{12,8},{16,20},{20,16},{24,28},{28,24},{1,5},{5... | collective-permute-start | bytes 786440 | tf_op jit(solution)/shard_map/ppermute | solution.py:463
  51.6 27.6 %collective-permute-start.16 = (bf16[32,4096]{1,0:T(8,128)(2,1)S(1)}, bf16[32,4096]{1,0:T(8,128)(2,1)S(1)}, u32[]{:S(2)}, u32[]{:S(2)}) collective-permute-start(bf16[32,4096]{1,0:T(8,128)(2,1)S(1)} %get-tuple-element.68), channel_id=1, source_target_pairs={{0,20},{4,16},{8,28},{12,24},{16,4},{20,0},{24,12},{28,8},{1,21},{... | collective-permute-start | bytes 786440 | tf_op jit(solution)/shard_map/ppermute | solution.py:463
  51.6 31.9 %collective-permute-start.17 = (bf16[32,4096]{1,0:T(8,128)(2,1)S(1)}, bf16[32,4096]{1,0:T(8,128)(2,1)S(1)}, u32[]{:S(2)}, u32[]{:S(2)}) collective-permute-start(bf16[32,4096]{1,0:T(8,128)(2,1)S(1)} %get-tuple-element.69), channel_id=1, source_target_pairs={{0,8},{4,12},{8,0},{12,4},{16,24},{20,28},{24,16},{28,20},{1,9},{5... | collective-permute-start | bytes 786440 | tf_op jit(solution)/shard_map/ppermute | solution.py:463
  64.1 32.5 %collective-permute-start.18 = (bf16[32,4096]{1,0:T(8,128)(2,1)S(1)}, bf16[32,4096]{1,0:T(8,128)(2,1)S(1)}, u32[]{:S(2)}, u32[]{:S(2)}) collective-permute-start(bf16[32,4096]{1,0:T(8,128)(2,1)S(1)} %get-tuple-element.70), channel_id=1, source_target_pairs={{0,24},{4,28},{8,16},{12,20},{16,8},{20,12},{24,0},{28,4},{1,25},{... | collective-permute-start | bytes 786440 | tf_op jit(solution)/shard_map/ppermute | solution.py:463
  73.5 23.1 %collective-permute-start.19 = (bf16[32,4096]{1,0:T(8,128)(2,1)S(1)}, bf16[32,4096]{1,0:T(8,128)(2,1)S(1)}, u32[]{:S(2)}, u32[]{:S(2)}) collective-permute-start(bf16[32,4096]{1,0:T(8,128)(2,1)S(1)} %get-tuple-element.71), channel_id=1, source_target_pairs={{0,12},{4,8},{8,4},{12,0},{16,28},{20,24},{24,20},{28,16},{1,13},{... | collective-permute-start | bytes 786440 | tf_op jit(solution)/shard_map/ppermute | solution.py:463
  76.8 32.3 %collective-permute-start.20 = (bf16[32,4096]{1,0:T(8,128)(2,1)S(1)}, bf16[32,4096]{1,0:T(8,128)(2,1)S(1)}, u32[]{:S(2)}, u32[]{:S(2)}) collective-permute-start(bf16[32,4096]{1,0:T(8,128)(2,1)S(1)} %get-tuple-element.72), channel_id=1, source_target_pairs={{0,28},{4,24},{8,20},{12,16},{16,12},{20,8},{24,4},{28,0},{1,29},{... | collective-permute-start | bytes 786440 | tf_op jit(solution)/shard_map/ppermute | solution.py:463
  79.2 39.3 %collective-permute-start.7 = (bf16[32,4096]{1,0:T(8,128)(2,1)S(1)}, bf16[32,4096]{1,0:T(8,128)(2,1)S(1)}, u32[]{:S(2)}, u32[]{:S(2)}) collective-permute-start(bf16[32,4096]{1,0:T(8,128)(2,1)S(1)} %get-tuple-element.59), channel_id=1, source_target_pairs={{0,16},{4,20},{8,24},{12,28},{16,0},{20,4},{24,8},{28,12},{1,17},{... | collective-permute-start | bytes 786440 | tf_op jit(solution)/shard_map/ppermute | solution.py:463
  83.5 38.3 %collective-permute-start.8 = (bf16[32,4096]{1,0:T(8,128)(2,1)S(1)}, bf16[32,4096]{1,0:T(8,128)(2,1)S(1)}, u32[]{:S(2)}, u32[]{:S(2)}) collective-permute-start(bf16[32,4096]{1,0:T(8,128)(2,1)S(1)} %get-tuple-element.60), channel_id=1, source_target_pairs={{0,4},{4,0},{8,12},{12,8},{16,20},{20,16},{24,28},{28,24},{1,5},{5... | collective-permute-start | bytes 786440 | tf_op jit(solution)/shard_map/ppermute | solution.py:463
  96.6 32.8 %collective-permute-start.9 = (bf16[32,4096]{1,0:T(8,128)(2,1)S(1)}, bf16[32,4096]{1,0:T(8,128)(2,1)S(1)}, u32[]{:S(2)}, u32[]{:S(2)}) collective-permute-start(bf16[32,4096]{1,0:T(8,128)(2,1)S(1)} %get-tuple-element.61), channel_id=1, source_target_pairs={{0,20},{4,16},{8,28},{12,24},{16,4},{20,0},{24,12},{28,8},{1,21},{... | collective-permute-start | bytes 786440 | tf_op jit(solution)/shard_map/ppermute | solution.py:463
  96.6 32.8 %collective-permute-start.10 = (bf16[32,4096]{1,0:T(8,128)(2,1)S(1)}, bf16[32,4096]{1,0:T(8,128)(2,1)S(1)}, u32[]{:S(2)}, u32[]{:S(2)}) collective-permute-start(bf16[32,4096]{1,0:T(8,128)(2,1)S(1)} %get-tuple-element.62), channel_id=1, source_target_pairs={{0,8},{4,12},{8,0},{12,4},{16,24},{20,28},{24,16},{28,20},{1,9},{5... | collective-permute-start | bytes 786440 | tf_op jit(solution)/shard_map/ppermute | solution.py:463
  109.1 26.9 %collective-permute-start.11 = (bf16[32,4096]{1,0:T(8,128)(2,1)S(1)}, bf16[32,4096]{1,0:T(8,128)(2,1)S(1)}, u32[]{:S(2)}, u32[]{:S(2)}) collective-permute-start(bf16[32,4096]{1,0:T(8,128)(2,1)S(1)} %get-tuple-element.63), channel_id=1, source_target_pairs={{0,24},{4,28},{8,16},{12,20},{16,8},{20,12},{24,0},{28,4},{1,25},{... | collective-permute-start | bytes 786440 | tf_op jit(solution)/shard_map/ppermute | solution.py:463
  118.5 17.5 %collective-permute-start.12 = (bf16[32,4096]{1,0:T(8,128)(2,1)S(1)}, bf16[32,4096]{1,0:T(8,128)(2,1)S(1)}, u32[]{:S(2)}, u32[]{:S(2)}) collective-permute-start(bf16[32,4096]{1,0:T(8,128)(2,1)S(1)} %get-tuple-element.64), channel_id=1, source_target_pairs={{0,12},{4,8},{8,4},{12,0},{16,28},{20,24},{24,20},{28,16},{1,13},{... | collective-permute-start | bytes 786440 | tf_op jit(solution)/shard_map/ppermute | solution.py:463
  121.8 19.9 %collective-permute-start.13 = (bf16[32,4096]{1,0:T(8,128)(2,1)S(1)}, bf16[32,4096]{1,0:T(8,128)(2,1)S(1)}, u32[]{:S(2)}, u32[]{:S(2)}) collective-permute-start(bf16[32,4096]{1,0:T(8,128)(2,1)S(1)} %get-tuple-element.65), channel_id=1, source_target_pairs={{0,28},{4,24},{8,20},{12,16},{16,12},{20,8},{24,4},{28,0},{1,29},{... | collective-permute-start | bytes 786440 | tf_op jit(solution)/shard_map/ppermute | solution.py:463
  144.3 1.2 collective-permute-start.21
  145.5 3.9 %collective-permute-start.22 = (f32[2,16,224]{2,1,0:T(8,128)S(1)}, f32[2,16,224]{2,1,0:T(8,128)S(1)}, u32[]{:S(2)}, u32[]{:S(2)}) collective-permute-start(f32[2,16,224]{2,1,0:T(8,128)S(1)} %add.126), channel_id=1, source_target_pairs={{0,2},{1,3},{2,0},{3,1},{4,6},{5,7},{6,4},{7,5},{8,10},{9,11},{10,... | collective-permute-start | bytes 86024 | tf_op jit(solution)/shard_map/ppermute | solution.py:474
  149.4 3.9 %collective-permute-start.23 = (f32[2,16,224]{2,1,0:T(8,128)S(1)}, f32[2,16,224]{2,1,0:T(8,128)S(1)}, u32[]{:S(2)}, u32[]{:S(2)}) collective-permute-start(f32[2,16,224]{2,1,0:T(8,128)S(1)} %add.127.after_ref), channel_id=1, source_target_pairs={{0,4},{4,0},{8,12},{12,8},{16,20},{20,16},{24,28},{28,24},{1,5},{5... | collective-permute-start | bytes 86024 | tf_op jit(solution)/shard_map/ppermute | solution.py:474
  153.4 3.9 %collective-permute-start.24 = (f32[2,16,224]{2,1,0:T(8,128)S(1)}, f32[2,16,224]{2,1,0:T(8,128)S(1)}, u32[]{:S(2)}, u32[]{:S(2)}) collective-permute-start(f32[2,16,224]{2,1,0:T(8,128)S(1)} %add.128), channel_id=1, source_target_pairs={{0,8},{4,12},{8,0},{12,4},{16,24},{20,28},{24,16},{28,20},{1,9},{5... | collective-permute-start | bytes 86024 | tf_op jit(solution)/shard_map/ppermute | solution.py:474
  157.3 4.8 %collective-permute-start.25 = (f32[2,16,224]{2,1,0:T(8,128)S(1)}, f32[2,16,224]{2,1,0:T(8,128)S(1)}, u32[]{:S(2)}, u32[]{:S(2)}) collective-permute-start(f32[2,16,224]{2,1,0:T(8,128)S(1)} %add.129), channel_id=1, source_target_pairs={{0,16},{4,20},{8,24},{12,28},{16,0},{20,4},{24,8},{28,12},{1,17},{... | collective-permute-start | bytes 86024 | tf_op jit(solution)/shard_map/ppermute | solution.py:474
  163.9 19.9 %collective-permute-start.26 = (bf16[4,4,2,4096]{3,2,1,0:T(2,128)(2,1)S(1)}, bf16[4,4,2,4096]{3,2,1,0:T(2,128)(2,1)S(1)}, u32[]{:S(2)}, u32[]{:S(2)}) collective-permute-start(bf16[4,4,2,4096]{3,2,1,0:T(2,128)(2,1)S(1)} %get-tuple-element.78), channel_id=1, source_target_pairs={{0,16},{4,20},{8,24},{12,28},{16,0},{20,4},{24,8},{28,12},{1,17},{... | collective-permute-start | bytes 786440 | tf_op jit(solution)/shard_map/ppermute | solution.py:463
  167.7 60.8 %slice-start = ((s8[6291456]{0:T(1024)(128)(4,1)}), s8[4194304]{0:T(1024)(128)(4,1)S(1)}, s32[]{:S(2)}) async-start(s8[6291456]{0:T(1024)(128)(4,1)} %bitcast.25), calls=%async_computation | async-start | bytes 8388608
  167.7 19.2 %collective-permute-start.27 = (bf16[4,4,2,4096]{3,2,1,0:T(2,128)(2,1)S(1)}, bf16[4,4,2,4096]{3,2,1,0:T(2,128)(2,1)S(1)}, u32[]{:S(2)}, u32[]{:S(2)}) collective-permute-start(bf16[4,4,2,4096]{3,2,1,0:T(2,128)(2,1)S(1)} %get-tuple-element.79), channel_id=1, source_target_pairs={{0,4},{4,0},{8,12},{12,8},{16,20},{20,16},{24,28},{28,24},{1,5},{5... | collective-permute-start | bytes 786440 | tf_op jit(solution)/shard_map/ppermute | solution.py:463
  168.3 28.2 %collective-permute-start.28 = (bf16[4,4,2,4096]{3,2,1,0:T(2,128)(2,1)S(1)}, bf16[4,4,2,4096]{3,2,1,0:T(2,128)(2,1)S(1)}, u32[]{:S(2)}, u32[]{:S(2)}) collective-permute-start(bf16[4,4,2,4096]{3,2,1,0:T(2,128)(2,1)S(1)} %get-tuple-element.80), channel_id=1, source_target_pairs={{0,20},{4,16},{8,28},{12,24},{16,4},{20,0},{24,12},{28,8},{1,21},{... | collective-permute-start | bytes 786440 | tf_op jit(solution)/shard_map/ppermute | solution.py:463
  169.9 34.3 %collective-permute-start.29 = (bf16[4,4,2,4096]{3,2,1,0:T(2,128)(2,1)S(1)}, bf16[4,4,2,4096]{3,2,1,0:T(2,128)(2,1)S(1)}, u32[]{:S(2)}, u32[]{:S(2)}) collective-permute-start(bf16[4,4,2,4096]{3,2,1,0:T(2,128)(2,1)S(1)} %get-tuple-element.81), channel_id=1, source_target_pairs={{0,8},{4,12},{8,0},{12,4},{16,24},{20,28},{24,16},{28,20},{1,9},{5... | collective-permute-start | bytes 786440 | tf_op jit(solution)/shard_map/ppermute | solution.py:463
  171.4 42.1 %collective-permute-start.30 = (bf16[4,4,2,4096]{3,2,1,0:T(2,128)(2,1)S(1)}, bf16[4,4,2,4096]{3,2,1,0:T(2,128)(2,1)S(1)}, u32[]{:S(2)}, u32[]{:S(2)}) collective-permute-start(bf16[4,4,2,4096]{3,2,1,0:T(2,128)(2,1)S(1)} %get-tuple-element.82), channel_id=1, source_target_pairs={{0,24},{4,28},{8,16},{12,20},{16,8},{20,12},{24,0},{28,4},{1,25},{... | collective-permute-start | bytes 786440 | tf_op jit(solution)/shard_map/ppermute | solution.py:463
  183.8 29.7 %collective-permute-start.31 = (bf16[4,4,2,4096]{3,2,1,0:T(2,128)(2,1)S(1)}, bf16[4,4,2,4096]{3,2,1,0:T(2,128)(2,1)S(1)}, u32[]{:S(2)}, u32[]{:S(2)}) collective-permute-start(bf16[4,4,2,4096]{3,2,1,0:T(2,128)(2,1)S(1)} %get-tuple-element.83), channel_id=1, source_target_pairs={{0,12},{4,8},{8,4},{12,0},{16,28},{20,24},{24,20},{28,16},{1,13},{... | collective-permute-start | bytes 786440 | tf_op jit(solution)/shard_map/ppermute | solution.py:463
  186.9 39.1 %collective-permute-start.32 = (bf16[4,4,2,4096]{3,2,1,0:T(2,128)(2,1)S(1)}, bf16[4,4,2,4096]{3,2,1,0:T(2,128)(2,1)S(1)}, u32[]{:S(2)}, u32[]{:S(2)}) collective-permute-start(bf16[4,4,2,4096]{3,2,1,0:T(2,128)(2,1)S(1)} %get-tuple-element.84), channel_id=1, source_target_pairs={{0,28},{4,24},{8,20},{12,16},{16,12},{20,8},{24,4},{28,0},{1,29},{... | collective-permute-start | bytes 786440 | tf_op jit(solution)/shard_map/ppermute | solution.py:463
  196.4 41.0 %collective-permute-start.40 = (bf16[4,4,2,4096]{3,2,1,0:T(2,128)(2,1)S(1)}, bf16[4,4,2,4096]{3,2,1,0:T(2,128)(2,1)S(1)}, u32[]{:S(2)}, u32[]{:S(2)}) collective-permute-start(bf16[4,4,2,4096]{3,2,1,0:T(2,128)(2,1)S(1)} %get-tuple-element.95), channel_id=1, source_target_pairs={{0,16},{4,20},{8,24},{12,28},{16,0},{20,4},{24,8},{28,12},{1,17},{... | collective-permute-start | bytes 786440 | tf_op jit(solution)/shard_map/ppermute | solution.py:463
  204.1 33.3 %collective-permute-start.41 = (bf16[4,4,2,4096]{3,2,1,0:T(2,128)(2,1)S(1)}, bf16[4,4,2,4096]{3,2,1,0:T(2,128)(2,1)S(1)}, u32[]{:S(2)}, u32[]{:S(2)}) collective-permute-start(bf16[4,4,2,4096]{3,2,1,0:T(2,128)(2,1)S(1)} %get-tuple-element.96), channel_id=1, source_target_pairs={{0,4},{4,0},{8,12},{12,8},{16,20},{20,16},{24,28},{28,24},{1,5},{5... | collective-permute-start | bytes 786440 | tf_op jit(solution)/shard_map/ppermute | solution.py:463
  213.5 27.4 %collective-permute-start.42 = (bf16[4,4,2,4096]{3,2,1,0:T(2,128)(2,1)S(1)}, bf16[4,4,2,4096]{3,2,1,0:T(2,128)(2,1)S(1)}, u32[]{:S(2)}, u32[]{:S(2)}) collective-permute-start(bf16[4,4,2,4096]{3,2,1,0:T(2,128)(2,1)S(1)} %get-tuple-element.97), channel_id=1, source_target_pairs={{0,20},{4,16},{8,28},{12,24},{16,4},{20,0},{24,12},{28,8},{1,21},{... | collective-permute-start | bytes 786440 | tf_op jit(solution)/shard_map/ppermute | solution.py:463
  213.5 29.2 %collective-permute-start.43 = (bf16[4,4,2,4096]{3,2,1,0:T(2,128)(2,1)S(1)}, bf16[4,4,2,4096]{3,2,1,0:T(2,128)(2,1)S(1)}, u32[]{:S(2)}, u32[]{:S(2)}) collective-permute-start(bf16[4,4,2,4096]{3,2,1,0:T(2,128)(2,1)S(1)} %get-tuple-element.98), channel_id=1, source_target_pairs={{0,8},{4,12},{8,0},{12,4},{16,24},{20,28},{24,16},{28,20},{1,9},{5... | collective-permute-start | bytes 786440 | tf_op jit(solution)/shard_map/ppermute | solution.py:463
  226.0 38.1 %collective-permute-start.44 = (bf16[4,4,2,4096]{3,2,1,0:T(2,128)(2,1)S(1)}, bf16[4,4,2,4096]{3,2,1,0:T(2,128)(2,1)S(1)}, u32[]{:S(2)}, u32[]{:S(2)}) collective-permute-start(bf16[4,4,2,4096]{3,2,1,0:T(2,128)(2,1)S(1)} %get-tuple-element.99), channel_id=1, source_target_pairs={{0,24},{4,28},{8,16},{12,20},{16,8},{20,12},{24,0},{28,4},{1,25},{... | collective-permute-start | bytes 786440 | tf_op jit(solution)/shard_map/ppermute | solution.py:463
  237.4 28.3 %collective-permute-start.45 = (bf16[4,4,2,4096]{3,2,1,0:T(2,128)(2,1)S(1)}, bf16[4,4,2,4096]{3,2,1,0:T(2,128)(2,1)S(1)}, u32[]{:S(2)}, u32[]{:S(2)}) collective-permute-start(bf16[4,4,2,4096]{3,2,1,0:T(2,128)(2,1)S(1)} %get-tuple-element.100), channel_id=1, source_target_pairs={{0,12},{4,8},{8,4},{12,0},{16,28},{20,24},{24,20},{28,16},{1,13},{... | collective-permute-start | bytes 786440 | tf_op jit(solution)/shard_map/ppermute | solution.py:463
  237.4 32.3 %collective-permute-start.46 = (bf16[4,4,2,4096]{3,2,1,0:T(2,128)(2,1)S(1)}, bf16[4,4,2,4096]{3,2,1,0:T(2,128)(2,1)S(1)}, u32[]{:S(2)}, u32[]{:S(2)}) collective-permute-start(bf16[4,4,2,4096]{3,2,1,0:T(2,128)(2,1)S(1)} %get-tuple-element.101), channel_id=1, source_target_pairs={{0,28},{4,24},{8,20},{12,16},{16,12},{20,8},{24,4},{28,0},{1,29},{... | collective-permute-start | bytes 786440 | tf_op jit(solution)/shard_map/ppermute | solution.py:463
  240.9 35.8 %collective-permute-start.36 = (bf16[4,4,2,4096]{3,2,1,0:T(2,128)(2,1)S(1)}, bf16[4,4,2,4096]{3,2,1,0:T(2,128)(2,1)S(1)}, u32[]{:S(2)}, u32[]{:S(2)}) collective-permute-start(bf16[4,4,2,4096]{3,2,1,0:T(2,128)(2,1)S(1)} %get-tuple-element.89), channel_id=1, source_target_pairs={{0,16},{4,20},{8,24},{12,28},{16,0},{20,4},{24,8},{28,12},{1,17},{... | collective-permute-start | bytes 786440 | tf_op jit(solution)/shard_map/ppermute | solution.py:463
  242.7 36.9 %collective-permute-start.37 = (bf16[4,4,2,4096]{3,2,1,0:T(2,128)(2,1)S(1)}, bf16[4,4,2,4096]{3,2,1,0:T(2,128)(2,1)S(1)}, u32[]{:S(2)}, u32[]{:S(2)}) collective-permute-start(bf16[4,4,2,4096]{3,2,1,0:T(2,128)(2,1)S(1)} %get-tuple-element.90), channel_id=1, source_target_pairs={{0,4},{4,0},{8,12},{12,8},{16,20},{20,16},{24,28},{28,24},{1,5},{5... | collective-permute-start | bytes 786440 | tf_op jit(solution)/shard_map/ppermute | solution.py:463
  264.8 29.9 %collective-permute-start.33 = (bf16[4,4,2,4096]{3,2,1,0:T(2,128)(2,1)}, bf16[4,4,2,4096]{3,2,1,0:T(2,128)(2,1)S(1)}, u32[]{:S(2)}, u32[]{:S(2)}) collective-permute-start(bf16[4,4,2,4096]{3,2,1,0:T(2,128)(2,1)} %get-tuple-element.85), channel_id=1, source_target_pairs={{0,24},{4,28},{8,16},{12,20},{16,8},{20,12},{24,0},{28,4},{1,25},{... | collective-permute-start | bytes 786440 | tf_op jit(solution)/shard_map/ppermute | solution.py:463
  265.8 27.8 %collective-permute-start.38 = (bf16[4,4,2,4096]{3,2,1,0:T(2,128)(2,1)}, bf16[4,4,2,4096]{3,2,1,0:T(2,128)(2,1)S(1)}, u32[]{:S(2)}, u32[]{:S(2)}) collective-permute-start(bf16[4,4,2,4096]{3,2,1,0:T(2,128)(2,1)} %get-tuple-element.91), channel_id=1, source_target_pairs={{0,20},{4,16},{8,28},{12,24},{16,4},{20,0},{24,12},{28,8},{1,21},{... | collective-permute-start | bytes 786440 | tf_op jit(solution)/shard_map/ppermute | solution.py:463
  269.7 23.9 %collective-permute-start.39 = (bf16[4,4,2,4096]{3,2,1,0:T(2,128)(2,1)}, bf16[4,4,2,4096]{3,2,1,0:T(2,128)(2,1)S(1)}, u32[]{:S(2)}, u32[]{:S(2)}) collective-permute-start(bf16[4,4,2,4096]{3,2,1,0:T(2,128)(2,1)} %get-tuple-element.92), channel_id=1, source_target_pairs={{0,8},{4,12},{8,0},{12,4},{16,24},{20,28},{24,16},{28,20},{1,9},{5... | collective-permute-start | bytes 786440 | tf_op jit(solution)/shard_map/ppermute | solution.py:463
  276.6 18.1 %collective-permute-start.34 = (bf16[4,4,2,4096]{3,2,1,0:T(2,128)(2,1)}, bf16[4,4,2,4096]{3,2,1,0:T(2,128)(2,1)}, u32[]{:S(2)}, u32[]{:S(2)}) collective-permute-start(bf16[4,4,2,4096]{3,2,1,0:T(2,128)(2,1)} %get-tuple-element.86), channel_id=1, source_target_pairs={{0,12},{4,8},{8,4},{12,0},{16,28},{20,24},{24,20},{28,16},{1,13},{... | collective-permute-start | bytes 786440 | tf_op jit(solution)/shard_map/ppermute | solution.py:463
  279.6 19.3 %collective-permute-start.35 = (bf16[4,4,2,4096]{3,2,1,0:T(2,128)(2,1)}, bf16[4,4,2,4096]{3,2,1,0:T(2,128)(2,1)}, u32[]{:S(2)}, u32[]{:S(2)}) collective-permute-start(bf16[4,4,2,4096]{3,2,1,0:T(2,128)(2,1)} %get-tuple-element.87), channel_id=1, source_target_pairs={{0,28},{4,24},{8,20},{12,16},{16,12},{20,8},{24,4},{28,0},{1,29},{... | collective-permute-start | bytes 786440 | tf_op jit(solution)/shard_map/ppermute | solution.py:463
  (16 other events, 136.5 us)

commit v5 on v4

--- a/solution.py
+++ b/solution.py
@@ -19,7 +19,6 @@
 CHUNKS_IN = ((0, 0, 4), (1, 0, 4), (2, 0, 4))
 CHUNKS_OUT = (0, 1, 2)
 QUARTERS = 4
-EARLY = 0
 
 shift_rate = 0.61
 MIB = 1024 * 1024
@@ -86,7 +85,7 @@
         out_specs=[pl.BlockSpec(memory_space=pltpu.VMEM)] * count,
         out_shape=[jax.ShapeDtypeStruct((own.shape[1], size), own.dtype)] * count,
         scratch_shapes=[pltpu.SemaphoreType.DMA((count,))],
-        compiler_params=pltpu.CompilerParams(vmem_limit_bytes=vmem(devices)),
+        compiler_params=pltpu.CompilerParams(vmem_limit_bytes=60 * MIB if len(wanted) < devices - 1 else vmem(devices)),
         name="pick",
     )(me, own, *after)
 
@@ -253,23 +252,22 @@
     )(me, scales, sums, start, tiles)
 
 
-def fetch_kernel(me_ref, spectra_ref, after_ref, out_ref, sem):
-    side = jnp.bitwise_xor(me_ref[0], 1)
-    copy = pltpu.make_async_copy(spectra_ref.at[pl.ds(side, 1)], out_ref, sem)
+def fetch_kernel(spectra_ref, after_ref, out_ref, sem):
+    copy = pltpu.make_async_copy(spectra_ref, out_ref, sem)
     copy.start()
     copy.wait()
 
 
-def fetch(side, spectra, after, devices):
+def fetch(spectra, after, devices):
     return pl.pallas_call(
         fetch_kernel,
-        in_specs=[pl.BlockSpec(memory_space=pltpu.SMEM)] + [pl.BlockSpec(memory_space=pl.ANY)] * 2,
+        in_specs=[pl.BlockSpec(memory_space=pl.ANY)] * 2,
         out_specs=pl.BlockSpec(memory_space=pltpu.VMEM),
-        out_shape=jax.ShapeDtypeStruct((1,) + spectra.shape[1:], spectra.dtype),
+        out_shape=jax.ShapeDtypeStruct(spectra.shape, spectra.dtype),
         scratch_shapes=[pltpu.SemaphoreType.DMA(())],
         compiler_params=pltpu.CompilerParams(vmem_limit_bytes=vmem(devices)),
         name="fetch",
-    )(side, spectra, after)
+    )(spectra, after)
 
 
 def modes_kernel(after, sides, me_ref, mix_ref, spectra_ref, *refs):
@@ -295,24 +293,22 @@
             out[f, k] = wide[place : place + 2].astype(out.dtype)
 
 
-def modes_of(me, mix, spectra, after, devices, sides, skip, tile):
+def modes_of(me, mix, spectra, after, devices, sides, tile):
     freqs = NF // devices
     part = devices // GROUPS
     groups, rows, size = spectra.shape
     count = part * len(sides)
-    if groups == 1:
-        source = pl.BlockSpec((1, rows, tile), lambda g, m: (0, 0, skip // tile + g))
-    elif len(sides) == 1:
+    if len(sides) == 1:
         source = pl.BlockSpec(
-            (1, rows, tile), lambda g, m: (jnp.bitwise_xor(m[0] // part, sides[0]), 0, skip // tile + g)
+            (1, rows, tile), lambda g, m: (jnp.bitwise_xor(m[0] // part, sides[0]), 0, g)
         )
     else:
-        source = pl.BlockSpec((groups, rows, tile), lambda g, m: (0, 0, skip // tile + g))
+        source = pl.BlockSpec((groups, rows, tile), lambda g, m: (0, 0, g))
     made = pl.pallas_call(
         functools.partial(modes_kernel, len(after), sides),
         grid_spec=pltpu.PrefetchScalarGridSpec(
             num_scalar_prefetch=1,
-            grid=((size - skip) // tile,),
+            grid=(size // tile,),
             in_specs=[
                 pl.BlockSpec(mix.shape, lambda g, m: (0, 0, 0)),
                 source,
@@ -320,7 +316,7 @@
             + [pl.BlockSpec(memory_space=pl.ANY)] * len(after),
             out_specs=[pl.BlockSpec((freqs, MODES, 2, tile), lambda g, m: (0, 0, 0, g))] * count,
         ),
-        out_shape=[jax.ShapeDtypeStruct((freqs, MODES, 2, size - skip), jnp.bfloat16)] * count,
+        out_shape=[jax.ShapeDtypeStruct((freqs, MODES, 2, size), jnp.bfloat16)] * count,
         compiler_params=pltpu.CompilerParams(vmem_limit_bytes=vmem(devices)),
         name="modes",
     )(me, mix, spectra, *after)
@@ -369,60 +365,6 @@
     return dict(enumerate(made))
 
 
-def choose_kernel(me_ref, table_ref, spectra_ref, after_ref, *outs):
-    part = len(outs)
-    other = jnp.bitwise_xor(me_ref[0] // part, 1)
-    for near, out in enumerate(outs):
-        out[...] = jnp.dot(table_ref[near], spectra_ref[other], preferred_element_type=jnp.float32).astype(out.dtype)
-
-
-def choose(me, table, spectra, after, devices, size, tile):
-    groups, rows, _ = spectra.shape
-    part = devices // GROUPS
-    return pl.pallas_call(
-        choose_kernel,
-        grid_spec=pltpu.PrefetchScalarGridSpec(
-            num_scalar_prefetch=1,
-            grid=(size // tile,),
-            in_specs=[
-                pl.BlockSpec(table.shape, lambda g, m: (0, 0, 0)),
-                pl.BlockSpec((groups, rows, tile), lambda g, m: (0, 0, g)),
-                pl.BlockSpec(memory_space=pl.ANY),
-            ],
-            out_specs=[pl.BlockSpec((table.shape[1], tile), lambda g, m: (0, g))] * part,
-        ),
-        out_shape=[jax.ShapeDtypeStruct((table.shape[1], size), jnp.bfloat16)] * part,
-        compiler_params=pltpu.CompilerParams(vmem_limit_bytes=vmem(devices)),
-        name="choose",
-    )(me, table, spectra, after)
-
-
-def finish_kernel(count, mix_ref, table_ref, *refs):
-    mix = lax.dot_general(
-        mix_ref[0], table_ref[...], (((1,), (1,)), ((), ())), preferred_element_type=jnp.float32
-    ).astype(jnp.bfloat16)
-    for landed, out in zip(refs[:count], refs[count:]):
-        split_rows(jnp.dot(mix, landed[...], preferred_element_type=jnp.float32), out)
-
-
-def finish(mix, table, landed, devices, freqs, tile):
-    count = len(landed)
-    rows, size = landed[0].shape
-    return pl.pallas_call(
-        functools.partial(finish_kernel, count),
-        grid=(size // tile,),
-        in_specs=[
-            pl.BlockSpec((1,) + mix.shape[1:], lambda g: (0, 0, 0)),
-            pl.BlockSpec(table.shape, lambda g: (0, 0)),
-        ]
-        + [pl.BlockSpec((rows, tile), lambda g: (0, g))] * count,
-        out_specs=[pl.BlockSpec((freqs, MODES, 2, tile), lambda g: (0, 0, 0, g))] * count,
-        out_shape=[jax.ShapeDtypeStruct((freqs, MODES, 2, size), jnp.bfloat16)] * count,
-        compiler_params=pltpu.CompilerParams(vmem_limit_bytes=vmem(devices)),
-        name="finish",
-    )(mix, table, *landed)
-
-
 def place_kernel(spots, comp, sub, me_ref, *refs):
     count = len(spots)
     pieces, out_ref, sems = refs[:count], refs[-2], refs[-1]
@@ -524,20 +466,8 @@
         *made, sums = gather(me, band, fold, weights, own, landed, sums, keep, comp, start, size, sub, unit if keep else 4 * unit)
         spectra += made
         history.append(sums)
-    part = devices // GROUPS
-    early = EARLY * unit // 2
-    lines = jnp.arange(blocks * 2 * freqs, dtype=jnp.int32)
-    near = jnp.bitwise_xor(index.astype(jnp.int32), jnp.arange(part, dtype=jnp.int32)) % part
-    same_part = (lines // freqs)[:, None] == (line // PER_GROUP)[None, :]
-    wanted = (near[:, None] * freqs + lines % freqs)[:, :, None] == (line % PER_GROUP)[None, None, :]
-    table = (same_part[None] & wanted).astype(jnp.bfloat16)
-    crossed = []
-    if early:
-        chosen = choose(me, table, spectra[0], history[-2], devices, early, unit // 2)
-        crossed = [send(value, part + n, devices) for n, value in enumerate(chosen)]
-
     sums = sum_over(sums, "space")
-    ready = fetch(me // part, spectra[0], sums, devices)
+    ready = fetch(spectra[0], sums, devices)
     sums = sum_over(sums, "tm")
     mix, energies = solve(me, scales, sums, start_table, tiles, devices)
     placed = [None]
@@ -547,22 +477,18 @@
         after = [] if len(placed) < 3 else placed[-2:-1]
         pieces = []
         if chunk == 0:
-            made = modes_of(me, mix, ready, after, devices, (1,), early, 4 * unit)
-            made.update(modes_of(me, mix, spectra[0], after, devices, (0,), 0, unit))
+            made = modes_of(me, mix, ready, after, devices, (1,), QUARTERS * unit)
+            made.update(modes_of(me, mix, ready, after, devices, (0,), unit))
         elif chunk == len(CHUNKS_IN) - 1:
             made = modes_again(
                 me, band, mix, own, landed, after, devices, comp, first * unit, length * unit, sub, unit
             )
         else:
-            made = modes_of(me, mix, spectra[chunk], after, devices, (0, 1), 0, unit)
+            made = modes_of(me, mix, spectra[chunk], after, devices, (0, 1), unit)
         for turn in turns(devices):
-            skip = early if chunk == 0 and turn >= part else 0
             value = send(made[turn], turn, devices) if turn else made[turn]
-            pieces.append((value, turn, first * unit + skip))
-        if chunk == 0 and early:
-            late = finish(mix, table[0], crossed, devices, freqs, unit // 2)
-            pieces += [(value, part + n, first * unit) for n, value in enumerate(late)]
-        soon = pieces[:5] if chunk == CHUNKS_OUT[-1] else []
+            pieces.append((value, turn, first * unit))
+        soon = pieces[:6] if chunk == CHUNKS_OUT[-1] else []
         done = place(me, soon, placed[-1], devices, comp, sub, shape) if soon else placed[-1]
         placed.append(place(me, pieces[len(soon) :], done, devices, comp, sub, shape))
     mine = lax.dynamic_slice_in_dim(energies, index * freqs, freqs, 1)

time: 302 us -> 301 us (level)
  local copies, waits for them, and re-layouts: 27.8 us -> 18.2 us
  waiting for transfers between devices: 154 us -> 159 us
  Pallas kernels: 27 us -> 31.8 us
    broadcast_in_dim x8, local copies, waits for them, and re-layouts: 9.46 us -> 2.6 us  [band_table(): band = jnp.where(first, low, jnp.where(second, high, nothing))]
    ppermute x42, waiting for transfers between devices: 145 us -> 150 us  [send(): return lax.ppermute(value, 'tm', [(d, d ^ turn) for d in range(devices)])]
    pallas_call x4, Pallas kernels: 0.61 us -> 4.65 us  [pick(): pl.pallas_call(functools.partial(pick_kernel, wanted, comp, start, size,...]
    unnamed x35 -> x33, local copies, waits for them, and re-layouts: 18 us -> 15.2 us
  transfers between devices with their start and end apart: 47 -> 47, of which waited for: 25 -> 26; matrix products, arithmetic and copies ran while one was open for 4% -> 2% of each run, Pallas kernels for 7% -> 8%
where the time goes in v5:
time: 301 us; the launch traced here: 300 us
  waiting for transfers between devices  159 us (53%)
  starting transfers between devices  87.7 us (29%)
  Pallas kernels  31.8 us (11%)
  local copies, waits for them, and re-layouts  18.2 us (6%)
    ppermute x42, waiting for transfers between devices, send(): return lax.ppermute(value, 'tm', [(d, d ^ turn) for d in range(devices)])  150 us
    ppermute x42, starting transfers between devices, send(): return lax.ppermute(value, 'tm', [(d, d ^ turn) for d in range(devices)])  83.2 us
    unnamed x33, local copies, waits for them, and re-layouts  15.2 us
    pallas_call x3, Pallas kernels, gather(): pl.pallas_call(functools.partial(gather_kernel, count), grid_spec=pltpu.P...  11 us
    ppermute x5, waiting for transfers between devices, sum_over(): lax.ppermute(value, axis, [(d, d ^ step) for d in range(count)])  8.77 us
    pallas_call x4, Pallas kernels, place(): pl.pallas_call(functools.partial(place_kernel, [piece[1:] for piece in pi...  6.63 us
  transfers between devices with their start and end apart: 47, of which 26 were waited for; matrix products, arithmetic and copies ran while one was open for 2% of the time, Pallas kernels for 8%

profile of v5, /device:TPU:8, one launch (start us, length us, event | category | flops | bytes accessed | tf_op | source)
XLA Modules:
  0.0 300.1 jit_solution(16447170674831390978)
XLA Ops:
  2.3 2.7 collective-permute-start
  5.0 2.6 pick.5
  9.6 3.0 %collective-permute-start.4 = (bf16[32,4096]{1,0:T(8,128)(2,1)}, bf16[32,4096]{1,0:T(8,128)(2,1)S(1)}, u32[]{:S(2)}, u32[]{:S(2)}) collective-permute-start(bf16[32,4096]{1,0:T(8,128)(2,1)} %get-tuple-element.55), channel_id=1, source_target_pairs={{0,24},{4,28},{8,16},{12,20},{16,8},{20,12},{24,0},{28,4},{1,25},{... | collective-permute-start | bytes 786440 | tf_op jit(solution)/shard_map/ppermute | solution.py:405
  15.8 7.1 %collective-permute-done.refs_0_ = bf16[32,4096]{1,0:T(8,128)(2,1)S(1)} collective-permute-done((bf16[32,4096]{1,0:T(8,128)(2,1)}, bf16[32,4096]{1,0:T(8,128)(2,1)S(1)}, u32[]{:S(2)}, u32[]{:S(2)}) %collective-permute-start) | collective-permute-done | bytes 262176 | tf_op jit(solution)/shard_map/ppermute | solution.py:405
  22.9 3.7 %collective-permute-start.5 = (bf16[32,4096]{1,0:T(8,128)(2,1)}, bf16[32,4096]{1,0:T(8,128)(2,1)S(1)}, u32[]{:S(2)}, u32[]{:S(2)}) collective-permute-start(bf16[32,4096]{1,0:T(8,128)(2,1)} %get-tuple-element.56), channel_id=1, source_target_pairs={{0,12},{4,8},{8,4},{12,0},{16,28},{20,24},{24,20},{28,16},{1,13},{... | collective-permute-start | bytes 786440 | tf_op jit(solution)/shard_map/ppermute | solution.py:405
  26.6 2.8 copy-done
  31.1 3.1 %collective-permute-done.2.refs_2_ = bf16[32,4096]{1,0:T(8,128)(2,1)S(1)} collective-permute-done((bf16[32,4096]{1,0:T(8,128)(2,1)}, bf16[32,4096]{1,0:T(8,128)(2,1)S(1)}, u32[]{:S(2)}, u32[]{:S(2)}) %collective-permute-start.2) | collective-permute-done | bytes 262176 | tf_op jit(solution)/shard_map/ppermute | solution.py:405
  34.2 4.5 %collective-permute-start.14 = (bf16[32,4096]{1,0:T(8,128)(2,1)S(1)}, bf16[32,4096]{1,0:T(8,128)(2,1)S(1)}, u32[]{:S(2)}, u32[]{:S(2)}) collective-permute-start(bf16[32,4096]{1,0:T(8,128)(2,1)S(1)} %get-tuple-element.66), channel_id=1, source_target_pairs={{0,16},{4,20},{8,24},{12,28},{16,0},{20,4},{24,8},{28,12},{1,17},{... | collective-permute-start | bytes 786440 | tf_op jit(solution)/shard_map/ppermute | solution.py:405
  39.3 11.4 %collective-permute-done.4.refs_4_ = bf16[32,4096]{1,0:T(8,128)(2,1)S(1)} collective-permute-done((bf16[32,4096]{1,0:T(8,128)(2,1)}, bf16[32,4096]{1,0:T(8,128)(2,1)S(1)}, u32[]{:S(2)}, u32[]{:S(2)}) %collective-permute-start.4) | collective-permute-done | bytes 262176 | tf_op jit(solution)/shard_map/ppermute | solution.py:405
  50.7 4.3 %collective-permute-start.17 = (bf16[32,4096]{1,0:T(8,128)(2,1)S(1)}, bf16[32,4096]{1,0:T(8,128)(2,1)S(1)}, u32[]{:S(2)}, u32[]{:S(2)}) collective-permute-start(bf16[32,4096]{1,0:T(8,128)(2,1)S(1)} %get-tuple-element.69), channel_id=1, source_target_pairs={{0,8},{4,12},{8,0},{12,4},{16,24},{20,28},{24,16},{28,20},{1,9},{5... | collective-permute-start | bytes 786440 | tf_op jit(solution)/shard_map/ppermute | solution.py:405
  55.0 8.2 %collective-permute-done.6.refs_6_ = bf16[32,4096]{1,0:T(8,128)(2,1)S(1)} collective-permute-done((bf16[32,4096]{1,0:T(8,128)(2,1)S(1)}, bf16[32,4096]{1,0:T(8,128)(2,1)S(1)}, u32[]{:S(2)}, u32[]{:S(2)}) %collective-permute-start.6) | collective-permute-done | bytes 262176 | tf_op jit(solution)/shard_map/ppermute | solution.py:405
  64.8 4.2 %gather.3 = (bf16[2,224,4096]{2,1,0:T(8,128)(2,1)S(1)}, f32[2,16,224]{2,1,0:T(8,128)S(1)}) custom-call(s32[1]{0:T(128)} %bitcast.me_ref, bf16[2,224,256]{2,1,0:T(8,128)(2,1)S(1)} %select_select_fusion.band_ref, f32[16,224]{1,0:T(8,128)S(1)} %fusion.6.fold_ref, f32[1,32768]{1,0:T(1,128)S(1)} %bitcast.29, bf16[3,32,32768]{2,1,0:T(8,128)(2,1)S(1)} %bitcast.21, ...), custom_call_target="tpu_custom_call" | custom-call | flops 1761607680 | bytes 5767168 | tf_op jit(solution)/shard_map/gather/pallas_call | solution.py:134
  72.6 3.3 %collective-permute-start.19 = (bf16[32,4096]{1,0:T(8,128)(2,1)S(1)}, bf16[32,4096]{1,0:T(8,128)(2,1)S(1)}, u32[]{:S(2)}, u32[]{:S(2)}) collective-permute-start(bf16[32,4096]{1,0:T(8,128)(2,1)S(1)} %get-tuple-element.71), channel_id=1, source_target_pairs={{0,12},{4,8},{8,4},{12,0},{16,28},{20,24},{24,20},{28,16},{1,13},{... | collective-permute-start | bytes 786440 | tf_op jit(solution)/shard_map/ppermute | solution.py:405
  78.2 4.4 %collective-permute-start.7 = (bf16[32,4096]{1,0:T(8,128)(2,1)S(1)}, bf16[32,4096]{1,0:T(8,128)(2,1)S(1)}, u32[]{:S(2)}, u32[]{:S(2)}) collective-permute-start(bf16[32,4096]{1,0:T(8,128)(2,1)S(1)} %get-tuple-element.59), channel_id=1, source_target_pairs={{0,16},{4,20},{8,24},{12,28},{16,0},{20,4},{24,8},{28,12},{1,17},{... | collective-permute-start | bytes 786440 | tf_op jit(solution)/shard_map/ppermute | solution.py:405
  83.1 12.6 %collective-permute-done.18.refs_4_ = bf16[32,4096]{1,0:T(8,128)(2,1)S(1)} collective-permute-done((bf16[32,4096]{1,0:T(8,128)(2,1)S(1)}, bf16[32,4096]{1,0:T(8,128)(2,1)S(1)}, u32[]{:S(2)}, u32[]{:S(2)}) %collective-permute-start.18) | collective-permute-done | bytes 262176 | tf_op jit(solution)/shard_map/ppermute | solution.py:405
  95.7 4.3 %collective-permute-start.10 = (bf16[32,4096]{1,0:T(8,128)(2,1)S(1)}, bf16[32,4096]{1,0:T(8,128)(2,1)S(1)}, u32[]{:S(2)}, u32[]{:S(2)}) collective-permute-start(bf16[32,4096]{1,0:T(8,128)(2,1)S(1)} %get-tuple-element.62), channel_id=1, source_target_pairs={{0,8},{4,12},{8,0},{12,4},{16,24},{20,28},{24,16},{28,20},{1,9},{5... | collective-permute-start | bytes 786440 | tf_op jit(solution)/shard_map/ppermute | solution.py:405
  100.0 8.2 %collective-permute-done.20.refs_6_ = bf16[32,4096]{1,0:T(8,128)(2,1)S(1)} collective-permute-done((bf16[32,4096]{1,0:T(8,128)(2,1)S(1)}, bf16[32,4096]{1,0:T(8,128)(2,1)S(1)}, u32[]{:S(2)}, u32[]{:S(2)}) %collective-permute-start.20) | collective-permute-done | bytes 262176 | tf_op jit(solution)/shard_map/ppermute | solution.py:405
  109.7 7.8 %collective-permute-done.7.refs_0_ = bf16[32,4096]{1,0:T(8,128)(2,1)S(1)} collective-permute-done((bf16[32,4096]{1,0:T(8,128)(2,1)S(1)}, bf16[32,4096]{1,0:T(8,128)(2,1)S(1)}, u32[]{:S(2)}, u32[]{:S(2)}) %collective-permute-start.7) | collective-permute-done | bytes 262176 | tf_op jit(solution)/shard_map/ppermute | solution.py:405
  117.6 3.3 %collective-permute-start.12 = (bf16[32,4096]{1,0:T(8,128)(2,1)S(1)}, bf16[32,4096]{1,0:T(8,128)(2,1)S(1)}, u32[]{:S(2)}, u32[]{:S(2)}) collective-permute-start(bf16[32,4096]{1,0:T(8,128)(2,1)S(1)} %get-tuple-element.64), channel_id=1, source_target_pairs={{0,12},{4,8},{8,4},{12,0},{16,28},{20,24},{24,20},{28,16},{1,13},{... | collective-permute-start | bytes 786440 | tf_op jit(solution)/shard_map/ppermute | solution.py:405
  122.4 4.2 %gather.4 = (bf16[2,224,4096]{2,1,0:T(8,128)(2,1)S(1)}, f32[2,16,224]{2,1,0:T(8,128)S(1)}) custom-call(s32[1]{0:T(128)} %bitcast.me_ref, bf16[2,224,256]{2,1,0:T(8,128)(2,1)S(1)} %select_select_fusion.band_ref, f32[16,224]{1,0:T(8,128)S(1)} %fusion.6.fold_ref, f32[1,32768]{1,0:T(1,128)S(1)} %bitcast.30, bf16[3,32,32768]{2,1,0:T(8,128)(2,1)S(1)} %bitcast.23, ...), custom_call_target="tpu_custom_call" | custom-call | flops 1761607680 | bytes 5767168 | tf_op jit(solution)/shard_map/gather/pallas_call | solution.py:134
  128.5 6.6 %collective-permute-done.11.refs_4_ = bf16[32,4096]{1,0:T(8,128)(2,1)S(1)} collective-permute-done((bf16[32,4096]{1,0:T(8,128)(2,1)S(1)}, bf16[32,4096]{1,0:T(8,128)(2,1)S(1)}, u32[]{:S(2)}, u32[]{:S(2)}) %collective-permute-start.11) | collective-permute-done | bytes 262176 | tf_op jit(solution)/shard_map/ppermute | solution.py:405
  135.0 5.8 %collective-permute-done.13.refs_6_ = bf16[32,4096]{1,0:T(8,128)(2,1)S(1)} collective-permute-done((bf16[32,4096]{1,0:T(8,128)(2,1)S(1)}, bf16[32,4096]{1,0:T(8,128)(2,1)S(1)}, u32[]{:S(2)}, u32[]{:S(2)}) %collective-permute-start.13) | collective-permute-done | bytes 262176 | tf_op jit(solution)/shard_map/ppermute | solution.py:405
  140.8 2.6 gather.5
  146.1 2.4 collective-permute-done.22
  149.3 3.1 %collective-permute-done.23 = f32[2,16,224]{2,1,0:T(8,128)S(1)} collective-permute-done((f32[2,16,224]{2,1,0:T(8,128)S(1)}, f32[2,16,224]{2,1,0:T(8,128)S(1)}, u32[]{:S(2)}, u32[]{:S(2)}) %collective-permute-start.23) | collective-permute-done | bytes 28704 | tf_op jit(solution)/shard_map/ppermute | solution.py:416
  154.5 1.9 collective-permute-done.24
  156.4 2.3 collective-permute-start.25
  158.7 2.0 copy-done.3
  163.0 2.3 collective-permute-start.26
  171.6 11.2 %collective-permute-done.26.refs_1_ = bf16[4,4,2,4096]{3,2,1,0:T(2,128)(2,1)S(1)} collective-permute-done((bf16[4,4,2,4096]{3,2,1,0:T(2,128)(2,1)S(1)}, bf16[4,4,2,4096]{3,2,1,0:T(2,128)(2,1)S(1)}, u32[]{:S(2)}, u32[]{:S(2)}) %collective-permute-start.26) | collective-permute-done | bytes 262176 | tf_op jit(solution)/shard_map/ppermute | solution.py:405
  182.8 3.2 %collective-permute-start.31 = (bf16[4,4,2,4096]{3,2,1,0:T(2,128)(2,1)S(1)}, bf16[4,4,2,4096]{3,2,1,0:T(2,128)(2,1)S(1)}, u32[]{:S(2)}, u32[]{:S(2)}) collective-permute-start(bf16[4,4,2,4096]{3,2,1,0:T(2,128)(2,1)S(1)} %get-tuple-element.83), channel_id=1, source_target_pairs={{0,12},{4,8},{8,4},{12,0},{16,28},{20,24},{24,20},{28,16},{1,13},{... | collective-permute-start | bytes 786440 | tf_op jit(solution)/shard_map/ppermute | solution.py:405
  187.8 1.8 modes.5
  189.6 5.9 %collective-permute-done.28.refs_3_ = bf16[4,4,2,4096]{3,2,1,0:T(2,128)(2,1)S(1)} collective-permute-done((bf16[4,4,2,4096]{3,2,1,0:T(2,128)(2,1)S(1)}, bf16[4,4,2,4096]{3,2,1,0:T(2,128)(2,1)S(1)}, u32[]{:S(2)}, u32[]{:S(2)}) %collective-permute-start.28) | collective-permute-done | bytes 262176 | tf_op jit(solution)/shard_map/ppermute | solution.py:405
  195.5 7.6 %collective-permute-start.40 = (bf16[4,4,2,4096]{3,2,1,0:T(2,128)(2,1)S(1)}, bf16[4,4,2,4096]{3,2,1,0:T(2,128)(2,1)S(1)}, u32[]{:S(2)}, u32[]{:S(2)}) collective-permute-start(bf16[4,4,2,4096]{3,2,1,0:T(2,128)(2,1)S(1)} %get-tuple-element.95), channel_id=1, source_target_pairs={{0,16},{4,20},{8,24},{12,28},{16,0},{20,4},{24,8},{28,12},{1,17},{... | collective-permute-start | bytes 786440 | tf_op jit(solution)/shard_map/ppermute | solution.py:405
  204.6 8.0 %collective-permute-done.30.refs_5_ = bf16[4,4,2,4096]{3,2,1,0:T(2,128)(2,1)S(1)} collective-permute-done((bf16[4,4,2,4096]{3,2,1,0:T(2,128)(2,1)S(1)}, bf16[4,4,2,4096]{3,2,1,0:T(2,128)(2,1)S(1)}, u32[]{:S(2)}, u32[]{:S(2)}) %collective-permute-start.30) | collective-permute-done | bytes 262176 | tf_op jit(solution)/shard_map/ppermute | solution.py:405
  212.7 2.3 collective-permute-start.43
  214.9 11.8 %collective-permute-done.32.refs_7_ = bf16[4,4,2,4096]{3,2,1,0:T(2,128)(2,1)S(1)} collective-permute-done((bf16[4,4,2,4096]{3,2,1,0:T(2,128)(2,1)S(1)}, bf16[4,4,2,4096]{3,2,1,0:T(2,128)(2,1)S(1)}, u32[]{:S(2)}, u32[]{:S(2)}) %collective-permute-start.32) | collective-permute-done | bytes 262176 | tf_op jit(solution)/shard_map/ppermute | solution.py:405
  229.9 2.8 copy-done.1
  232.7 4.5 %again.1 = (bf16[4,4,2,4096]{3,2,1,0:T(2,128)(2,1)S(1)}, bf16[4,4,2,4096]{3,2,1,0:T(2,128)(2,1)S(1)}, bf16[4,4,2,4096]{3,2,1,0:T(2,128)(2,1)}, bf16[4,4,2,4096]{...) custom-call(s32[1]{0:T(128)} %bitcast.me_ref, ...), custom_call_target="tpu_custom_call" | custom-call | tf_op jit(solution)/shard_map/again/pallas_call | solution.py:347
  237.8 2.2 collective-permute-start.46
  240.0 3.1 %collective-permute-start.35 = (bf16[4,4,2,4096]{3,2,1,0:T(2,128)(2,1)S(1)}, bf16[4,4,2,4096]{3,2,1,0:T(2,128)(2,1)S(1)}, u32[]{:S(2)}, u32[]{:S(2)}) collective-permute-start(bf16[4,4,2,4096]{3,2,1,0:T(2,128)(2,1)S(1)} %get-tuple-element.88), channel_id=1, source_target_pairs={{0,16},{4,20},{8,24},{12,28},{16,0},{20,4},{24,8},{28,12},{1,17},{... | collective-permute-start | bytes 786440 | tf_op jit(solution)/shard_map/ppermute | solution.py:405
  244.6 13.0 %collective-permute-done.44.refs_5_ = bf16[4,4,2,4096]{3,2,1,0:T(2,128)(2,1)S(1)} collective-permute-done((bf16[4,4,2,4096]{3,2,1,0:T(2,128)(2,1)S(1)}, bf16[4,4,2,4096]{3,2,1,0:T(2,128)(2,1)S(1)}, u32[]{:S(2)}, u32[]{:S(2)}) %collective-permute-start.44) | collective-permute-done | bytes 262176 | tf_op jit(solution)/shard_map/ppermute | solution.py:405
  258.3 2.3 collective-permute-start.38
  260.6 8.2 %collective-permute-done.46.refs_7_ = bf16[4,4,2,4096]{3,2,1,0:T(2,128)(2,1)S(1)} collective-permute-done((bf16[4,4,2,4096]{3,2,1,0:T(2,128)(2,1)S(1)}, bf16[4,4,2,4096]{3,2,1,0:T(2,128)(2,1)S(1)}, u32[]{:S(2)}, u32[]{:S(2)}) %collective-permute-start.46) | collective-permute-done | bytes 262176 | tf_op jit(solution)/shard_map/ppermute | solution.py:405
  269.7 6.0 %collective-permute-done.35.refs_1_ = bf16[4,4,2,4096]{3,2,1,0:T(2,128)(2,1)S(1)} collective-permute-done((bf16[4,4,2,4096]{3,2,1,0:T(2,128)(2,1)S(1)}, bf16[4,4,2,4096]{3,2,1,0:T(2,128)(2,1)S(1)}, u32[]{:S(2)}, u32[]{:S(2)}) %collective-permute-start.35) | collective-permute-done | bytes 262176 | tf_op jit(solution)/shard_map/ppermute | solution.py:405
  275.7 3.1 %collective-permute-start.33 = (bf16[4,4,2,4096]{3,2,1,0:T(2,128)(2,1)}, bf16[4,4,2,4096]{3,2,1,0:T(2,128)(2,1)S(1)}, u32[]{:S(2)}, u32[]{:S(2)}) collective-permute-start(bf16[4,4,2,4096]{3,2,1,0:T(2,128)(2,1)} %get-tuple-element.85), channel_id=1, source_target_pairs={{0,12},{4,8},{8,4},{12,0},{16,28},{20,24},{24,20},{28,16},{1,13},{... | collective-permute-start | bytes 786440 | tf_op jit(solution)/shard_map/ppermute | solution.py:405
  284.3 10.0 %collective-permute-done.39.refs_5_ = bf16[4,4,2,4096]{3,2,1,0:T(2,128)(2,1)} collective-permute-done((bf16[4,4,2,4096]{3,2,1,0:T(2,128)(2,1)}, bf16[4,4,2,4096]{3,2,1,0:T(2,128)(2,1)}, u32[]{:S(2)}, u32[]{:S(2)}) %collective-permute-start.39) | collective-permute-done | bytes 262176 | tf_op jit(solution)/shard_map/ppermute | solution.py:405
  294.3 2.1 place.6.refs_2_
  (134 shorter events, 53.8 us)
Async XLA Ops:
  2.3 20.6 %collective-permute-start = (bf16[32,4096]{1,0:T(8,128)(2,1)}, bf16[32,4096]{1,0:T(8,128)(2,1)S(1)}, u32[]{:S(2)}, u32[]{:S(2)}) collective-permute-start(bf16[32,4096]{1,0:T(8,128)(2,1)} %pick.4), channel_id=1, source_target_pairs={{0,16},{4,20},{8,24},{12,28},{16,0},{20,4},{24,8},{28,12},{1,17},{... | collective-permute-start | bytes 786440 | tf_op jit(solution)/shard_map/ppermute | solution.py:405
  7.6 22.1 %collective-permute-start.1 = (bf16[32,4096]{1,0:T(8,128)(2,1)}, bf16[32,4096]{1,0:T(8,128)(2,1)S(1)}, u32[]{:S(2)}, u32[]{:S(2)}) collective-permute-start(bf16[32,4096]{1,0:T(8,128)(2,1)} %get-tuple-element.52), channel_id=1, source_target_pairs={{0,4},{4,0},{8,12},{12,8},{16,20},{20,16},{24,28},{28,24},{1,5},{5... | collective-permute-start | bytes 786440 | tf_op jit(solution)/shard_map/ppermute | solution.py:405
  9.1 25.0 %collective-permute-start.2 = (bf16[32,4096]{1,0:T(8,128)(2,1)}, bf16[32,4096]{1,0:T(8,128)(2,1)S(1)}, u32[]{:S(2)}, u32[]{:S(2)}) collective-permute-start(bf16[32,4096]{1,0:T(8,128)(2,1)} %get-tuple-element.53), channel_id=1, source_target_pairs={{0,20},{4,16},{8,28},{12,24},{16,4},{20,0},{24,12},{28,8},{1,21},{... | collective-permute-start | bytes 786440 | tf_op jit(solution)/shard_map/ppermute | solution.py:405
  9.5 29.3 %collective-permute-start.3 = (bf16[32,4096]{1,0:T(8,128)(2,1)}, bf16[32,4096]{1,0:T(8,128)(2,1)S(1)}, u32[]{:S(2)}, u32[]{:S(2)}) collective-permute-start(bf16[32,4096]{1,0:T(8,128)(2,1)} %get-tuple-element.54), channel_id=1, source_target_pairs={{0,8},{4,12},{8,0},{12,4},{16,24},{20,28},{24,16},{28,20},{1,9},{5... | collective-permute-start | bytes 786440 | tf_op jit(solution)/shard_map/ppermute | solution.py:405
  9.6 41.1 %collective-permute-start.4 = (bf16[32,4096]{1,0:T(8,128)(2,1)}, bf16[32,4096]{1,0:T(8,128)(2,1)S(1)}, u32[]{:S(2)}, u32[]{:S(2)}) collective-permute-start(bf16[32,4096]{1,0:T(8,128)(2,1)} %get-tuple-element.55), channel_id=1, source_target_pairs={{0,24},{4,28},{8,16},{12,20},{16,8},{20,12},{24,0},{28,4},{1,25},{... | collective-permute-start | bytes 786440 | tf_op jit(solution)/shard_map/ppermute | solution.py:405
  22.9 27.8 %collective-permute-start.5 = (bf16[32,4096]{1,0:T(8,128)(2,1)}, bf16[32,4096]{1,0:T(8,128)(2,1)S(1)}, u32[]{:S(2)}, u32[]{:S(2)}) collective-permute-start(bf16[32,4096]{1,0:T(8,128)(2,1)} %get-tuple-element.56), channel_id=1, source_target_pairs={{0,12},{4,8},{8,4},{12,0},{16,28},{20,24},{24,20},{28,16},{1,13},{... | collective-permute-start | bytes 786440 | tf_op jit(solution)/shard_map/ppermute | solution.py:405
  29.7 33.5 %collective-permute-start.6 = (bf16[32,4096]{1,0:T(8,128)(2,1)S(1)}, bf16[32,4096]{1,0:T(8,128)(2,1)S(1)}, u32[]{:S(2)}, u32[]{:S(2)}) collective-permute-start(bf16[32,4096]{1,0:T(8,128)(2,1)S(1)} %copy-done.11), channel_id=1, source_target_pairs={{0,28},{4,24},{8,20},{12,16},{16,12},{20,8},{24,4},{28,0},{1,29},{... | collective-permute-start | bytes 786440 | tf_op jit(solution)/shard_map/ppermute | solution.py:405
  34.2 38.4 %collective-permute-start.14 = (bf16[32,4096]{1,0:T(8,128)(2,1)S(1)}, bf16[32,4096]{1,0:T(8,128)(2,1)S(1)}, u32[]{:S(2)}, u32[]{:S(2)}) collective-permute-start(bf16[32,4096]{1,0:T(8,128)(2,1)S(1)} %get-tuple-element.66), channel_id=1, source_target_pairs={{0,16},{4,20},{8,24},{12,28},{16,0},{20,4},{24,8},{28,12},{1,17},{... | collective-permute-start | bytes 786440 | tf_op jit(solution)/shard_map/ppermute | solution.py:405
  38.7 37.2 %collective-permute-start.15 = (bf16[32,4096]{1,0:T(8,128)(2,1)S(1)}, bf16[32,4096]{1,0:T(8,128)(2,1)S(1)}, u32[]{:S(2)}, u32[]{:S(2)}) collective-permute-start(bf16[32,4096]{1,0:T(8,128)(2,1)S(1)} %get-tuple-element.67), channel_id=1, source_target_pairs={{0,4},{4,0},{8,12},{12,8},{16,20},{20,16},{24,28},{28,24},{1,5},{5... | collective-permute-start | bytes 786440 | tf_op jit(solution)/shard_map/ppermute | solution.py:405
  50.7 27.6 %collective-permute-start.16 = (bf16[32,4096]{1,0:T(8,128)(2,1)S(1)}, bf16[32,4096]{1,0:T(8,128)(2,1)S(1)}, u32[]{:S(2)}, u32[]{:S(2)}) collective-permute-start(bf16[32,4096]{1,0:T(8,128)(2,1)S(1)} %get-tuple-element.68), channel_id=1, source_target_pairs={{0,20},{4,16},{8,28},{12,24},{16,4},{20,0},{24,12},{28,8},{1,21},{... | collective-permute-start | bytes 786440 | tf_op jit(solution)/shard_map/ppermute | solution.py:405
  50.7 31.9 %collective-permute-start.17 = (bf16[32,4096]{1,0:T(8,128)(2,1)S(1)}, bf16[32,4096]{1,0:T(8,128)(2,1)S(1)}, u32[]{:S(2)}, u32[]{:S(2)}) collective-permute-start(bf16[32,4096]{1,0:T(8,128)(2,1)S(1)} %get-tuple-element.69), channel_id=1, source_target_pairs={{0,8},{4,12},{8,0},{12,4},{16,24},{20,28},{24,16},{28,20},{1,9},{5... | collective-permute-start | bytes 786440 | tf_op jit(solution)/shard_map/ppermute | solution.py:405
  63.2 32.5 %collective-permute-start.18 = (bf16[32,4096]{1,0:T(8,128)(2,1)S(1)}, bf16[32,4096]{1,0:T(8,128)(2,1)S(1)}, u32[]{:S(2)}, u32[]{:S(2)}) collective-permute-start(bf16[32,4096]{1,0:T(8,128)(2,1)S(1)} %get-tuple-element.70), channel_id=1, source_target_pairs={{0,24},{4,28},{8,16},{12,20},{16,8},{20,12},{24,0},{28,4},{1,25},{... | collective-permute-start | bytes 786440 | tf_op jit(solution)/shard_map/ppermute | solution.py:405
  72.6 23.1 %collective-permute-start.19 = (bf16[32,4096]{1,0:T(8,128)(2,1)S(1)}, bf16[32,4096]{1,0:T(8,128)(2,1)S(1)}, u32[]{:S(2)}, u32[]{:S(2)}) collective-permute-start(bf16[32,4096]{1,0:T(8,128)(2,1)S(1)} %get-tuple-element.71), channel_id=1, source_target_pairs={{0,12},{4,8},{8,4},{12,0},{16,28},{20,24},{24,20},{28,16},{1,13},{... | collective-permute-start | bytes 786440 | tf_op jit(solution)/shard_map/ppermute | solution.py:405
  75.9 32.3 %collective-permute-start.20 = (bf16[32,4096]{1,0:T(8,128)(2,1)S(1)}, bf16[32,4096]{1,0:T(8,128)(2,1)S(1)}, u32[]{:S(2)}, u32[]{:S(2)}) collective-permute-start(bf16[32,4096]{1,0:T(8,128)(2,1)S(1)} %get-tuple-element.72), channel_id=1, source_target_pairs={{0,28},{4,24},{8,20},{12,16},{16,12},{20,8},{24,4},{28,0},{1,29},{... | collective-permute-start | bytes 786440 | tf_op jit(solution)/shard_map/ppermute | solution.py:405
  78.2 39.3 %collective-permute-start.7 = (bf16[32,4096]{1,0:T(8,128)(2,1)S(1)}, bf16[32,4096]{1,0:T(8,128)(2,1)S(1)}, u32[]{:S(2)}, u32[]{:S(2)}) collective-permute-start(bf16[32,4096]{1,0:T(8,128)(2,1)S(1)} %get-tuple-element.59), channel_id=1, source_target_pairs={{0,16},{4,20},{8,24},{12,28},{16,0},{20,4},{24,8},{28,12},{1,17},{... | collective-permute-start | bytes 786440 | tf_op jit(solution)/shard_map/ppermute | solution.py:405
  82.6 38.3 %collective-permute-start.8 = (bf16[32,4096]{1,0:T(8,128)(2,1)S(1)}, bf16[32,4096]{1,0:T(8,128)(2,1)S(1)}, u32[]{:S(2)}, u32[]{:S(2)}) collective-permute-start(bf16[32,4096]{1,0:T(8,128)(2,1)S(1)} %get-tuple-element.60), channel_id=1, source_target_pairs={{0,4},{4,0},{8,12},{12,8},{16,20},{20,16},{24,28},{28,24},{1,5},{5... | collective-permute-start | bytes 786440 | tf_op jit(solution)/shard_map/ppermute | solution.py:405
  95.7 32.8 %collective-permute-start.9 = (bf16[32,4096]{1,0:T(8,128)(2,1)S(1)}, bf16[32,4096]{1,0:T(8,128)(2,1)S(1)}, u32[]{:S(2)}, u32[]{:S(2)}) collective-permute-start(bf16[32,4096]{1,0:T(8,128)(2,1)S(1)} %get-tuple-element.61), channel_id=1, source_target_pairs={{0,20},{4,16},{8,28},{12,24},{16,4},{20,0},{24,12},{28,8},{1,21},{... | collective-permute-start | bytes 786440 | tf_op jit(solution)/shard_map/ppermute | solution.py:405
  95.7 32.8 %collective-permute-start.10 = (bf16[32,4096]{1,0:T(8,128)(2,1)S(1)}, bf16[32,4096]{1,0:T(8,128)(2,1)S(1)}, u32[]{:S(2)}, u32[]{:S(2)}) collective-permute-start(bf16[32,4096]{1,0:T(8,128)(2,1)S(1)} %get-tuple-element.62), channel_id=1, source_target_pairs={{0,8},{4,12},{8,0},{12,4},{16,24},{20,28},{24,16},{28,20},{1,9},{5... | collective-permute-start | bytes 786440 | tf_op jit(solution)/shard_map/ppermute | solution.py:405
  108.2 26.9 %collective-permute-start.11 = (bf16[32,4096]{1,0:T(8,128)(2,1)S(1)}, bf16[32,4096]{1,0:T(8,128)(2,1)S(1)}, u32[]{:S(2)}, u32[]{:S(2)}) collective-permute-start(bf16[32,4096]{1,0:T(8,128)(2,1)S(1)} %get-tuple-element.63), channel_id=1, source_target_pairs={{0,24},{4,28},{8,16},{12,20},{16,8},{20,12},{24,0},{28,4},{1,25},{... | collective-permute-start | bytes 786440 | tf_op jit(solution)/shard_map/ppermute | solution.py:405
  117.6 17.5 %collective-permute-start.12 = (bf16[32,4096]{1,0:T(8,128)(2,1)S(1)}, bf16[32,4096]{1,0:T(8,128)(2,1)S(1)}, u32[]{:S(2)}, u32[]{:S(2)}) collective-permute-start(bf16[32,4096]{1,0:T(8,128)(2,1)S(1)} %get-tuple-element.64), channel_id=1, source_target_pairs={{0,12},{4,8},{8,4},{12,0},{16,28},{20,24},{24,20},{28,16},{1,13},{... | collective-permute-start | bytes 786440 | tf_op jit(solution)/shard_map/ppermute | solution.py:405
  120.9 19.9 %collective-permute-start.13 = (bf16[32,4096]{1,0:T(8,128)(2,1)S(1)}, bf16[32,4096]{1,0:T(8,128)(2,1)S(1)}, u32[]{:S(2)}, u32[]{:S(2)}) collective-permute-start(bf16[32,4096]{1,0:T(8,128)(2,1)S(1)} %get-tuple-element.65), channel_id=1, source_target_pairs={{0,28},{4,24},{8,20},{12,16},{16,12},{20,8},{24,4},{28,0},{1,29},{... | collective-permute-start | bytes 786440 | tf_op jit(solution)/shard_map/ppermute | solution.py:405
  143.4 1.2 collective-permute-start.21
  144.6 3.9 %collective-permute-start.22 = (f32[2,16,224]{2,1,0:T(8,128)S(1)}, f32[2,16,224]{2,1,0:T(8,128)S(1)}, u32[]{:S(2)}, u32[]{:S(2)}) collective-permute-start(f32[2,16,224]{2,1,0:T(8,128)S(1)} %add.125), channel_id=1, source_target_pairs={{0,2},{1,3},{2,0},{3,1},{4,6},{5,7},{6,4},{7,5},{8,10},{9,11},{10,... | collective-permute-start | bytes 86024 | tf_op jit(solution)/shard_map/ppermute | solution.py:416
  148.5 3.9 %collective-permute-start.23 = (f32[2,16,224]{2,1,0:T(8,128)S(1)}, f32[2,16,224]{2,1,0:T(8,128)S(1)}, u32[]{:S(2)}, u32[]{:S(2)}) collective-permute-start(f32[2,16,224]{2,1,0:T(8,128)S(1)} %add.126.after_ref), channel_id=1, source_target_pairs={{0,4},{4,0},{8,12},{12,8},{16,20},{20,16},{24,28},{28,24},{1,5},{5... | collective-permute-start | bytes 86024 | tf_op jit(solution)/shard_map/ppermute | solution.py:416
  152.4 3.9 %collective-permute-start.24 = (f32[2,16,224]{2,1,0:T(8,128)S(1)}, f32[2,16,224]{2,1,0:T(8,128)S(1)}, u32[]{:S(2)}, u32[]{:S(2)}) collective-permute-start(f32[2,16,224]{2,1,0:T(8,128)S(1)} %add.127), channel_id=1, source_target_pairs={{0,8},{4,12},{8,0},{12,4},{16,24},{20,28},{24,16},{28,20},{1,9},{5... | collective-permute-start | bytes 86024 | tf_op jit(solution)/shard_map/ppermute | solution.py:416
  156.4 4.8 %collective-permute-start.25 = (f32[2,16,224]{2,1,0:T(8,128)S(1)}, f32[2,16,224]{2,1,0:T(8,128)S(1)}, u32[]{:S(2)}, u32[]{:S(2)}) collective-permute-start(f32[2,16,224]{2,1,0:T(8,128)S(1)} %add.128), channel_id=1, source_target_pairs={{0,16},{4,20},{8,24},{12,28},{16,0},{20,4},{24,8},{28,12},{1,17},{... | collective-permute-start | bytes 86024 | tf_op jit(solution)/shard_map/ppermute | solution.py:416
  163.0 19.9 %collective-permute-start.26 = (bf16[4,4,2,4096]{3,2,1,0:T(2,128)(2,1)S(1)}, bf16[4,4,2,4096]{3,2,1,0:T(2,128)(2,1)S(1)}, u32[]{:S(2)}, u32[]{:S(2)}) collective-permute-start(bf16[4,4,2,4096]{3,2,1,0:T(2,128)(2,1)S(1)} %get-tuple-element.78), channel_id=1, source_target_pairs={{0,16},{4,20},{8,24},{12,28},{16,0},{20,4},{24,8},{28,12},{1,17},{... | collective-permute-start | bytes 786440 | tf_op jit(solution)/shard_map/ppermute | solution.py:405
  166.6 62.3 %slice-start = ((s8[6291456]{0:T(1024)(128)(4,1)}), s8[4194304]{0:T(1024)(128)(4,1)S(1)}, s32[]{:S(2)}) async-start(s8[6291456]{0:T(1024)(128)(4,1)} %bitcast.25), calls=%async_computation | async-start | bytes 8388608
  166.6 19.5 %collective-permute-start.27 = (bf16[4,4,2,4096]{3,2,1,0:T(2,128)(2,1)S(1)}, bf16[4,4,2,4096]{3,2,1,0:T(2,128)(2,1)S(1)}, u32[]{:S(2)}, u32[]{:S(2)}) collective-permute-start(bf16[4,4,2,4096]{3,2,1,0:T(2,128)(2,1)S(1)} %get-tuple-element.79), channel_id=1, source_target_pairs={{0,4},{4,0},{8,12},{12,8},{16,20},{20,16},{24,28},{28,24},{1,5},{5... | collective-permute-start | bytes 786440 | tf_op jit(solution)/shard_map/ppermute | solution.py:405
  167.2 28.3 %collective-permute-start.28 = (bf16[4,4,2,4096]{3,2,1,0:T(2,128)(2,1)S(1)}, bf16[4,4,2,4096]{3,2,1,0:T(2,128)(2,1)S(1)}, u32[]{:S(2)}, u32[]{:S(2)}) collective-permute-start(bf16[4,4,2,4096]{3,2,1,0:T(2,128)(2,1)S(1)} %get-tuple-element.80), channel_id=1, source_target_pairs={{0,20},{4,16},{8,28},{12,24},{16,4},{20,0},{24,12},{28,8},{1,21},{... | collective-permute-start | bytes 786440 | tf_op jit(solution)/shard_map/ppermute | solution.py:405
  168.8 34.4 %collective-permute-start.29 = (bf16[4,4,2,4096]{3,2,1,0:T(2,128)(2,1)S(1)}, bf16[4,4,2,4096]{3,2,1,0:T(2,128)(2,1)S(1)}, u32[]{:S(2)}, u32[]{:S(2)}) collective-permute-start(bf16[4,4,2,4096]{3,2,1,0:T(2,128)(2,1)S(1)} %get-tuple-element.81), channel_id=1, source_target_pairs={{0,8},{4,12},{8,0},{12,4},{16,24},{20,28},{24,16},{28,20},{1,9},{5... | collective-permute-start | bytes 786440 | tf_op jit(solution)/shard_map/ppermute | solution.py:405
  170.4 42.3 %collective-permute-start.30 = (bf16[4,4,2,4096]{3,2,1,0:T(2,128)(2,1)S(1)}, bf16[4,4,2,4096]{3,2,1,0:T(2,128)(2,1)S(1)}, u32[]{:S(2)}, u32[]{:S(2)}) collective-permute-start(bf16[4,4,2,4096]{3,2,1,0:T(2,128)(2,1)S(1)} %get-tuple-element.82), channel_id=1, source_target_pairs={{0,24},{4,28},{8,16},{12,20},{16,8},{20,12},{24,0},{28,4},{1,25},{... | collective-permute-start | bytes 786440 | tf_op jit(solution)/shard_map/ppermute | solution.py:405
  182.8 29.8 %collective-permute-start.31 = (bf16[4,4,2,4096]{3,2,1,0:T(2,128)(2,1)S(1)}, bf16[4,4,2,4096]{3,2,1,0:T(2,128)(2,1)S(1)}, u32[]{:S(2)}, u32[]{:S(2)}) collective-permute-start(bf16[4,4,2,4096]{3,2,1,0:T(2,128)(2,1)S(1)} %get-tuple-element.83), channel_id=1, source_target_pairs={{0,12},{4,8},{8,4},{12,0},{16,28},{20,24},{24,20},{28,16},{1,13},{... | collective-permute-start | bytes 786440 | tf_op jit(solution)/shard_map/ppermute | solution.py:405
  186.1 40.6 %collective-permute-start.32 = (bf16[4,4,2,4096]{3,2,1,0:T(2,128)(2,1)S(1)}, bf16[4,4,2,4096]{3,2,1,0:T(2,128)(2,1)S(1)}, u32[]{:S(2)}, u32[]{:S(2)}) collective-permute-start(bf16[4,4,2,4096]{3,2,1,0:T(2,128)(2,1)S(1)} %get-tuple-element.84), channel_id=1, source_target_pairs={{0,28},{4,24},{8,20},{12,16},{16,12},{20,8},{24,4},{28,0},{1,29},{... | collective-permute-start | bytes 786440 | tf_op jit(solution)/shard_map/ppermute | solution.py:405
  195.5 42.3 %collective-permute-start.40 = (bf16[4,4,2,4096]{3,2,1,0:T(2,128)(2,1)S(1)}, bf16[4,4,2,4096]{3,2,1,0:T(2,128)(2,1)S(1)}, u32[]{:S(2)}, u32[]{:S(2)}) collective-permute-start(bf16[4,4,2,4096]{3,2,1,0:T(2,128)(2,1)S(1)} %get-tuple-element.95), channel_id=1, source_target_pairs={{0,16},{4,20},{8,24},{12,28},{16,0},{20,4},{24,8},{28,12},{1,17},{... | collective-permute-start | bytes 786440 | tf_op jit(solution)/shard_map/ppermute | solution.py:405
  203.2 34.7 %collective-permute-start.41 = (bf16[4,4,2,4096]{3,2,1,0:T(2,128)(2,1)S(1)}, bf16[4,4,2,4096]{3,2,1,0:T(2,128)(2,1)S(1)}, u32[]{:S(2)}, u32[]{:S(2)}) collective-permute-start(bf16[4,4,2,4096]{3,2,1,0:T(2,128)(2,1)S(1)} %get-tuple-element.96), channel_id=1, source_target_pairs={{0,4},{4,0},{8,12},{12,8},{16,20},{20,16},{24,28},{28,24},{1,5},{5... | collective-permute-start | bytes 786440 | tf_op jit(solution)/shard_map/ppermute | solution.py:405
  212.7 27.4 %collective-permute-start.42 = (bf16[4,4,2,4096]{3,2,1,0:T(2,128)(2,1)S(1)}, bf16[4,4,2,4096]{3,2,1,0:T(2,128)(2,1)S(1)}, u32[]{:S(2)}, u32[]{:S(2)}) collective-permute-start(bf16[4,4,2,4096]{3,2,1,0:T(2,128)(2,1)S(1)} %get-tuple-element.97), channel_id=1, source_target_pairs={{0,20},{4,16},{8,28},{12,24},{16,4},{20,0},{24,12},{28,8},{1,21},{... | collective-permute-start | bytes 786440 | tf_op jit(solution)/shard_map/ppermute | solution.py:405
  212.7 30.4 %collective-permute-start.43 = (bf16[4,4,2,4096]{3,2,1,0:T(2,128)(2,1)S(1)}, bf16[4,4,2,4096]{3,2,1,0:T(2,128)(2,1)S(1)}, u32[]{:S(2)}, u32[]{:S(2)}) collective-permute-start(bf16[4,4,2,4096]{3,2,1,0:T(2,128)(2,1)S(1)} %get-tuple-element.98), channel_id=1, source_target_pairs={{0,8},{4,12},{8,0},{12,4},{16,24},{20,28},{24,16},{28,20},{1,9},{5... | collective-permute-start | bytes 786440 | tf_op jit(solution)/shard_map/ppermute | solution.py:405
  226.7 30.9 %collective-permute-start.44 = (bf16[4,4,2,4096]{3,2,1,0:T(2,128)(2,1)S(1)}, bf16[4,4,2,4096]{3,2,1,0:T(2,128)(2,1)S(1)}, u32[]{:S(2)}, u32[]{:S(2)}) collective-permute-start(bf16[4,4,2,4096]{3,2,1,0:T(2,128)(2,1)S(1)} %get-tuple-element.99), channel_id=1, source_target_pairs={{0,24},{4,28},{8,16},{12,20},{16,8},{20,12},{24,0},{28,4},{1,25},{... | collective-permute-start | bytes 786440 | tf_op jit(solution)/shard_map/ppermute | solution.py:405
  237.8 20.5 %collective-permute-start.45 = (bf16[4,4,2,4096]{3,2,1,0:T(2,128)(2,1)S(1)}, bf16[4,4,2,4096]{3,2,1,0:T(2,128)(2,1)S(1)}, u32[]{:S(2)}, u32[]{:S(2)}) collective-permute-start(bf16[4,4,2,4096]{3,2,1,0:T(2,128)(2,1)S(1)} %get-tuple-element.100), channel_id=1, source_target_pairs={{0,12},{4,8},{8,4},{12,0},{16,28},{20,24},{24,20},{28,16},{1,13},{... | collective-permute-start | bytes 786440 | tf_op jit(solution)/shard_map/ppermute | solution.py:405
  237.8 31.0 %collective-permute-start.46 = (bf16[4,4,2,4096]{3,2,1,0:T(2,128)(2,1)S(1)}, bf16[4,4,2,4096]{3,2,1,0:T(2,128)(2,1)S(1)}, u32[]{:S(2)}, u32[]{:S(2)}) collective-permute-start(bf16[4,4,2,4096]{3,2,1,0:T(2,128)(2,1)S(1)} %get-tuple-element.101), channel_id=1, source_target_pairs={{0,28},{4,24},{8,20},{12,16},{16,12},{20,8},{24,4},{28,0},{1,29},{... | collective-permute-start | bytes 786440 | tf_op jit(solution)/shard_map/ppermute | solution.py:405
  240.0 35.6 %collective-permute-start.35 = (bf16[4,4,2,4096]{3,2,1,0:T(2,128)(2,1)S(1)}, bf16[4,4,2,4096]{3,2,1,0:T(2,128)(2,1)S(1)}, u32[]{:S(2)}, u32[]{:S(2)}) collective-permute-start(bf16[4,4,2,4096]{3,2,1,0:T(2,128)(2,1)S(1)} %get-tuple-element.88), channel_id=1, source_target_pairs={{0,16},{4,20},{8,24},{12,28},{16,0},{20,4},{24,8},{28,12},{1,17},{... | collective-permute-start | bytes 786440 | tf_op jit(solution)/shard_map/ppermute | solution.py:405
  243.1 35.6 %collective-permute-start.36 = (bf16[4,4,2,4096]{3,2,1,0:T(2,128)(2,1)S(1)}, bf16[4,4,2,4096]{3,2,1,0:T(2,128)(2,1)S(1)}, u32[]{:S(2)}, u32[]{:S(2)}) collective-permute-start(bf16[4,4,2,4096]{3,2,1,0:T(2,128)(2,1)S(1)} %get-tuple-element.89), channel_id=1, source_target_pairs={{0,4},{4,0},{8,12},{12,8},{16,20},{20,16},{24,28},{28,24},{1,5},{5... | collective-permute-start | bytes 786440 | tf_op jit(solution)/shard_map/ppermute | solution.py:405
  258.3 26.0 %collective-permute-start.37 = (bf16[4,4,2,4096]{3,2,1,0:T(2,128)(2,1)}, bf16[4,4,2,4096]{3,2,1,0:T(2,128)(2,1)S(1)}, u32[]{:S(2)}, u32[]{:S(2)}) collective-permute-start(bf16[4,4,2,4096]{3,2,1,0:T(2,128)(2,1)} %get-tuple-element.90), channel_id=1, source_target_pairs={{0,20},{4,16},{8,28},{12,24},{16,4},{20,0},{24,12},{28,8},{1,21},{... | collective-permute-start | bytes 786440 | tf_op jit(solution)/shard_map/ppermute | solution.py:405
  258.3 26.0 %collective-permute-start.38 = (bf16[4,4,2,4096]{3,2,1,0:T(2,128)(2,1)}, bf16[4,4,2,4096]{3,2,1,0:T(2,128)(2,1)S(1)}, u32[]{:S(2)}, u32[]{:S(2)}) collective-permute-start(bf16[4,4,2,4096]{3,2,1,0:T(2,128)(2,1)} %get-tuple-element.91), channel_id=1, source_target_pairs={{0,8},{4,12},{8,0},{12,4},{16,24},{20,28},{24,16},{28,20},{1,9},{5... | collective-permute-start | bytes 786440 | tf_op jit(solution)/shard_map/ppermute | solution.py:405
  268.8 25.4 %collective-permute-start.39 = (bf16[4,4,2,4096]{3,2,1,0:T(2,128)(2,1)}, bf16[4,4,2,4096]{3,2,1,0:T(2,128)(2,1)}, u32[]{:S(2)}, u32[]{:S(2)}) collective-permute-start(bf16[4,4,2,4096]{3,2,1,0:T(2,128)(2,1)} %get-tuple-element.92), channel_id=1, source_target_pairs={{0,24},{4,28},{8,16},{12,20},{16,8},{20,12},{24,0},{28,4},{1,25},{... | collective-permute-start | bytes 786440 | tf_op jit(solution)/shard_map/ppermute | solution.py:405
  275.7 20.8 %collective-permute-start.33 = (bf16[4,4,2,4096]{3,2,1,0:T(2,128)(2,1)}, bf16[4,4,2,4096]{3,2,1,0:T(2,128)(2,1)S(1)}, u32[]{:S(2)}, u32[]{:S(2)}) collective-permute-start(bf16[4,4,2,4096]{3,2,1,0:T(2,128)(2,1)} %get-tuple-element.85), channel_id=1, source_target_pairs={{0,12},{4,8},{8,4},{12,0},{16,28},{20,24},{24,20},{28,16},{1,13},{... | collective-permute-start | bytes 786440 | tf_op jit(solution)/shard_map/ppermute | solution.py:405
  278.7 19.4 %collective-permute-start.34 = (bf16[4,4,2,4096]{3,2,1,0:T(2,128)(2,1)}, bf16[4,4,2,4096]{3,2,1,0:T(2,128)(2,1)}, u32[]{:S(2)}, u32[]{:S(2)}) collective-permute-start(bf16[4,4,2,4096]{3,2,1,0:T(2,128)(2,1)} %get-tuple-element.86), channel_id=1, source_target_pairs={{0,28},{4,24},{8,20},{12,16},{16,12},{20,8},{24,4},{28,0},{1,29},{... | collective-permute-start | bytes 786440 | tf_op jit(solution)/shard_map/ppermute | solution.py:405
  (15 other events, 158.7 us)

commit v6 on v5

--- a/solution.py
+++ b/solution.py
@@ -160,16 +160,18 @@
     )(me, band, fold, weights, own, *landed, before)
 
 
-def solve_kernel(blocks, me_ref, scale_ref, sums_ref, start_ref, tile_ref, mix_ref, energy_ref):
+def solve_kernel(blocks, me_ref, scale_ref, sums_ref, others_ref, start_ref, tile_ref, mix_ref, energy_ref):
     devices = mix_ref.shape[0]
     freqs = mix_ref.shape[1] // (2 * MODES)
     padded = sums_ref.shape[1] // 2
     gram_scale = scale_ref[0]
     factor = scale_ref[1]
 
+    total = [sums_ref[g] + others_ref[g] for g in range(GROUPS)]
+
     def lanes(block, part):
         place = (2 * block + part) * PER_GROUP
-        return jnp.concatenate([sums_ref[g, :, place : place + PER_GROUP] for g in range(GROUPS)], 1)
+        return jnp.concatenate([total[g][:, place : place + PER_GROUP] for g in range(GROUPS)], 1)
 
     real, imag = [], []
     for block in range(blocks):
@@ -236,12 +238,12 @@
             mix_ref[jnp.bitwise_xor(me, device)] = jnp.concatenate(pieces, 0).astype(jnp.bfloat16)
 
 
-def solve(me, scales, sums, start, tiles, devices):
+def solve(me, scales, sums, others, start, tiles, devices):
     freqs = NF // devices
     rows = sums.shape[2]
     return pl.pallas_call(
         functools.partial(solve_kernel, devices - 1),
-        in_specs=[pl.BlockSpec(memory_space=pltpu.SMEM)] * 2 + [pl.BlockSpec(memory_space=pltpu.VMEM)] * 3,
+        in_specs=[pl.BlockSpec(memory_space=pltpu.SMEM)] * 2 + [pl.BlockSpec(memory_space=pltpu.VMEM)] * 4,
         out_specs=[pl.BlockSpec(memory_space=pltpu.VMEM)] * 2,
         out_shape=[
             jax.ShapeDtypeStruct((devices, freqs * MODES * 2, rows), jnp.bfloat16),
@@ -249,7 +251,7 @@
         ],
         compiler_params=pltpu.CompilerParams(vmem_limit_bytes=vmem(devices)),
         name="solve",
-    )(me, scales, sums, start, tiles)
+    )(me, scales, sums, others, start, tiles)
 
 
 def fetch_kernel(spectra_ref, after_ref, out_ref, sem):
@@ -409,10 +411,10 @@
     return [send(piece, turn, devices) for piece, turn in zip(pieces, turns(devices)[1:])]
 
 
-def sum_over(value, axis):
+def sum_over(value, axis, whole=True):
     count = lax.axis_size(axis)
     step = 1
-    while step < count:
+    while step < (count if whole else count // 2):
         value = value + lax.ppermute(value, axis, [(d, d ^ step) for d in range(count)])
         step *= 2
     return value
@@ -468,8 +470,9 @@
         history.append(sums)
     sums = sum_over(sums, "space")
     ready = fetch(spectra[0], sums, devices)
-    sums = sum_over(sums, "tm")
-    mix, energies = solve(me, scales, sums, start_table, tiles, devices)
+    sums = sum_over(sums, "tm", False)
+    others = lax.ppermute(sums, "tm", [(d, d ^ (devices // 2)) for d in range(devices)])
+    mix, energies = solve(me, scales, sums, others, start_table, tiles, devices)
     placed = [None]
     shape = (freqs, MODES, comps, 2, cells)
     for chunk in CHUNKS_OUT:

time: 301 us -> 301 us (level)
    ppermute x5 -> x4, waiting for transfers between devices: 8.77 us -> 8.58 us  [sum_over(): lax.ppermute(value, axis, [(d, d ^ step) for d in range(count)])]
where the time goes in v6:
time: 301 us; the launch traced here: 300 us
  waiting for transfers between devices  159 us (53%)
  starting transfers between devices  87.7 us (29%)
  Pallas kernels  31.8 us (11%)
  local copies, waits for them, and re-layouts  18.2 us (6%)
    ppermute x42, waiting for transfers between devices, send(): return lax.ppermute(value, 'tm', [(d, d ^ turn) for d in range(devices)])  150 us
    ppermute x42, starting transfers between devices, send(): return lax.ppermute(value, 'tm', [(d, d ^ turn) for d in range(devices)])  83.3 us
    unnamed x33, local copies, waits for them, and re-layouts  15.2 us
    pallas_call x3, Pallas kernels, gather(): pl.pallas_call(functools.partial(gather_kernel, count), grid_spec=pltpu.P...  11 us
    ppermute x4, waiting for transfers between devices, sum_over(): lax.ppermute(value, axis, [(d, d ^ step) for d in range(count)])  8.58 us
    pallas_call x4, Pallas kernels, place(): pl.pallas_call(functools.partial(place_kernel, [piece[1:] for piece in pi...  6.63 us
  transfers between devices with their start and end apart: 47, of which 26 were waited for; matrix products, arithmetic and copies ran while one was open for 2% of the time, Pallas kernels for 8%

profile of v6, /device:TPU:8, one launch (start us, length us, event | category | flops | bytes accessed | tf_op | source)
XLA Modules:
  0.0 300.1 jit_solution(14081864722569030113)
XLA Ops:
  2.3 2.7 collective-permute-start
  5.0 2.6 pick.5
  9.6 3.0 %collective-permute-start.4 = (bf16[32,4096]{1,0:T(8,128)(2,1)}, bf16[32,4096]{1,0:T(8,128)(2,1)S(1)}, u32[]{:S(2)}, u32[]{:S(2)}) collective-permute-start(bf16[32,4096]{1,0:T(8,128)(2,1)} %get-tuple-element.55), channel_id=1, source_target_pairs={{0,24},{4,28},{8,16},{12,20},{16,8},{20,12},{24,0},{28,4},{1,25},{... | collective-permute-start | bytes 786440 | tf_op jit(solution)/shard_map/ppermute | solution.py:407
  15.8 7.1 %collective-permute-done.refs_0_ = bf16[32,4096]{1,0:T(8,128)(2,1)S(1)} collective-permute-done((bf16[32,4096]{1,0:T(8,128)(2,1)}, bf16[32,4096]{1,0:T(8,128)(2,1)S(1)}, u32[]{:S(2)}, u32[]{:S(2)}) %collective-permute-start) | collective-permute-done | bytes 262176 | tf_op jit(solution)/shard_map/ppermute | solution.py:407
  22.9 3.7 %collective-permute-start.5 = (bf16[32,4096]{1,0:T(8,128)(2,1)}, bf16[32,4096]{1,0:T(8,128)(2,1)S(1)}, u32[]{:S(2)}, u32[]{:S(2)}) collective-permute-start(bf16[32,4096]{1,0:T(8,128)(2,1)} %get-tuple-element.56), channel_id=1, source_target_pairs={{0,12},{4,8},{8,4},{12,0},{16,28},{20,24},{24,20},{28,16},{1,13},{... | collective-permute-start | bytes 786440 | tf_op jit(solution)/shard_map/ppermute | solution.py:407
  26.6 2.8 copy-done
  31.1 3.1 %collective-permute-done.2.refs_2_ = bf16[32,4096]{1,0:T(8,128)(2,1)S(1)} collective-permute-done((bf16[32,4096]{1,0:T(8,128)(2,1)}, bf16[32,4096]{1,0:T(8,128)(2,1)S(1)}, u32[]{:S(2)}, u32[]{:S(2)}) %collective-permute-start.2) | collective-permute-done | bytes 262176 | tf_op jit(solution)/shard_map/ppermute | solution.py:407
  34.2 4.5 %collective-permute-start.14 = (bf16[32,4096]{1,0:T(8,128)(2,1)S(1)}, bf16[32,4096]{1,0:T(8,128)(2,1)S(1)}, u32[]{:S(2)}, u32[]{:S(2)}) collective-permute-start(bf16[32,4096]{1,0:T(8,128)(2,1)S(1)} %get-tuple-element.66), channel_id=1, source_target_pairs={{0,16},{4,20},{8,24},{12,28},{16,0},{20,4},{24,8},{28,12},{1,17},{... | collective-permute-start | bytes 786440 | tf_op jit(solution)/shard_map/ppermute | solution.py:407
  39.3 11.4 %collective-permute-done.4.refs_4_ = bf16[32,4096]{1,0:T(8,128)(2,1)S(1)} collective-permute-done((bf16[32,4096]{1,0:T(8,128)(2,1)}, bf16[32,4096]{1,0:T(8,128)(2,1)S(1)}, u32[]{:S(2)}, u32[]{:S(2)}) %collective-permute-start.4) | collective-permute-done | bytes 262176 | tf_op jit(solution)/shard_map/ppermute | solution.py:407
  50.7 4.3 %collective-permute-start.17 = (bf16[32,4096]{1,0:T(8,128)(2,1)S(1)}, bf16[32,4096]{1,0:T(8,128)(2,1)S(1)}, u32[]{:S(2)}, u32[]{:S(2)}) collective-permute-start(bf16[32,4096]{1,0:T(8,128)(2,1)S(1)} %get-tuple-element.69), channel_id=1, source_target_pairs={{0,8},{4,12},{8,0},{12,4},{16,24},{20,28},{24,16},{28,20},{1,9},{5... | collective-permute-start | bytes 786440 | tf_op jit(solution)/shard_map/ppermute | solution.py:407
  55.0 8.2 %collective-permute-done.6.refs_6_ = bf16[32,4096]{1,0:T(8,128)(2,1)S(1)} collective-permute-done((bf16[32,4096]{1,0:T(8,128)(2,1)S(1)}, bf16[32,4096]{1,0:T(8,128)(2,1)S(1)}, u32[]{:S(2)}, u32[]{:S(2)}) %collective-permute-start.6) | collective-permute-done | bytes 262176 | tf_op jit(solution)/shard_map/ppermute | solution.py:407
  64.8 4.2 %gather.3 = (bf16[2,224,4096]{2,1,0:T(8,128)(2,1)S(1)}, f32[2,16,224]{2,1,0:T(8,128)S(1)}) custom-call(s32[1]{0:T(128)} %bitcast.me_ref, bf16[2,224,256]{2,1,0:T(8,128)(2,1)S(1)} %select_select_fusion.band_ref, f32[16,224]{1,0:T(8,128)S(1)} %fusion.6.fold_ref, f32[1,32768]{1,0:T(1,128)S(1)} %bitcast.29, bf16[3,32,32768]{2,1,0:T(8,128)(2,1)S(1)} %bitcast.21, ...), custom_call_target="tpu_custom_call" | custom-call | flops 1761607680 | bytes 5767168 | tf_op jit(solution)/shard_map/gather/pallas_call | solution.py:134
  72.6 3.3 %collective-permute-start.19 = (bf16[32,4096]{1,0:T(8,128)(2,1)S(1)}, bf16[32,4096]{1,0:T(8,128)(2,1)S(1)}, u32[]{:S(2)}, u32[]{:S(2)}) collective-permute-start(bf16[32,4096]{1,0:T(8,128)(2,1)S(1)} %get-tuple-element.71), channel_id=1, source_target_pairs={{0,12},{4,8},{8,4},{12,0},{16,28},{20,24},{24,20},{28,16},{1,13},{... | collective-permute-start | bytes 786440 | tf_op jit(solution)/shard_map/ppermute | solution.py:407
  78.2 4.4 %collective-permute-start.7 = (bf16[32,4096]{1,0:T(8,128)(2,1)S(1)}, bf16[32,4096]{1,0:T(8,128)(2,1)S(1)}, u32[]{:S(2)}, u32[]{:S(2)}) collective-permute-start(bf16[32,4096]{1,0:T(8,128)(2,1)S(1)} %get-tuple-element.59), channel_id=1, source_target_pairs={{0,16},{4,20},{8,24},{12,28},{16,0},{20,4},{24,8},{28,12},{1,17},{... | collective-permute-start | bytes 786440 | tf_op jit(solution)/shard_map/ppermute | solution.py:407
  83.1 12.6 %collective-permute-done.18.refs_4_ = bf16[32,4096]{1,0:T(8,128)(2,1)S(1)} collective-permute-done((bf16[32,4096]{1,0:T(8,128)(2,1)S(1)}, bf16[32,4096]{1,0:T(8,128)(2,1)S(1)}, u32[]{:S(2)}, u32[]{:S(2)}) %collective-permute-start.18) | collective-permute-done | bytes 262176 | tf_op jit(solution)/shard_map/ppermute | solution.py:407
  95.7 4.3 %collective-permute-start.10 = (bf16[32,4096]{1,0:T(8,128)(2,1)S(1)}, bf16[32,4096]{1,0:T(8,128)(2,1)S(1)}, u32[]{:S(2)}, u32[]{:S(2)}) collective-permute-start(bf16[32,4096]{1,0:T(8,128)(2,1)S(1)} %get-tuple-element.62), channel_id=1, source_target_pairs={{0,8},{4,12},{8,0},{12,4},{16,24},{20,28},{24,16},{28,20},{1,9},{5... | collective-permute-start | bytes 786440 | tf_op jit(solution)/shard_map/ppermute | solution.py:407
  100.0 8.2 %collective-permute-done.20.refs_6_ = bf16[32,4096]{1,0:T(8,128)(2,1)S(1)} collective-permute-done((bf16[32,4096]{1,0:T(8,128)(2,1)S(1)}, bf16[32,4096]{1,0:T(8,128)(2,1)S(1)}, u32[]{:S(2)}, u32[]{:S(2)}) %collective-permute-start.20) | collective-permute-done | bytes 262176 | tf_op jit(solution)/shard_map/ppermute | solution.py:407
  109.7 7.8 %collective-permute-done.7.refs_0_ = bf16[32,4096]{1,0:T(8,128)(2,1)S(1)} collective-permute-done((bf16[32,4096]{1,0:T(8,128)(2,1)S(1)}, bf16[32,4096]{1,0:T(8,128)(2,1)S(1)}, u32[]{:S(2)}, u32[]{:S(2)}) %collective-permute-start.7) | collective-permute-done | bytes 262176 | tf_op jit(solution)/shard_map/ppermute | solution.py:407
  117.6 3.3 %collective-permute-start.12 = (bf16[32,4096]{1,0:T(8,128)(2,1)S(1)}, bf16[32,4096]{1,0:T(8,128)(2,1)S(1)}, u32[]{:S(2)}, u32[]{:S(2)}) collective-permute-start(bf16[32,4096]{1,0:T(8,128)(2,1)S(1)} %get-tuple-element.64), channel_id=1, source_target_pairs={{0,12},{4,8},{8,4},{12,0},{16,28},{20,24},{24,20},{28,16},{1,13},{... | collective-permute-start | bytes 786440 | tf_op jit(solution)/shard_map/ppermute | solution.py:407
  122.4 4.2 %gather.4 = (bf16[2,224,4096]{2,1,0:T(8,128)(2,1)S(1)}, f32[2,16,224]{2,1,0:T(8,128)S(1)}) custom-call(s32[1]{0:T(128)} %bitcast.me_ref, bf16[2,224,256]{2,1,0:T(8,128)(2,1)S(1)} %select_select_fusion.band_ref, f32[16,224]{1,0:T(8,128)S(1)} %fusion.6.fold_ref, f32[1,32768]{1,0:T(1,128)S(1)} %bitcast.30, bf16[3,32,32768]{2,1,0:T(8,128)(2,1)S(1)} %bitcast.23, ...), custom_call_target="tpu_custom_call" | custom-call | flops 1761607680 | bytes 5767168 | tf_op jit(solution)/shard_map/gather/pallas_call | solution.py:134
  128.5 6.6 %collective-permute-done.11.refs_4_ = bf16[32,4096]{1,0:T(8,128)(2,1)S(1)} collective-permute-done((bf16[32,4096]{1,0:T(8,128)(2,1)S(1)}, bf16[32,4096]{1,0:T(8,128)(2,1)S(1)}, u32[]{:S(2)}, u32[]{:S(2)}) %collective-permute-start.11) | collective-permute-done | bytes 262176 | tf_op jit(solution)/shard_map/ppermute | solution.py:407
  135.0 5.8 %collective-permute-done.13.refs_6_ = bf16[32,4096]{1,0:T(8,128)(2,1)S(1)} collective-permute-done((bf16[32,4096]{1,0:T(8,128)(2,1)S(1)}, bf16[32,4096]{1,0:T(8,128)(2,1)S(1)}, u32[]{:S(2)}, u32[]{:S(2)}) %collective-permute-start.13) | collective-permute-done | bytes 262176 | tf_op jit(solution)/shard_map/ppermute | solution.py:407
  140.8 2.6 gather.5
  146.1 2.4 collective-permute-done.22
  149.3 3.1 %collective-permute-done.23 = f32[2,16,224]{2,1,0:T(8,128)S(1)} collective-permute-done((f32[2,16,224]{2,1,0:T(8,128)S(1)}, f32[2,16,224]{2,1,0:T(8,128)S(1)}, u32[]{:S(2)}, u32[]{:S(2)}) %collective-permute-start.23) | collective-permute-done | bytes 28704 | tf_op jit(solution)/shard_map/ppermute | solution.py:418
  154.5 1.9 collective-permute-done.24
  156.4 2.3 collective-permute-start.25
  158.7 2.0 copy-done.3
  163.0 2.3 collective-permute-start.26
  171.6 11.3 %collective-permute-done.26.refs_1_ = bf16[4,4,2,4096]{3,2,1,0:T(2,128)(2,1)S(1)} collective-permute-done((bf16[4,4,2,4096]{3,2,1,0:T(2,128)(2,1)S(1)}, bf16[4,4,2,4096]{3,2,1,0:T(2,128)(2,1)S(1)}, u32[]{:S(2)}, u32[]{:S(2)}) %collective-permute-start.26) | collective-permute-done | bytes 262176 | tf_op jit(solution)/shard_map/ppermute | solution.py:407
  182.9 3.2 %collective-permute-start.31 = (bf16[4,4,2,4096]{3,2,1,0:T(2,128)(2,1)S(1)}, bf16[4,4,2,4096]{3,2,1,0:T(2,128)(2,1)S(1)}, u32[]{:S(2)}, u32[]{:S(2)}) collective-permute-start(bf16[4,4,2,4096]{3,2,1,0:T(2,128)(2,1)S(1)} %get-tuple-element.83), channel_id=1, source_target_pairs={{0,12},{4,8},{8,4},{12,0},{16,28},{20,24},{24,20},{28,16},{1,13},{... | collective-permute-start | bytes 786440 | tf_op jit(solution)/shard_map/ppermute | solution.py:407
  187.8 1.8 modes.5
  189.6 5.9 %collective-permute-done.28.refs_3_ = bf16[4,4,2,4096]{3,2,1,0:T(2,128)(2,1)S(1)} collective-permute-done((bf16[4,4,2,4096]{3,2,1,0:T(2,128)(2,1)S(1)}, bf16[4,4,2,4096]{3,2,1,0:T(2,128)(2,1)S(1)}, u32[]{:S(2)}, u32[]{:S(2)}) %collective-permute-start.28) | collective-permute-done | bytes 262176 | tf_op jit(solution)/shard_map/ppermute | solution.py:407
  195.5 7.6 %collective-permute-start.40 = (bf16[4,4,2,4096]{3,2,1,0:T(2,128)(2,1)S(1)}, bf16[4,4,2,4096]{3,2,1,0:T(2,128)(2,1)S(1)}, u32[]{:S(2)}, u32[]{:S(2)}) collective-permute-start(bf16[4,4,2,4096]{3,2,1,0:T(2,128)(2,1)S(1)} %get-tuple-element.95), channel_id=1, source_target_pairs={{0,16},{4,20},{8,24},{12,28},{16,0},{20,4},{24,8},{28,12},{1,17},{... | collective-permute-start | bytes 786440 | tf_op jit(solution)/shard_map/ppermute | solution.py:407
  204.6 8.0 %collective-permute-done.30.refs_5_ = bf16[4,4,2,4096]{3,2,1,0:T(2,128)(2,1)S(1)} collective-permute-done((bf16[4,4,2,4096]{3,2,1,0:T(2,128)(2,1)S(1)}, bf16[4,4,2,4096]{3,2,1,0:T(2,128)(2,1)S(1)}, u32[]{:S(2)}, u32[]{:S(2)}) %collective-permute-start.30) | collective-permute-done | bytes 262176 | tf_op jit(solution)/shard_map/ppermute | solution.py:407
  212.7 2.3 collective-permute-start.43
  214.9 11.7 %collective-permute-done.32.refs_7_ = bf16[4,4,2,4096]{3,2,1,0:T(2,128)(2,1)S(1)} collective-permute-done((bf16[4,4,2,4096]{3,2,1,0:T(2,128)(2,1)S(1)}, bf16[4,4,2,4096]{3,2,1,0:T(2,128)(2,1)S(1)}, u32[]{:S(2)}, u32[]{:S(2)}) %collective-permute-start.32) | collective-permute-done | bytes 262176 | tf_op jit(solution)/shard_map/ppermute | solution.py:407
  229.9 2.8 copy-done.1
  232.7 4.5 %again.1 = (bf16[4,4,2,4096]{3,2,1,0:T(2,128)(2,1)S(1)}, bf16[4,4,2,4096]{3,2,1,0:T(2,128)(2,1)S(1)}, bf16[4,4,2,4096]{3,2,1,0:T(2,128)(2,1)}, bf16[4,4,2,4096]{...) custom-call(s32[1]{0:T(128)} %bitcast.me_ref, ...), custom_call_target="tpu_custom_call" | custom-call | tf_op jit(solution)/shard_map/again/pallas_call | solution.py:349
  237.8 2.2 collective-permute-start.46
  240.0 3.1 %collective-permute-start.35 = (bf16[4,4,2,4096]{3,2,1,0:T(2,128)(2,1)S(1)}, bf16[4,4,2,4096]{3,2,1,0:T(2,128)(2,1)S(1)}, u32[]{:S(2)}, u32[]{:S(2)}) collective-permute-start(bf16[4,4,2,4096]{3,2,1,0:T(2,128)(2,1)S(1)} %get-tuple-element.88), channel_id=1, source_target_pairs={{0,16},{4,20},{8,24},{12,28},{16,0},{20,4},{24,8},{28,12},{1,17},{... | collective-permute-start | bytes 786440 | tf_op jit(solution)/shard_map/ppermute | solution.py:407
  244.6 13.0 %collective-permute-done.44.refs_5_ = bf16[4,4,2,4096]{3,2,1,0:T(2,128)(2,1)S(1)} collective-permute-done((bf16[4,4,2,4096]{3,2,1,0:T(2,128)(2,1)S(1)}, bf16[4,4,2,4096]{3,2,1,0:T(2,128)(2,1)S(1)}, u32[]{:S(2)}, u32[]{:S(2)}) %collective-permute-start.44) | collective-permute-done | bytes 262176 | tf_op jit(solution)/shard_map/ppermute | solution.py:407
  258.3 2.3 collective-permute-start.38
  260.6 8.2 %collective-permute-done.46.refs_7_ = bf16[4,4,2,4096]{3,2,1,0:T(2,128)(2,1)S(1)} collective-permute-done((bf16[4,4,2,4096]{3,2,1,0:T(2,128)(2,1)S(1)}, bf16[4,4,2,4096]{3,2,1,0:T(2,128)(2,1)S(1)}, u32[]{:S(2)}, u32[]{:S(2)}) %collective-permute-start.46) | collective-permute-done | bytes 262176 | tf_op jit(solution)/shard_map/ppermute | solution.py:407
  269.7 6.0 %collective-permute-done.35.refs_1_ = bf16[4,4,2,4096]{3,2,1,0:T(2,128)(2,1)S(1)} collective-permute-done((bf16[4,4,2,4096]{3,2,1,0:T(2,128)(2,1)S(1)}, bf16[4,4,2,4096]{3,2,1,0:T(2,128)(2,1)S(1)}, u32[]{:S(2)}, u32[]{:S(2)}) %collective-permute-start.35) | collective-permute-done | bytes 262176 | tf_op jit(solution)/shard_map/ppermute | solution.py:407
  275.7 3.0 %collective-permute-start.33 = (bf16[4,4,2,4096]{3,2,1,0:T(2,128)(2,1)}, bf16[4,4,2,4096]{3,2,1,0:T(2,128)(2,1)S(1)}, u32[]{:S(2)}, u32[]{:S(2)}) collective-permute-start(bf16[4,4,2,4096]{3,2,1,0:T(2,128)(2,1)} %get-tuple-element.85), channel_id=1, source_target_pairs={{0,12},{4,8},{8,4},{12,0},{16,28},{20,24},{24,20},{28,16},{1,13},{... | collective-permute-start | bytes 786440 | tf_op jit(solution)/shard_map/ppermute | solution.py:407
  284.3 10.0 %collective-permute-done.39.refs_5_ = bf16[4,4,2,4096]{3,2,1,0:T(2,128)(2,1)} collective-permute-done((bf16[4,4,2,4096]{3,2,1,0:T(2,128)(2,1)}, bf16[4,4,2,4096]{3,2,1,0:T(2,128)(2,1)}, u32[]{:S(2)}, u32[]{:S(2)}) %collective-permute-start.39) | collective-permute-done | bytes 262176 | tf_op jit(solution)/shard_map/ppermute | solution.py:407
  294.3 2.1 place.6.refs_2_
  (133 shorter events, 53.9 us)
Async XLA Ops:
  2.3 20.6 %collective-permute-start = (bf16[32,4096]{1,0:T(8,128)(2,1)}, bf16[32,4096]{1,0:T(8,128)(2,1)S(1)}, u32[]{:S(2)}, u32[]{:S(2)}) collective-permute-start(bf16[32,4096]{1,0:T(8,128)(2,1)} %pick.4), channel_id=1, source_target_pairs={{0,16},{4,20},{8,24},{12,28},{16,0},{20,4},{24,8},{28,12},{1,17},{... | collective-permute-start | bytes 786440 | tf_op jit(solution)/shard_map/ppermute | solution.py:407
  7.6 22.1 %collective-permute-start.1 = (bf16[32,4096]{1,0:T(8,128)(2,1)}, bf16[32,4096]{1,0:T(8,128)(2,1)S(1)}, u32[]{:S(2)}, u32[]{:S(2)}) collective-permute-start(bf16[32,4096]{1,0:T(8,128)(2,1)} %get-tuple-element.52), channel_id=1, source_target_pairs={{0,4},{4,0},{8,12},{12,8},{16,20},{20,16},{24,28},{28,24},{1,5},{5... | collective-permute-start | bytes 786440 | tf_op jit(solution)/shard_map/ppermute | solution.py:407
  9.1 25.0 %collective-permute-start.2 = (bf16[32,4096]{1,0:T(8,128)(2,1)}, bf16[32,4096]{1,0:T(8,128)(2,1)S(1)}, u32[]{:S(2)}, u32[]{:S(2)}) collective-permute-start(bf16[32,4096]{1,0:T(8,128)(2,1)} %get-tuple-element.53), channel_id=1, source_target_pairs={{0,20},{4,16},{8,28},{12,24},{16,4},{20,0},{24,12},{28,8},{1,21},{... | collective-permute-start | bytes 786440 | tf_op jit(solution)/shard_map/ppermute | solution.py:407
  9.5 29.3 %collective-permute-start.3 = (bf16[32,4096]{1,0:T(8,128)(2,1)}, bf16[32,4096]{1,0:T(8,128)(2,1)S(1)}, u32[]{:S(2)}, u32[]{:S(2)}) collective-permute-start(bf16[32,4096]{1,0:T(8,128)(2,1)} %get-tuple-element.54), channel_id=1, source_target_pairs={{0,8},{4,12},{8,0},{12,4},{16,24},{20,28},{24,16},{28,20},{1,9},{5... | collective-permute-start | bytes 786440 | tf_op jit(solution)/shard_map/ppermute | solution.py:407
  9.6 41.1 %collective-permute-start.4 = (bf16[32,4096]{1,0:T(8,128)(2,1)}, bf16[32,4096]{1,0:T(8,128)(2,1)S(1)}, u32[]{:S(2)}, u32[]{:S(2)}) collective-permute-start(bf16[32,4096]{1,0:T(8,128)(2,1)} %get-tuple-element.55), channel_id=1, source_target_pairs={{0,24},{4,28},{8,16},{12,20},{16,8},{20,12},{24,0},{28,4},{1,25},{... | collective-permute-start | bytes 786440 | tf_op jit(solution)/shard_map/ppermute | solution.py:407
  22.9 27.8 %collective-permute-start.5 = (bf16[32,4096]{1,0:T(8,128)(2,1)}, bf16[32,4096]{1,0:T(8,128)(2,1)S(1)}, u32[]{:S(2)}, u32[]{:S(2)}) collective-permute-start(bf16[32,4096]{1,0:T(8,128)(2,1)} %get-tuple-element.56), channel_id=1, source_target_pairs={{0,12},{4,8},{8,4},{12,0},{16,28},{20,24},{24,20},{28,16},{1,13},{... | collective-permute-start | bytes 786440 | tf_op jit(solution)/shard_map/ppermute | solution.py:407
  29.7 33.5 %collective-permute-start.6 = (bf16[32,4096]{1,0:T(8,128)(2,1)S(1)}, bf16[32,4096]{1,0:T(8,128)(2,1)S(1)}, u32[]{:S(2)}, u32[]{:S(2)}) collective-permute-start(bf16[32,4096]{1,0:T(8,128)(2,1)S(1)} %copy-done.11), channel_id=1, source_target_pairs={{0,28},{4,24},{8,20},{12,16},{16,12},{20,8},{24,4},{28,0},{1,29},{... | collective-permute-start | bytes 786440 | tf_op jit(solution)/shard_map/ppermute | solution.py:407
  34.2 38.4 %collective-permute-start.14 = (bf16[32,4096]{1,0:T(8,128)(2,1)S(1)}, bf16[32,4096]{1,0:T(8,128)(2,1)S(1)}, u32[]{:S(2)}, u32[]{:S(2)}) collective-permute-start(bf16[32,4096]{1,0:T(8,128)(2,1)S(1)} %get-tuple-element.66), channel_id=1, source_target_pairs={{0,16},{4,20},{8,24},{12,28},{16,0},{20,4},{24,8},{28,12},{1,17},{... | collective-permute-start | bytes 786440 | tf_op jit(solution)/shard_map/ppermute | solution.py:407
  38.7 37.2 %collective-permute-start.15 = (bf16[32,4096]{1,0:T(8,128)(2,1)S(1)}, bf16[32,4096]{1,0:T(8,128)(2,1)S(1)}, u32[]{:S(2)}, u32[]{:S(2)}) collective-permute-start(bf16[32,4096]{1,0:T(8,128)(2,1)S(1)} %get-tuple-element.67), channel_id=1, source_target_pairs={{0,4},{4,0},{8,12},{12,8},{16,20},{20,16},{24,28},{28,24},{1,5},{5... | collective-permute-start | bytes 786440 | tf_op jit(solution)/shard_map/ppermute | solution.py:407
  50.7 27.6 %collective-permute-start.16 = (bf16[32,4096]{1,0:T(8,128)(2,1)S(1)}, bf16[32,4096]{1,0:T(8,128)(2,1)S(1)}, u32[]{:S(2)}, u32[]{:S(2)}) collective-permute-start(bf16[32,4096]{1,0:T(8,128)(2,1)S(1)} %get-tuple-element.68), channel_id=1, source_target_pairs={{0,20},{4,16},{8,28},{12,24},{16,4},{20,0},{24,12},{28,8},{1,21},{... | collective-permute-start | bytes 786440 | tf_op jit(solution)/shard_map/ppermute | solution.py:407
  50.7 31.9 %collective-permute-start.17 = (bf16[32,4096]{1,0:T(8,128)(2,1)S(1)}, bf16[32,4096]{1,0:T(8,128)(2,1)S(1)}, u32[]{:S(2)}, u32[]{:S(2)}) collective-permute-start(bf16[32,4096]{1,0:T(8,128)(2,1)S(1)} %get-tuple-element.69), channel_id=1, source_target_pairs={{0,8},{4,12},{8,0},{12,4},{16,24},{20,28},{24,16},{28,20},{1,9},{5... | collective-permute-start | bytes 786440 | tf_op jit(solution)/shard_map/ppermute | solution.py:407
  63.2 32.5 %collective-permute-start.18 = (bf16[32,4096]{1,0:T(8,128)(2,1)S(1)}, bf16[32,4096]{1,0:T(8,128)(2,1)S(1)}, u32[]{:S(2)}, u32[]{:S(2)}) collective-permute-start(bf16[32,4096]{1,0:T(8,128)(2,1)S(1)} %get-tuple-element.70), channel_id=1, source_target_pairs={{0,24},{4,28},{8,16},{12,20},{16,8},{20,12},{24,0},{28,4},{1,25},{... | collective-permute-start | bytes 786440 | tf_op jit(solution)/shard_map/ppermute | solution.py:407
  72.6 23.1 %collective-permute-start.19 = (bf16[32,4096]{1,0:T(8,128)(2,1)S(1)}, bf16[32,4096]{1,0:T(8,128)(2,1)S(1)}, u32[]{:S(2)}, u32[]{:S(2)}) collective-permute-start(bf16[32,4096]{1,0:T(8,128)(2,1)S(1)} %get-tuple-element.71), channel_id=1, source_target_pairs={{0,12},{4,8},{8,4},{12,0},{16,28},{20,24},{24,20},{28,16},{1,13},{... | collective-permute-start | bytes 786440 | tf_op jit(solution)/shard_map/ppermute | solution.py:407
  75.9 32.3 %collective-permute-start.20 = (bf16[32,4096]{1,0:T(8,128)(2,1)S(1)}, bf16[32,4096]{1,0:T(8,128)(2,1)S(1)}, u32[]{:S(2)}, u32[]{:S(2)}) collective-permute-start(bf16[32,4096]{1,0:T(8,128)(2,1)S(1)} %get-tuple-element.72), channel_id=1, source_target_pairs={{0,28},{4,24},{8,20},{12,16},{16,12},{20,8},{24,4},{28,0},{1,29},{... | collective-permute-start | bytes 786440 | tf_op jit(solution)/shard_map/ppermute | solution.py:407
  78.2 39.3 %collective-permute-start.7 = (bf16[32,4096]{1,0:T(8,128)(2,1)S(1)}, bf16[32,4096]{1,0:T(8,128)(2,1)S(1)}, u32[]{:S(2)}, u32[]{:S(2)}) collective-permute-start(bf16[32,4096]{1,0:T(8,128)(2,1)S(1)} %get-tuple-element.59), channel_id=1, source_target_pairs={{0,16},{4,20},{8,24},{12,28},{16,0},{20,4},{24,8},{28,12},{1,17},{... | collective-permute-start | bytes 786440 | tf_op jit(solution)/shard_map/ppermute | solution.py:407
  82.6 38.3 %collective-permute-start.8 = (bf16[32,4096]{1,0:T(8,128)(2,1)S(1)}, bf16[32,4096]{1,0:T(8,128)(2,1)S(1)}, u32[]{:S(2)}, u32[]{:S(2)}) collective-permute-start(bf16[32,4096]{1,0:T(8,128)(2,1)S(1)} %get-tuple-element.60), channel_id=1, source_target_pairs={{0,4},{4,0},{8,12},{12,8},{16,20},{20,16},{24,28},{28,24},{1,5},{5... | collective-permute-start | bytes 786440 | tf_op jit(solution)/shard_map/ppermute | solution.py:407
  95.7 32.8 %collective-permute-start.9 = (bf16[32,4096]{1,0:T(8,128)(2,1)S(1)}, bf16[32,4096]{1,0:T(8,128)(2,1)S(1)}, u32[]{:S(2)}, u32[]{:S(2)}) collective-permute-start(bf16[32,4096]{1,0:T(8,128)(2,1)S(1)} %get-tuple-element.61), channel_id=1, source_target_pairs={{0,20},{4,16},{8,28},{12,24},{16,4},{20,0},{24,12},{28,8},{1,21},{... | collective-permute-start | bytes 786440 | tf_op jit(solution)/shard_map/ppermute | solution.py:407
  95.7 32.8 %collective-permute-start.10 = (bf16[32,4096]{1,0:T(8,128)(2,1)S(1)}, bf16[32,4096]{1,0:T(8,128)(2,1)S(1)}, u32[]{:S(2)}, u32[]{:S(2)}) collective-permute-start(bf16[32,4096]{1,0:T(8,128)(2,1)S(1)} %get-tuple-element.62), channel_id=1, source_target_pairs={{0,8},{4,12},{8,0},{12,4},{16,24},{20,28},{24,16},{28,20},{1,9},{5... | collective-permute-start | bytes 786440 | tf_op jit(solution)/shard_map/ppermute | solution.py:407
  108.2 26.9 %collective-permute-start.11 = (bf16[32,4096]{1,0:T(8,128)(2,1)S(1)}, bf16[32,4096]{1,0:T(8,128)(2,1)S(1)}, u32[]{:S(2)}, u32[]{:S(2)}) collective-permute-start(bf16[32,4096]{1,0:T(8,128)(2,1)S(1)} %get-tuple-element.63), channel_id=1, source_target_pairs={{0,24},{4,28},{8,16},{12,20},{16,8},{20,12},{24,0},{28,4},{1,25},{... | collective-permute-start | bytes 786440 | tf_op jit(solution)/shard_map/ppermute | solution.py:407
  117.6 17.5 %collective-permute-start.12 = (bf16[32,4096]{1,0:T(8,128)(2,1)S(1)}, bf16[32,4096]{1,0:T(8,128)(2,1)S(1)}, u32[]{:S(2)}, u32[]{:S(2)}) collective-permute-start(bf16[32,4096]{1,0:T(8,128)(2,1)S(1)} %get-tuple-element.64), channel_id=1, source_target_pairs={{0,12},{4,8},{8,4},{12,0},{16,28},{20,24},{24,20},{28,16},{1,13},{... | collective-permute-start | bytes 786440 | tf_op jit(solution)/shard_map/ppermute | solution.py:407
  120.9 19.9 %collective-permute-start.13 = (bf16[32,4096]{1,0:T(8,128)(2,1)S(1)}, bf16[32,4096]{1,0:T(8,128)(2,1)S(1)}, u32[]{:S(2)}, u32[]{:S(2)}) collective-permute-start(bf16[32,4096]{1,0:T(8,128)(2,1)S(1)} %get-tuple-element.65), channel_id=1, source_target_pairs={{0,28},{4,24},{8,20},{12,16},{16,12},{20,8},{24,4},{28,0},{1,29},{... | collective-permute-start | bytes 786440 | tf_op jit(solution)/shard_map/ppermute | solution.py:407
  143.4 1.2 collective-permute-start.21
  144.6 3.9 %collective-permute-start.22 = (f32[2,16,224]{2,1,0:T(8,128)S(1)}, f32[2,16,224]{2,1,0:T(8,128)S(1)}, u32[]{:S(2)}, u32[]{:S(2)}) collective-permute-start(f32[2,16,224]{2,1,0:T(8,128)S(1)} %add.122), channel_id=1, source_target_pairs={{0,2},{1,3},{2,0},{3,1},{4,6},{5,7},{6,4},{7,5},{8,10},{9,11},{10,... | collective-permute-start | bytes 86024 | tf_op jit(solution)/shard_map/ppermute | solution.py:418
  148.5 3.9 %collective-permute-start.23 = (f32[2,16,224]{2,1,0:T(8,128)S(1)}, f32[2,16,224]{2,1,0:T(8,128)S(1)}, u32[]{:S(2)}, u32[]{:S(2)}) collective-permute-start(f32[2,16,224]{2,1,0:T(8,128)S(1)} %add.123.after_ref), channel_id=1, source_target_pairs={{0,4},{4,0},{8,12},{12,8},{16,20},{20,16},{24,28},{28,24},{1,5},{5... | collective-permute-start | bytes 86024 | tf_op jit(solution)/shard_map/ppermute | solution.py:418
  152.4 3.9 %collective-permute-start.24 = (f32[2,16,224]{2,1,0:T(8,128)S(1)}, f32[2,16,224]{2,1,0:T(8,128)S(1)}, u32[]{:S(2)}, u32[]{:S(2)}) collective-permute-start(f32[2,16,224]{2,1,0:T(8,128)S(1)} %add.124), channel_id=1, source_target_pairs={{0,8},{4,12},{8,0},{12,4},{16,24},{20,28},{24,16},{28,20},{1,9},{5... | collective-permute-start | bytes 86024 | tf_op jit(solution)/shard_map/ppermute | solution.py:418
  156.4 4.8 %collective-permute-start.25 = (f32[2,16,224]{2,1,0:T(8,128)S(1)}, f32[2,16,224]{2,1,0:T(8,128)S(1)}, u32[]{:S(2)}, u32[]{:S(2)}) collective-permute-start(f32[2,16,224]{2,1,0:T(8,128)S(1)} %add.125.sums_ref), channel_id=1, source_target_pairs={{0,16},{4,20},{8,24},{12,28},{16,0},{20,4},{24,8},{28,12},{1,17},{... | collective-permute-start | bytes 86024 | tf_op jit(solution)/shard_map/ppermute | solution.py:474
  163.0 19.9 %collective-permute-start.26 = (bf16[4,4,2,4096]{3,2,1,0:T(2,128)(2,1)S(1)}, bf16[4,4,2,4096]{3,2,1,0:T(2,128)(2,1)S(1)}, u32[]{:S(2)}, u32[]{:S(2)}) collective-permute-start(bf16[4,4,2,4096]{3,2,1,0:T(2,128)(2,1)S(1)} %get-tuple-element.78), channel_id=1, source_target_pairs={{0,16},{4,20},{8,24},{12,28},{16,0},{20,4},{24,8},{28,12},{1,17},{... | collective-permute-start | bytes 786440 | tf_op jit(solution)/shard_map/ppermute | solution.py:407
  166.6 62.3 %slice-start = ((s8[6291456]{0:T(1024)(128)(4,1)}), s8[4194304]{0:T(1024)(128)(4,1)S(1)}, s32[]{:S(2)}) async-start(s8[6291456]{0:T(1024)(128)(4,1)} %bitcast.25), calls=%async_computation | async-start | bytes 8388608
  166.6 19.4 %collective-permute-start.27 = (bf16[4,4,2,4096]{3,2,1,0:T(2,128)(2,1)S(1)}, bf16[4,4,2,4096]{3,2,1,0:T(2,128)(2,1)S(1)}, u32[]{:S(2)}, u32[]{:S(2)}) collective-permute-start(bf16[4,4,2,4096]{3,2,1,0:T(2,128)(2,1)S(1)} %get-tuple-element.79), channel_id=1, source_target_pairs={{0,4},{4,0},{8,12},{12,8},{16,20},{20,16},{24,28},{28,24},{1,5},{5... | collective-permute-start | bytes 786440 | tf_op jit(solution)/shard_map/ppermute | solution.py:407
  167.2 28.4 %collective-permute-start.28 = (bf16[4,4,2,4096]{3,2,1,0:T(2,128)(2,1)S(1)}, bf16[4,4,2,4096]{3,2,1,0:T(2,128)(2,1)S(1)}, u32[]{:S(2)}, u32[]{:S(2)}) collective-permute-start(bf16[4,4,2,4096]{3,2,1,0:T(2,128)(2,1)S(1)} %get-tuple-element.80), channel_id=1, source_target_pairs={{0,20},{4,16},{8,28},{12,24},{16,4},{20,0},{24,12},{28,8},{1,21},{... | collective-permute-start | bytes 786440 | tf_op jit(solution)/shard_map/ppermute | solution.py:407
  168.8 34.4 %collective-permute-start.29 = (bf16[4,4,2,4096]{3,2,1,0:T(2,128)(2,1)S(1)}, bf16[4,4,2,4096]{3,2,1,0:T(2,128)(2,1)S(1)}, u32[]{:S(2)}, u32[]{:S(2)}) collective-permute-start(bf16[4,4,2,4096]{3,2,1,0:T(2,128)(2,1)S(1)} %get-tuple-element.81), channel_id=1, source_target_pairs={{0,8},{4,12},{8,0},{12,4},{16,24},{20,28},{24,16},{28,20},{1,9},{5... | collective-permute-start | bytes 786440 | tf_op jit(solution)/shard_map/ppermute | solution.py:407
  170.4 42.3 %collective-permute-start.30 = (bf16[4,4,2,4096]{3,2,1,0:T(2,128)(2,1)S(1)}, bf16[4,4,2,4096]{3,2,1,0:T(2,128)(2,1)S(1)}, u32[]{:S(2)}, u32[]{:S(2)}) collective-permute-start(bf16[4,4,2,4096]{3,2,1,0:T(2,128)(2,1)S(1)} %get-tuple-element.82), channel_id=1, source_target_pairs={{0,24},{4,28},{8,16},{12,20},{16,8},{20,12},{24,0},{28,4},{1,25},{... | collective-permute-start | bytes 786440 | tf_op jit(solution)/shard_map/ppermute | solution.py:407
  182.9 29.8 %collective-permute-start.31 = (bf16[4,4,2,4096]{3,2,1,0:T(2,128)(2,1)S(1)}, bf16[4,4,2,4096]{3,2,1,0:T(2,128)(2,1)S(1)}, u32[]{:S(2)}, u32[]{:S(2)}) collective-permute-start(bf16[4,4,2,4096]{3,2,1,0:T(2,128)(2,1)S(1)} %get-tuple-element.83), channel_id=1, source_target_pairs={{0,12},{4,8},{8,4},{12,0},{16,28},{20,24},{24,20},{28,16},{1,13},{... | collective-permute-start | bytes 786440 | tf_op jit(solution)/shard_map/ppermute | solution.py:407
  186.0 40.7 %collective-permute-start.32 = (bf16[4,4,2,4096]{3,2,1,0:T(2,128)(2,1)S(1)}, bf16[4,4,2,4096]{3,2,1,0:T(2,128)(2,1)S(1)}, u32[]{:S(2)}, u32[]{:S(2)}) collective-permute-start(bf16[4,4,2,4096]{3,2,1,0:T(2,128)(2,1)S(1)} %get-tuple-element.84), channel_id=1, source_target_pairs={{0,28},{4,24},{8,20},{12,16},{16,12},{20,8},{24,4},{28,0},{1,29},{... | collective-permute-start | bytes 786440 | tf_op jit(solution)/shard_map/ppermute | solution.py:407
  195.5 42.3 %collective-permute-start.40 = (bf16[4,4,2,4096]{3,2,1,0:T(2,128)(2,1)S(1)}, bf16[4,4,2,4096]{3,2,1,0:T(2,128)(2,1)S(1)}, u32[]{:S(2)}, u32[]{:S(2)}) collective-permute-start(bf16[4,4,2,4096]{3,2,1,0:T(2,128)(2,1)S(1)} %get-tuple-element.95), channel_id=1, source_target_pairs={{0,16},{4,20},{8,24},{12,28},{16,0},{20,4},{24,8},{28,12},{1,17},{... | collective-permute-start | bytes 786440 | tf_op jit(solution)/shard_map/ppermute | solution.py:407
  203.2 34.7 %collective-permute-start.41 = (bf16[4,4,2,4096]{3,2,1,0:T(2,128)(2,1)S(1)}, bf16[4,4,2,4096]{3,2,1,0:T(2,128)(2,1)S(1)}, u32[]{:S(2)}, u32[]{:S(2)}) collective-permute-start(bf16[4,4,2,4096]{3,2,1,0:T(2,128)(2,1)S(1)} %get-tuple-element.96), channel_id=1, source_target_pairs={{0,4},{4,0},{8,12},{12,8},{16,20},{20,16},{24,28},{28,24},{1,5},{5... | collective-permute-start | bytes 786440 | tf_op jit(solution)/shard_map/ppermute | solution.py:407
  212.7 27.3 %collective-permute-start.42 = (bf16[4,4,2,4096]{3,2,1,0:T(2,128)(2,1)S(1)}, bf16[4,4,2,4096]{3,2,1,0:T(2,128)(2,1)S(1)}, u32[]{:S(2)}, u32[]{:S(2)}) collective-permute-start(bf16[4,4,2,4096]{3,2,1,0:T(2,128)(2,1)S(1)} %get-tuple-element.97), channel_id=1, source_target_pairs={{0,20},{4,16},{8,28},{12,24},{16,4},{20,0},{24,12},{28,8},{1,21},{... | collective-permute-start | bytes 786440 | tf_op jit(solution)/shard_map/ppermute | solution.py:407
  212.7 30.4 %collective-permute-start.43 = (bf16[4,4,2,4096]{3,2,1,0:T(2,128)(2,1)S(1)}, bf16[4,4,2,4096]{3,2,1,0:T(2,128)(2,1)S(1)}, u32[]{:S(2)}, u32[]{:S(2)}) collective-permute-start(bf16[4,4,2,4096]{3,2,1,0:T(2,128)(2,1)S(1)} %get-tuple-element.98), channel_id=1, source_target_pairs={{0,8},{4,12},{8,0},{12,4},{16,24},{20,28},{24,16},{28,20},{1,9},{5... | collective-permute-start | bytes 786440 | tf_op jit(solution)/shard_map/ppermute | solution.py:407
  226.7 30.9 %collective-permute-start.44 = (bf16[4,4,2,4096]{3,2,1,0:T(2,128)(2,1)S(1)}, bf16[4,4,2,4096]{3,2,1,0:T(2,128)(2,1)S(1)}, u32[]{:S(2)}, u32[]{:S(2)}) collective-permute-start(bf16[4,4,2,4096]{3,2,1,0:T(2,128)(2,1)S(1)} %get-tuple-element.99), channel_id=1, source_target_pairs={{0,24},{4,28},{8,16},{12,20},{16,8},{20,12},{24,0},{28,4},{1,25},{... | collective-permute-start | bytes 786440 | tf_op jit(solution)/shard_map/ppermute | solution.py:407
  237.8 20.5 %collective-permute-start.45 = (bf16[4,4,2,4096]{3,2,1,0:T(2,128)(2,1)S(1)}, bf16[4,4,2,4096]{3,2,1,0:T(2,128)(2,1)S(1)}, u32[]{:S(2)}, u32[]{:S(2)}) collective-permute-start(bf16[4,4,2,4096]{3,2,1,0:T(2,128)(2,1)S(1)} %get-tuple-element.100), channel_id=1, source_target_pairs={{0,12},{4,8},{8,4},{12,0},{16,28},{20,24},{24,20},{28,16},{1,13},{... | collective-permute-start | bytes 786440 | tf_op jit(solution)/shard_map/ppermute | solution.py:407
  237.8 31.0 %collective-permute-start.46 = (bf16[4,4,2,4096]{3,2,1,0:T(2,128)(2,1)S(1)}, bf16[4,4,2,4096]{3,2,1,0:T(2,128)(2,1)S(1)}, u32[]{:S(2)}, u32[]{:S(2)}) collective-permute-start(bf16[4,4,2,4096]{3,2,1,0:T(2,128)(2,1)S(1)} %get-tuple-element.101), channel_id=1, source_target_pairs={{0,28},{4,24},{8,20},{12,16},{16,12},{20,8},{24,4},{28,0},{1,29},{... | collective-permute-start | bytes 786440 | tf_op jit(solution)/shard_map/ppermute | solution.py:407
  240.0 35.6 %collective-permute-start.35 = (bf16[4,4,2,4096]{3,2,1,0:T(2,128)(2,1)S(1)}, bf16[4,4,2,4096]{3,2,1,0:T(2,128)(2,1)S(1)}, u32[]{:S(2)}, u32[]{:S(2)}) collective-permute-start(bf16[4,4,2,4096]{3,2,1,0:T(2,128)(2,1)S(1)} %get-tuple-element.88), channel_id=1, source_target_pairs={{0,16},{4,20},{8,24},{12,28},{16,0},{20,4},{24,8},{28,12},{1,17},{... | collective-permute-start | bytes 786440 | tf_op jit(solution)/shard_map/ppermute | solution.py:407
  243.1 35.6 %collective-permute-start.36 = (bf16[4,4,2,4096]{3,2,1,0:T(2,128)(2,1)S(1)}, bf16[4,4,2,4096]{3,2,1,0:T(2,128)(2,1)S(1)}, u32[]{:S(2)}, u32[]{:S(2)}) collective-permute-start(bf16[4,4,2,4096]{3,2,1,0:T(2,128)(2,1)S(1)} %get-tuple-element.89), channel_id=1, source_target_pairs={{0,4},{4,0},{8,12},{12,8},{16,20},{20,16},{24,28},{28,24},{1,5},{5... | collective-permute-start | bytes 786440 | tf_op jit(solution)/shard_map/ppermute | solution.py:407
  258.3 26.0 %collective-permute-start.37 = (bf16[4,4,2,4096]{3,2,1,0:T(2,128)(2,1)}, bf16[4,4,2,4096]{3,2,1,0:T(2,128)(2,1)S(1)}, u32[]{:S(2)}, u32[]{:S(2)}) collective-permute-start(bf16[4,4,2,4096]{3,2,1,0:T(2,128)(2,1)} %get-tuple-element.90), channel_id=1, source_target_pairs={{0,20},{4,16},{8,28},{12,24},{16,4},{20,0},{24,12},{28,8},{1,21},{... | collective-permute-start | bytes 786440 | tf_op jit(solution)/shard_map/ppermute | solution.py:407
  258.3 26.0 %collective-permute-start.38 = (bf16[4,4,2,4096]{3,2,1,0:T(2,128)(2,1)}, bf16[4,4,2,4096]{3,2,1,0:T(2,128)(2,1)S(1)}, u32[]{:S(2)}, u32[]{:S(2)}) collective-permute-start(bf16[4,4,2,4096]{3,2,1,0:T(2,128)(2,1)} %get-tuple-element.91), channel_id=1, source_target_pairs={{0,8},{4,12},{8,0},{12,4},{16,24},{20,28},{24,16},{28,20},{1,9},{5... | collective-permute-start | bytes 786440 | tf_op jit(solution)/shard_map/ppermute | solution.py:407
  268.8 25.5 %collective-permute-start.39 = (bf16[4,4,2,4096]{3,2,1,0:T(2,128)(2,1)}, bf16[4,4,2,4096]{3,2,1,0:T(2,128)(2,1)}, u32[]{:S(2)}, u32[]{:S(2)}) collective-permute-start(bf16[4,4,2,4096]{3,2,1,0:T(2,128)(2,1)} %get-tuple-element.92), channel_id=1, source_target_pairs={{0,24},{4,28},{8,16},{12,20},{16,8},{20,12},{24,0},{28,4},{1,25},{... | collective-permute-start | bytes 786440 | tf_op jit(solution)/shard_map/ppermute | solution.py:407
  275.7 20.8 %collective-permute-start.33 = (bf16[4,4,2,4096]{3,2,1,0:T(2,128)(2,1)}, bf16[4,4,2,4096]{3,2,1,0:T(2,128)(2,1)S(1)}, u32[]{:S(2)}, u32[]{:S(2)}) collective-permute-start(bf16[4,4,2,4096]{3,2,1,0:T(2,128)(2,1)} %get-tuple-element.85), channel_id=1, source_target_pairs={{0,12},{4,8},{8,4},{12,0},{16,28},{20,24},{24,20},{28,16},{1,13},{... | collective-permute-start | bytes 786440 | tf_op jit(solution)/shard_map/ppermute | solution.py:407
  278.7 19.4 %collective-permute-start.34 = (bf16[4,4,2,4096]{3,2,1,0:T(2,128)(2,1)}, bf16[4,4,2,4096]{3,2,1,0:T(2,128)(2,1)}, u32[]{:S(2)}, u32[]{:S(2)}) collective-permute-start(bf16[4,4,2,4096]{3,2,1,0:T(2,128)(2,1)} %get-tuple-element.86), channel_id=1, source_target_pairs={{0,28},{4,24},{8,20},{12,16},{16,12},{20,8},{24,4},{28,0},{1,29},{... | collective-permute-start | bytes 786440 | tf_op jit(solution)/shard_map/ppermute | solution.py:407
  (15 other events, 158.7 us)
